TPU v7x, 1024 devices: a whole 8x8x8 slice. The times are simulated.
1024 devices in a mesh: rows: 64 (over y, x), cols: 16 (over z, core).
Axes of the slice: x: 8, y: 8, z: 8, core: 2. Of those that a mesh axis runs over, the one named last changes fastest.
Arguments:
- columns: int32 [2048, 12], P('rows'), may hold values from 0 to 2047, as said below
- fetch: int32 [2048, 12, 12], P('rows'), may hold values from -1 to 11, as said below
- values: bfloat16 [2048, 12, 128, 128], P('rows', None, 'cols'), may hold values from -6 to 6
Outputs:
- new_values: bfloat16 [2048, 12, 128, 128], P('rows', None, 'cols')
Inputs may be any that keep to these rules, and one draw needn't show every extreme that they name: Slot 0 of block row i holds column i; the columns of one block row are distinct, and the others are block rows at cyclic distance 1 to 7 from i, modulo 2048. fetch[i, t, s] is the slot u with columns[columns[i, t], u] == columns[i, s], or -1 where there is none.
All inputs are finite; a program needn't handle non-finite values.
Results may differ from a plain program's by a relative error of at most 0.0047.
Values may be sent and summed in bfloat16 or wider, within the bound.
No kernel may reach another device: no remote copies, remote signals or barrier semaphores. Data moves between devices by JAX's collectives and lax.ppermute only.
A program may use at most 64 MiB of HBM per device.

v0:
```python
import jax
import jax.numpy as jnp
from jax import lax
from jax.sharding import PartitionSpec as P


def padded(cells, sides, width):
    for axis, dim in sides:
        count = lax.axis_size(axis)
        head = lax.slice_in_dim(cells, 0, width, axis=dim)
        tail = lax.slice_in_dim(cells, cells.shape[dim] - width, cells.shape[dim], axis=dim)
        cells = jnp.concatenate(
            [
                lax.ppermute(tail, axis, [(i, (i + 1) % count) for i in range(count)]),
                cells,
                lax.ppermute(head, axis, [((i + 1) % count, i) for i in range(count)]),
            ],
            axis=dim,
        )
    return cells


def pick_blocks(window, index_group, present_group):
    picked = jnp.take(window, index_group.reshape(-1), axis=0)
    picked = picked.reshape(index_group.shape + window.shape[1:])
    return jnp.where(present_group[:, :, :, None, None], picked, jnp.zeros((), picked.dtype))


def contract(picked, left_group):
    return jnp.einsum("gtswm,gtmr->gswr", picked, left_group, preferred_element_type=jnp.float32)


def neighbour_window(field):
    wide = padded(field, (("rows", 0),), field.shape[0])
    return wide.reshape((-1,) + field.shape[2:])


def grouped(array, group_rows):
    return array.reshape((array.shape[0] // group_rows, group_rows) + array.shape[1:])


def local(columns, fetch, values):
    rows_here, slots, width, block_size = values.shape
    group_rows = 4
    cycle_size = lax.axis_size("rows")
    my_row = lax.axis_index("rows")
    scaling = 1.0 / (slots * block_size)
    owner_row = columns // rows_here
    window_row = (owner_row - my_row + 1) % cycle_size * rows_here + columns % rows_here
    pick_index = window_row[:, :, None] * slots + jnp.maximum(fetch, 0)
    present = fetch >= 0
    index_groups = grouped(pick_index, group_rows)
    present_groups = grouped(present, group_rows)
    start_carry = jnp.zeros((), jnp.int32)
    own_full = lax.all_gather(values, "cols", axis=2, tiled=True)
    own_groups = grouped(own_full, group_rows)

    def product(window):

        def one_group(carry, group):
            index_group, present_group, left_group = group
            return (carry, contract(pick_blocks(window, index_group, present_group), left_group))

        parts_out = lax.scan(one_group, start_carry, (index_groups, present_groups, own_groups))[1]
        return parts_out.reshape(values.shape)

    squared = scaling * product(neighbour_window(values))
    position = lax.axis_index("cols") * width + jnp.arange(width)
    diagonal = (jnp.arange(block_size)[None, :] == position[:, None]).astype(jnp.float32)
    first_slot = (jnp.arange(slots) == 0).astype(jnp.float32)
    shifted = (3.0 * first_slot[None, :, None, None] * diagonal[None, None] - squared).astype(
        jnp.bfloat16
    )
    result = 0.5 * product(neighbour_window(shifted))
    return result.astype(jnp.bfloat16)


def solution(mesh):
    in_specs = (P("rows", None), P("rows", None, None), P("rows", None, "cols", None))
    out_specs = P("rows", None, "cols", None)
    return jax.shard_map(local, mesh=mesh, in_specs=in_specs, out_specs=out_specs, check_vma=False)
```

profile of v0, /device:TPU:1, one launch (start us, length us, event | category | flops | bytes accessed | tf_op | source)
XLA Modules:
  0.0 292.4 jit_solution(5196817031482346045)
XLA Ops:
  7.3 4.0 %collective-permute-start = (bf16[32,12,8,128]{3,2,1,0:T(8,128)(2,1)}, bf16[32,12,8,128]{3,2,1,0:T(8,128)(2,1)}, u32[]{:S(2)}, u32[]{:S(2)}) collective-permute-start(bf16[32,12,8,128]{3,2,1,0:T(8,128)(2,1)} %param.11), channel_id=1, source_target_pairs={{0,16},{16,32},{32,48},{48,64},{64,80},{80,96},{96,112},{112,128},... | collective-permute-start | bytes 2359304 | tf_op jit(solution)/shard_map/ppermute | solution.py:14
  11.2 7.0 %collective-permute-start.1 = (bf16[32,12,8,128]{3,2,1,0:T(8,128)(2,1)}, bf16[32,12,8,128]{3,2,1,0:T(8,128)(2,1)}, u32[]{:S(2)}, u32[]{:S(2)}) collective-permute-start(bf16[32,12,8,128]{3,2,1,0:T(8,128)(2,1)} %param.11), channel_id=1, source_target_pairs={{16,0},{32,16},{48,32},{64,48},{80,64},{96,80},{112,96},{128,112},... | collective-permute-start | bytes 2359304 | tf_op jit(solution)/shard_map/ppermute | solution.py:16
  22.7 3.3 %collective-permute-done = bf16[32,12,8,128]{3,2,1,0:T(8,128)(2,1)} collective-permute-done((bf16[32,12,8,128]{3,2,1,0:T(8,128)(2,1)}, bf16[32,12,8,128]{3,2,1,0:T(8,128)(2,1)}, u32[]{:S(2)}, u32[]{:S(2)}) %collective-permute-start) | collective-permute-done | bytes 786464 | tf_op jit(solution)/shard_map/ppermute | solution.py:14
  29.1 83.0 %all-gather.2.cloned.1.call-done = bf16[32,12,128,128]{3,2,1,0:T(8,128)(2,1)} async-done(((bf16[32,12,8,128]{3,2,1,0:T(8,128)(2,1)}), bf16[32,12,128,128]{3,2,1,0:T(8,128)(2,1)}) %all-gather.2.cloned.1.call-update) | async-done | bytes 12582928 | tf_op jit(solution)/shard_map/all_gather | solution.py:55
  113.5 70.6 %while.20 = (s32[]{:T(128)}, f32[8,4,12,8,128]{4,3,2,1,0:T(8,128)}, pred[8,4,12,12]{2,3,1,0:T(8,128)(4,1)}, s32[8,4,12,12]{3,2,1,0:T(8,128)}, bf16[1152,8,128]{2...) while((s32[]{:T(128)}, f32[8,4,12,8,128]{4,3,2,1,0:T(8,128)}, ...), condition=%wide.region_1.3_spmd, body=%wide.region_0.2_spmd.sunk | while | flops 152180800 | bytes 7696533 | solution.py:64
  119.5 2.8 fusion.40
  128.3 2.8 fusion.40
  137.2 2.8 fusion.40
  146.0 2.8 fusion.40
  154.8 2.8 fusion.40
  163.6 2.8 fusion.40
  172.4 2.8 fusion.40
  181.2 2.8 fusion.40
  185.8 3.1 %collective-permute-start.2 = (bf16[32,12,8,128]{3,2,1,0:T(8,128)(2,1)S(1)}, bf16[32,12,8,128]{3,2,1,0:T(8,128)(2,1)S(1)}, u32[]{:S(2)}, u32[]{:S(2)}) collective-permute-start(bf16[32,12,8,128]{3,2,1,0:T(8,128)(2,1)S(1)} %fusion.26), channel_id=1, source_target_pairs={{0,16},{16,32},{32,48},{48,64},{64,80},{80,96},{96,112},{112,128},... | collective-permute-start | bytes 2359304 | tf_op jit(solution)/shard_map/ppermute | solution.py:14
  188.9 5.6 %collective-permute-start.3 = (bf16[32,12,8,128]{3,2,1,0:T(8,128)(2,1)S(1)}, bf16[32,12,8,128]{3,2,1,0:T(8,128)(2,1)S(1)}, u32[]{:S(2)}, u32[]{:S(2)}) collective-permute-start(bf16[32,12,8,128]{3,2,1,0:T(8,128)(2,1)S(1)} %fusion.26), channel_id=1, source_target_pairs={{16,0},{32,16},{48,32},{64,48},{80,64},{96,80},{112,96},{128,112},... | collective-permute-start | bytes 2359304 | tf_op jit(solution)/shard_map/ppermute | solution.py:16
  194.5 15.6 %collective-permute-done.2 = bf16[32,12,8,128]{3,2,1,0:T(8,128)(2,1)S(1)} collective-permute-done((bf16[32,12,8,128]{3,2,1,0:T(8,128)(2,1)S(1)}, bf16[32,12,8,128]{3,2,1,0:T(8,128)(2,1)S(1)}, u32[]{:S(2)}, u32[]{:S(2)}) %collective-permute-start.2) | collective-permute-done | bytes 786464 | tf_op jit(solution)/shard_map/ppermute | solution.py:14
  212.5 70.6 %while.21 = (s32[]{:T(128)}, f32[8,4,12,8,128]{4,3,2,1,0:T(8,128)}, pred[8,4,12,12]{2,3,1,0:T(8,128)(4,1)}, s32[8,4,12,12]{3,2,1,0:T(8,128)}, bf16[1152,8,128]{2...) while((s32[]{:T(128)}, f32[8,4,12,8,128]{4,3,2,1,0:T(8,128)}, ...), condition=%wide.region_3.5_spmd, body=%wide.region_2.4_spmd.sunk | while | flops 152180800 | bytes 7696533 | solution.py:64
  218.5 2.8 fusion.42
  227.4 2.8 fusion.42
  245.0 2.8 fusion.42
  253.8 2.8 fusion.42
  262.6 2.8 fusion.42
  271.5 2.8 fusion.42
  280.3 2.8 fusion.42
  (154 shorter events, 114.8 us)
Async XLA Ops:
  6.5 20.9 %copy-start = (bf16[32,12,8,128]{3,2,1,0:T(8,128)(2,1)S(1)}, bf16[32,12,8,128]{3,2,1,0:T(8,128)(2,1)}, u32[]{:S(2)}) copy-start(bf16[32,12,8,128]{3,2,1,0:T(8,128)(2,1)} %param.11) | copy-start | bytes 2359300
  6.5 105.6 %all-gather.2.cloned.1.call-start = ((), (), s32[]{:S(2)}) async-start(), calls=%async_computation | async-start | bytes 13369344 | tf_op jit(solution)/shard_map/all_gather | solution.py:55
  7.3 18.7 %collective-permute-start = (bf16[32,12,8,128]{3,2,1,0:T(8,128)(2,1)}, bf16[32,12,8,128]{3,2,1,0:T(8,128)(2,1)}, u32[]{:S(2)}, u32[]{:S(2)}) collective-permute-start(bf16[32,12,8,128]{3,2,1,0:T(8,128)(2,1)} %param.11), channel_id=1, source_target_pairs={{0,16},{16,32},{32,48},{48,64},{64,80},{80,96},{96,112},{112,128},... | collective-permute-start | bytes 2359304 | tf_op jit(solution)/shard_map/ppermute | solution.py:14
  11.2 16.2 %collective-permute-start.1 = (bf16[32,12,8,128]{3,2,1,0:T(8,128)(2,1)}, bf16[32,12,8,128]{3,2,1,0:T(8,128)(2,1)}, u32[]{:S(2)}, u32[]{:S(2)}) collective-permute-start(bf16[32,12,8,128]{3,2,1,0:T(8,128)(2,1)} %param.11), channel_id=1, source_target_pairs={{16,0},{32,16},{48,32},{64,48},{80,64},{96,80},{112,96},{128,112},... | collective-permute-start | bytes 2359304 | tf_op jit(solution)/shard_map/ppermute | solution.py:16
  184.0 1.6 copy-start.1
  185.8 24.3 %collective-permute-start.2 = (bf16[32,12,8,128]{3,2,1,0:T(8,128)(2,1)S(1)}, bf16[32,12,8,128]{3,2,1,0:T(8,128)(2,1)S(1)}, u32[]{:S(2)}, u32[]{:S(2)}) collective-permute-start(bf16[32,12,8,128]{3,2,1,0:T(8,128)(2,1)S(1)} %fusion.26), channel_id=1, source_target_pairs={{0,16},{16,32},{32,48},{48,64},{64,80},{80,96},{96,112},{112,128},... | collective-permute-start | bytes 2359304 | tf_op jit(solution)/shard_map/ppermute | solution.py:14
  188.9 22.1 %collective-permute-start.3 = (bf16[32,12,8,128]{3,2,1,0:T(8,128)(2,1)S(1)}, bf16[32,12,8,128]{3,2,1,0:T(8,128)(2,1)S(1)}, u32[]{:S(2)}, u32[]{:S(2)}) collective-permute-start(bf16[32,12,8,128]{3,2,1,0:T(8,128)(2,1)S(1)} %fusion.26), channel_id=1, source_target_pairs={{16,0},{32,16},{48,32},{64,48},{80,64},{96,80},{112,96},{128,112},... | collective-permute-start | bytes 2359304 | tf_op jit(solution)/shard_map/ppermute | solution.py:16
Sparse Core Ops, SparseCore 0:
  10.0 102.0 all-gather.1
where the time goes:
time: 297 us; the launch traced here: 292 us
  waiting for transfers between devices  105 us (35%)
  local copies, waits for them, and re-layouts  67.9 us (23%)
  matrix products  44.6 us (15%)
  other arithmetic  41.1 us (14%)
  starting transfers between devices  19.6 us (7%)
  between operations  13.5 us (5%)
    all_gather x1, waiting for transfers between devices, local(): own_full = lax.all_gather(values, 'cols', axis=2, tiled=True)  83 us
    dot_general x16, matrix products, contract(): jnp.einsum('gtswm,gtmr->gswr', picked, left_group, preferred_element_type...  44.6 us
    gather x16, local copies, waits for them, and re-layouts, pick_blocks(): picked = jnp.take(window, index_group.reshape(-1), axis=0)  37.4 us
    select_n x32, other arithmetic, pick_blocks(): picked = jnp.take(window, index_group.reshape(-1), axis=0)  33.2 us
    ppermute x2, waiting for transfers between devices, padded(): lax.ppermute(tail, axis, [(i, (i + 1) % count) for i in range(count)])  18.9 us
    ppermute x2, starting transfers between devices, padded(): lax.ppermute(head, axis, [((i + 1) % count, i) for i in range(count)])  12.6 us
    dynamic_slice x16, local copies, waits for them, and re-layouts, product(): lax.scan(one_group, start_carry, (index_groups, present_groups, own_groups))  12.2 us
    broadcast_in_dim x16, local copies, waits for them, and re-layouts, pick_blocks(): jnp.where(present_group[:, :, :, None, None], picked, jnp.zeros((), picke...  11.3 us
  transfers between devices with their start and end apart: 5, of which 5 were waited for; matrix products, arithmetic and copies ran while one was open for 2% of the time, Pallas kernels for 0%

commit v1 on v0

v1 whole, which is shorter than its diff:
```python
import functools

import jax
import jax.numpy as jnp
from jax import lax
from jax.experimental import pallas as pl
from jax.experimental.pallas import tpu as pltpu
from jax.sharding import PartitionSpec as P

GROUP = 4


def product_kernel(chunks, is_first, scale, where_ref, index_ref, *refs):
    parts = refs[:4]
    pieces = [refs[4 + 9 * k:13 + 9 * k] for k in range(chunks)]
    rest = refs[4 + 9 * chunks:]
    outs, (window, left, window_sem, left_sem) = rest[:-4], rest[-4:]
    slots, width, size = parts[0].shape[1:]
    ring = size // width
    z, core = where_ref[0], where_ref[1]

    window_copies = []
    for k, part in enumerate(parts):
        window_copies.append(pltpu.make_async_copy(part, window.at[pl.ds(8 * k, 8), pl.ds(0, slots)], window_sem.at[k]))
    left_copies = []
    for g in range(2 * chunks):
        chunk, half = divmod(g, 2)
        group_copies = []
        for k in range(ring):
            away = (0, -1, -2, -3, 1, 2, 3, 4)[k]
            source = pieces[chunk][8] if k == 7 and half == 1 else pieces[chunk][k]
            rows = pl.ds(0 if k == 7 else GROUP * half, GROUP)
            slot = lax.rem(z + away + ring, ring)
            group_copies.append(
                pltpu.make_async_copy(source.at[rows], left.at[pl.ds(GROUP * g, GROUP), :, slot], left_sem.at[g, k])
            )
        left_copies.append(group_copies)
    for copy in window_copies:
        copy.start()
    for group_copies in left_copies:
        for copy in group_copies:
            copy.start()
    window[32, 0] = jnp.zeros((width, size), window.dtype)
    tile_at = window.reshape(window.shape[0] * window.shape[1], width, size)
    for copy in window_copies:
        copy.wait()

    def one_row(i, carry):
        total = jnp.zeros((slots * width, size), jnp.float32)
        base = i * (slots * slots)
        for t in range(0, slots, 2):
            columns = []
            for u in (t, t + 1):
                tiles = []
                for s in range(slots):
                    tiles.append(tile_at[index_ref[base + u * slots + s]])
                columns.append(jnp.concatenate(tiles, axis=0))
            picked = jnp.concatenate(columns, axis=1)
            blocks = left[i, pl.ds(t, 2)].reshape(2 * size, size)
            total += jnp.dot(picked, blocks, preferred_element_type=jnp.float32)
        total = (total * scale).reshape(slots, width, size)
        if is_first:
            (out,) = outs
            out[i] = (-total).astype(out.dtype)
            line = lax.broadcasted_iota(jnp.int32, (width, size), 0)
            lane = lax.broadcasted_iota(jnp.int32, (width, size), 1)
            diagonal = jnp.where(lane == line + z * width, 3.0, 0.0)
            out[i, 0] = (diagonal - total[0]).astype(out.dtype)
        else:
            keep, send = outs
            low, high = total[:, :width // 2], total[:, width // 2:]
            to = lax.rem(i + 8 * core, 16)
            keep[to] = jnp.where(core == 0, low, high).astype(keep.dtype)
            send[to] = jnp.where(core == 0, high, low).astype(send.dtype)
        return carry

    for g in range(2 * chunks):
        for copy in left_copies[g]:
            copy.wait()
        lax.fori_loop(GROUP * g, GROUP * (g + 1), one_row, 0)


def product(is_first, scale, where, index, parts, streams):
    chunks = len(streams)
    slots, width, size = parts[0].shape[1:]
    rows = 8 * chunks
    dtype = parts[0].dtype
    if is_first:
        outs = jax.ShapeDtypeStruct((rows, slots, width, size), dtype)
        out_specs = pl.BlockSpec(memory_space=pltpu.VMEM)
    else:
        outs = [jax.ShapeDtypeStruct((rows, slots, width // 2, size), dtype)] * 2
        out_specs = [pl.BlockSpec(memory_space=pltpu.VMEM)] * 2
    operands = list(parts) + [piece for stream in streams for piece in stream]
    flops = 2 * rows * slots * slots * width * size * size
    return pl.pallas_call(
        functools.partial(product_kernel, chunks, is_first, scale),
        out_shape=outs,
        in_specs=[pl.BlockSpec(memory_space=pltpu.SMEM)] * 2 + [pl.BlockSpec(memory_space=pl.ANY)] * len(operands),
        out_specs=out_specs,
        scratch_shapes=[
            pltpu.VMEM((33, 16, width, size), dtype),
            pltpu.VMEM((rows, slots, size // width, width, size), dtype),
            pltpu.SemaphoreType.DMA((4,)),
            pltpu.SemaphoreType.DMA((2 * chunks, size // width)),
        ],
        compiler_params=pltpu.CompilerParams(vmem_limit_bytes=32 * 2**20),
        cost_estimate=pl.CostEstimate(flops=flops, bytes_accessed=rows * slots * size * size * 2, transcendentals=0),
    )(where, index, *operands)


def gather_ring(streams, ring):
    count = 2 * ring
    up = [(i, (i + 2) % count) for i in range(count)]
    down = [((i + 2) % count, i) for i in range(count)]
    risen = [[piece] for piece in streams]
    fallen = [[piece] for piece in streams]
    for step in range(ring // 2 - 1):
        for k in range(len(streams)):
            risen[k].append(lax.ppermute(risen[k][-1], "cols", up))
            fallen[k].append(lax.ppermute(fallen[k][-1], "cols", down))
    gathered = []
    for k in range(len(streams)):
        half = streams[k].shape[0] // 2
        last_up = lax.ppermute(risen[k][-1][:half], "cols", up)
        last_down = lax.ppermute(fallen[k][-1][half:], "cols", down)
        gathered.append(risen[k] + fallen[k][1:] + [last_up, last_down])
    return gathered


def local(columns, fetch, values):
    rows_here, slots, half_width, size = values.shape
    cols = lax.axis_size("cols")
    count = lax.axis_size("rows")
    col = lax.axis_index("cols")
    z, core = col // 2, col % 2
    first = core == 0
    swap = [(i, i ^ 1) for i in range(cols)]

    def outward(piece):
        pairs = []
        for r in range(count):
            for c in range(cols):
                to = ((r - 1) % count, c + 1) if c % 2 == 0 else ((r + 1) % count, c - 1)
                pairs.append((r * cols + c, to[0] * cols + to[1]))
        return lax.ppermute(piece, ("rows", "cols"), pairs)

    other = lax.ppermute(values, "cols", swap)

    def block(number_first, number_second):
        start = jnp.where(first, 8 * number_first, 8 * number_second)
        mine = lax.dynamic_slice_in_dim(values, start, 8, 0)
        theirs = lax.dynamic_slice_in_dim(other, start, 8, 0)
        low = jnp.where(first, mine, theirs)
        high = jnp.where(first, theirs, mine)
        return jnp.concatenate([low, high], axis=2)

    outer_rows, inner_rows, beyond = block(0, 3), block(1, 2), block(2, 1)
    streams = gather_ring([outer_rows, inner_rows], cols // 2)

    origin = lax.axis_index("rows") * rows_here + core * 16
    total = rows_here * count
    away = (columns - origin + total // 2) % total - total // 2 + 8
    part = jnp.where(first, away // 8, 3 - away // 8)
    place = (part * 8 + away % 8) * 16
    index = jnp.where(fetch >= 0, place[:, :, None] + fetch, 32 * 16)
    index = index.reshape(4, -1)
    index = jnp.where(first, index[:2], index[:1:-1])
    where = jnp.stack([z, core]).astype(jnp.int32)

    scale = 1.0 / (slots * size)
    window = (outward(outer_rows), outer_rows, inner_rows, beyond)
    shifted_outer = product(True, scale, where, index[0], window, streams[:1])
    shifted_outward = outward(shifted_outer)
    shifted_inner = product(True, scale, where, index[1], window, streams[1:])
    shifted_beyond = lax.ppermute(shifted_inner, "cols", swap)
    window = (shifted_outward, shifted_outer, shifted_inner, shifted_beyond)
    keep, send = product(False, 0.5, where, index.reshape(-1), window, streams)
    got = lax.ppermute(send, "cols", swap)
    return jnp.where(first, jnp.concatenate([keep, got]), jnp.concatenate([got, keep]))


def solution(mesh):
    in_specs = (P("rows", None), P("rows", None, None), P("rows", None, "cols", None))
    out_specs = P("rows", None, "cols", None)
    return jax.shard_map(local, mesh=mesh, in_specs=in_specs, out_specs=out_specs, check_vma=False)
```

time: 297 us -> 134 us (0.45); the launches traced: 292 us -> 133 us
  waiting for transfers between devices: 105 us -> 11.4 us
  starting transfers between devices: 19.6 us -> 87.8 us
  local copies, waits for them, and re-layouts: 67.9 us -> 10.3 us
  matrix products: 44.6 us -> 0 us
  other arithmetic: 41.1 us -> 3.98 us
  Pallas kernels: 0 us -> 18.6 us
  between operations: 13.5 us -> 0.53 us
    all_gather x1 -> x0, waiting for transfers between devices: 83 us -> none  [local(): own_full = lax.all_gather(values, 'cols', axis=2, tiled=True)]
    ppermute x4 -> x21, starting transfers between devices: 19.6 us -> 87.8 us  [the longest x6 28.5 us: gather_ring(): fallen[k].append(lax.ppermute(fallen[k][-1], 'cols', down))]
    dot_general x16 -> x0, matrix products: 44.6 us -> none  [contract(): jnp.einsum('gtswm,gtmr->gswr', picked, left_group, preferred_element_type...]
    gather x16 -> x0, local copies, waits for them, and re-layouts: 37.4 us -> none  [pick_blocks(): picked = jnp.take(window, index_group.reshape(-1), axis=0)]
    select_n x32 -> x4, other arithmetic: 33.2 us -> 3.67 us  [the longest x1 1.94 us: block(): low = jnp.where(first, mine, theirs)]
    pallas_call x0 -> x3, Pallas kernels: none -> 18.6 us  [product(): pl.pallas_call(functools.partial(product_kernel, chunks, is_first, scale)...]
    dynamic_slice x16 -> x0, local copies, waits for them, and re-layouts: 12.2 us -> none  [product(): lax.scan(one_group, start_carry, (index_groups, present_groups, own_groups))]
    broadcast_in_dim x16 -> x0, local copies, waits for them, and re-layouts: 11.3 us -> none  [pick_blocks(): jnp.where(present_group[:, :, :, None, None], picked, jnp.zeros((), picke...]
  transfers between devices with their start and end apart: 5 -> 21, of which waited for: 5 -> 6; matrix products, arithmetic and copies ran while one was open for 2% -> 4% of each run, Pallas kernels for 0% -> 8%
where the time goes in v1:
time: 134 us; the launch traced here: 133 us
  starting transfers between devices  87.8 us (66%)
  Pallas kernels  18.6 us (14%)
  waiting for transfers between devices  11.4 us (9%)
  local copies, waits for them, and re-layouts  10.3 us (8%)
  other arithmetic  3.98 us (3%)
    ppermute x6, starting transfers between devices, gather_ring(): fallen[k].append(lax.ppermute(fallen[k][-1], 'cols', down))  28.5 us
    pallas_call x3, Pallas kernels, product(): pl.pallas_call(functools.partial(product_kernel, chunks, is_first, scale)...  18.6 us
    ppermute x1, starting transfers between devices, local(): other = lax.ppermute(values, 'cols', swap)  16.1 us
    ppermute x2, starting transfers between devices, outward(): return lax.ppermute(piece, ('rows', 'cols'), pairs)  12.7 us
    ppermute x6, starting transfers between devices, gather_ring(): risen[k].append(lax.ppermute(risen[k][-1], 'cols', up))  11.5 us
    ppermute x2, starting transfers between devices, gather_ring(): last_down = lax.ppermute(fallen[k][-1][half:], 'cols', down)  9.28 us
    unnamed x32, local copies, waits for them, and re-layouts  5.31 us
    ppermute x2, waiting for transfers between devices, gather_ring(): last_up = lax.ppermute(risen[k][-1][:half], 'cols', up)  5.14 us
  transfers between devices with their start and end apart: 21, of which 6 were waited for; matrix products, arithmetic and copies ran while one was open for 4% of the time, Pallas kernels for 8%

profile of v1, /device:TPU:1, one launch (start us, length us, event | category | flops | bytes accessed | tf_op | source)
XLA Modules:
  0.0 132.5 jit_solution(14475245568307766223)
XLA Ops:
  0.0 16.1 %collective-permute-start = (bf16[32,12,8,128]{3,2,1,0:T(8,128)(2,1)}, bf16[32,12,8,128]{3,2,1,0:T(8,128)(2,1)S(1)}, u32[]{:S(2)}, u32[]{:S(2)}) collective-permute-start(bf16[32,12,8,128]{3,2,1,0:T(8,128)(2,1)} %param.5), channel_id=1, source_target_pairs={{0,1},{1,0},{2,3},{3,2},{4,5},{5,4},{6,7},{7,6},{8,9},{9,8},{10,11... | collective-permute-start | bytes 2359304 | tf_op jit(solution)/shard_map/ppermute | solution.py:148
  16.1 2.1 %collective-permute-done = bf16[32,12,8,128]{3,2,1,0:T(8,128)(2,1)S(1)} collective-permute-done((bf16[32,12,8,128]{3,2,1,0:T(8,128)(2,1)}, bf16[32,12,8,128]{3,2,1,0:T(8,128)(2,1)S(1)}, u32[]{:S(2)}, u32[]{:S(2)}) %collective-permute-start) | collective-permute-done | bytes 786464 | tf_op jit(solution)/shard_map/ppermute | solution.py:148
  18.2 1.9 %broadcast_select_fusion.1 = (bf16[8,12,8,128]{3,2,1,0:T(8,128)(2,1)}, bf16[8,12,8,128]{3,2,1,0:T(8,128)(2,1)S(1)}, bf16[8,12,8,128]{3,2,1,0:T(8,128)(2,1)S(1)},...) fusion(pred[]{:T(512)S(6)} %eq.8, ...), kind=kLoop, calls=%fused_computation.5 | loop fusion | flops 589824 | bytes 2359309 | tf_op jit(solution)/shard_map/jit(_where)/select_n | solution.py:154
  20.2 4.4 %collective-permute-start.14 = (bf16[8,12,16,128]{3,2,1,0:T(8,128)(2,1)S(1)}, bf16[8,12,16,128]{3,2,1,0:T(8,128)(2,1)S(1)}, u32[]{:S(2)}, u32[]{:S(2)}) collective-permute-start(bf16[8,12,16,128]{3,2,1,0:T(8,128)(2,1)S(1)} %pad_maximum_fusion.1.refs_2_.refs_4_.refs_13_), channel_id=1, source_target_pairs={{2,0},{3,1},{4,2},{5,3},{6,4},{7,5},{8,6},{9,7},{10,8},{11,9},{12,... | collective-permute-start | bytes 1179656 | tf_op jit(solution)/shard_map/ppermute | solution.py:121
  24.6 1.9 %collective-permute-start.11 = (bf16[8,12,16,128]{3,2,1,0:T(8,128)(2,1)S(1)}, bf16[8,12,16,128]{3,2,1,0:T(8,128)(2,1)S(1)}, u32[]{:S(2)}, u32[]{:S(2)}) collective-permute-start(bf16[8,12,16,128]{3,2,1,0:T(8,128)(2,1)S(1)} %pad_maximum_fusion.1.refs_2_.refs_4_.refs_13_), channel_id=1, source_target_pairs={{0,2},{1,3},{2,4},{3,5},{4,6},{5,7},{6,8},{7,9},{8,10},{9,11},{10,... | collective-permute-start | bytes 1179656 | tf_op jit(solution)/shard_map/ppermute | solution.py:120
  26.6 4.6 %collective-permute-start.5 = (bf16[8,12,16,128]{3,2,1,0:T(8,128)(2,1)S(1)}, bf16[8,12,16,128]{3,2,1,0:T(8,128)(2,1)S(1)}, u32[]{:S(2)}, u32[]{:S(2)}) collective-permute-start(bf16[8,12,16,128]{3,2,1,0:T(8,128)(2,1)S(1)} %pad_maximum_fusion.refs_1_.refs_4_), channel_id=1, source_target_pairs={{2,0},{3,1},{4,2},{5,3},{6,4},{7,5},{8,6},{9,7},{10,8},{11,9},{12,... | collective-permute-start | bytes 1179656 | tf_op jit(solution)/shard_map/ppermute | solution.py:121
  31.2 1.9 %collective-permute-start.2 = (bf16[8,12,16,128]{3,2,1,0:T(8,128)(2,1)S(1)}, bf16[8,12,16,128]{3,2,1,0:T(8,128)(2,1)S(1)}, u32[]{:S(2)}, u32[]{:S(2)}) collective-permute-start(bf16[8,12,16,128]{3,2,1,0:T(8,128)(2,1)S(1)} %pad_maximum_fusion.refs_1_.refs_4_), channel_id=1, source_target_pairs={{0,2},{1,3},{2,4},{3,5},{4,6},{5,7},{6,8},{7,9},{8,10},{9,11},{10,... | collective-permute-start | bytes 1179656 | tf_op jit(solution)/shard_map/ppermute | solution.py:120
  33.2 4.8 %collective-permute-start.15 = (bf16[8,12,16,128]{3,2,1,0:T(8,128)(2,1)S(1)}, bf16[8,12,16,128]{3,2,1,0:T(8,128)(2,1)}, u32[]{:S(2)}, u32[]{:S(2)}) collective-permute-start(bf16[8,12,16,128]{3,2,1,0:T(8,128)(2,1)S(1)} %collective-permute-done.14.refs_8_.refs_17_), channel_id=1, source_target_pairs={{2,0},{3,1},{4,2},{5,3},{6,4},{7,5},{8,6},{9,7},{10,8},{11,9},{12,... | collective-permute-start | bytes 1179656 | tf_op jit(solution)/shard_map/ppermute | solution.py:121
  38.0 1.9 %collective-permute-start.12 = (bf16[8,12,16,128]{3,2,1,0:T(8,128)(2,1)S(1)}, bf16[8,12,16,128]{3,2,1,0:T(8,128)(2,1)}, u32[]{:S(2)}, u32[]{:S(2)}) collective-permute-start(bf16[8,12,16,128]{3,2,1,0:T(8,128)(2,1)S(1)} %collective-permute-done.11.refs_5_.refs_14_), channel_id=1, source_target_pairs={{0,2},{1,3},{2,4},{3,5},{4,6},{5,7},{6,8},{7,9},{8,10},{9,11},{10,... | collective-permute-start | bytes 1179656 | tf_op jit(solution)/shard_map/ppermute | solution.py:120
  41.1 5.3 %collective-permute-start.6 = (bf16[8,12,16,128]{3,2,1,0:T(8,128)(2,1)S(1)}, bf16[8,12,16,128]{3,2,1,0:T(8,128)(2,1)}, u32[]{:S(2)}, u32[]{:S(2)}) collective-permute-start(bf16[8,12,16,128]{3,2,1,0:T(8,128)(2,1)S(1)} %collective-permute-done.5.refs_8_), channel_id=1, source_target_pairs={{2,0},{3,1},{4,2},{5,3},{6,4},{7,5},{8,6},{9,7},{10,8},{11,9},{12,... | collective-permute-start | bytes 1179656 | tf_op jit(solution)/shard_map/ppermute | solution.py:121
  46.4 1.9 %collective-permute-start.3 = (bf16[8,12,16,128]{3,2,1,0:T(8,128)(2,1)S(1)}, bf16[8,12,16,128]{3,2,1,0:T(8,128)(2,1)}, u32[]{:S(2)}, u32[]{:S(2)}) collective-permute-start(bf16[8,12,16,128]{3,2,1,0:T(8,128)(2,1)S(1)} %collective-permute-done.2.refs_5_), channel_id=1, source_target_pairs={{0,2},{1,3},{2,4},{3,5},{4,6},{5,7},{6,8},{7,9},{8,10},{9,11},{10,... | collective-permute-start | bytes 1179656 | tf_op jit(solution)/shard_map/ppermute | solution.py:120
  48.8 2.9 %rev.3 = s32[2,1152]{1,0:T(2,128)} reverse(s32[2,1152]{1,0:T(2,128)S(1)} %slice.33), dimensions={0} | reverse | bytes 18432 | tf_op jit(solution)/shard_map/rev | solution.py:168
  52.6 5.3 %collective-permute-start.1 = (bf16[8,12,16,128]{3,2,1,0:T(8,128)(2,1)S(1)}, bf16[8,12,16,128]{3,2,1,0:T(8,128)(2,1)}, u32[]{:S(2)}, u32[]{:S(2)}) collective-permute-start(bf16[8,12,16,128]{3,2,1,0:T(8,128)(2,1)S(1)} %pad_maximum_fusion.refs_1_.refs_4_), channel_id=1, source_target_pairs={{0,1009},{1,16},{2,1011},{3,18},{4,1013},{5,20},{6,1015},{7,22},{8... | collective-permute-start | bytes 1179656 | tf_op jit(solution)/shard_map/ppermute | solution.py:146
  57.9 4.9 %collective-permute-start.16 = (bf16[8,12,16,128]{3,2,1,0:T(8,128)(2,1)}, bf16[8,12,16,128]{3,2,1,0:T(8,128)(2,1)S(1)}, u32[]{:S(2)}, u32[]{:S(2)}) collective-permute-start(bf16[8,12,16,128]{3,2,1,0:T(8,128)(2,1)} %collective-permute-done.15.refs_9_.refs_18_), channel_id=1, source_target_pairs={{2,0},{3,1},{4,2},{5,3},{6,4},{7,5},{8,6},{9,7},{10,8},{11,9},{12,... | collective-permute-start | bytes 1179656 | tf_op jit(solution)/shard_map/ppermute | solution.py:121
  64.7 4.6 %collective-permute-start.7 = (bf16[8,12,16,128]{3,2,1,0:T(8,128)(2,1)}, bf16[8,12,16,128]{3,2,1,0:T(8,128)(2,1)S(1)}, u32[]{:S(2)}, u32[]{:S(2)}) collective-permute-start(bf16[8,12,16,128]{3,2,1,0:T(8,128)(2,1)} %collective-permute-done.6.refs_9_), channel_id=1, source_target_pairs={{2,0},{3,1},{4,2},{5,3},{6,4},{7,5},{8,6},{9,7},{10,8},{11,9},{12,... | collective-permute-start | bytes 1179656 | tf_op jit(solution)/shard_map/ppermute | solution.py:121
  72.6 4.6 %collective-permute-start.18 = (bf16[4,12,16,128]{3,2,1,0:T(8,128)(2,1)S(1)}, bf16[4,12,16,128]{3,2,1,0:T(8,128)(2,1)S(1)}, u32[]{:S(2)}, u32[]{:S(2)}) collective-permute-start(bf16[4,12,16,128]{3,2,1,0:T(8,128)(2,1)S(1)} %slice.47), channel_id=1, source_target_pairs={{2,0},{3,1},{4,2},{5,3},{6,4},{7,5},{8,6},{9,7},{10,8},{11,9},{12,... | collective-permute-start | bytes 589832 | tf_op jit(solution)/shard_map/ppermute | solution.py:126
  79.2 4.7 %collective-permute-start.9 = (bf16[4,12,16,128]{3,2,1,0:T(8,128)(2,1)S(1)}, bf16[4,12,16,128]{3,2,1,0:T(8,128)(2,1)S(1)}, u32[]{:S(2)}, u32[]{:S(2)}) collective-permute-start(bf16[4,12,16,128]{3,2,1,0:T(8,128)(2,1)S(1)} %slice.44), channel_id=1, source_target_pairs={{2,0},{3,1},{4,2},{5,3},{6,4},{7,5},{8,6},{9,7},{10,8},{11,9},{12,... | collective-permute-start | bytes 589832 | tf_op jit(solution)/shard_map/ppermute | solution.py:126
  86.6 5.1 %collective-permute-done.8.refs_11_ = bf16[4,12,16,128]{3,2,1,0:T(8,128)(2,1)S(1)} collective-permute-done((bf16[4,12,16,128]{3,2,1,0:T(8,128)(2,1)S(1)}, bf16[4,12,16,128]{3,2,1,0:T(8,128)(2,1)S(1)}, u32[]{:S(2)}, u32[]{:S(2)}) %collective-permute-start.8) | collective-permute-done | bytes 196640 | tf_op jit(solution)/shard_map/ppermute | solution.py:125
  91.8 5.4 %shard_map.37.refs_1_ = bf16[8,12,16,128]{3,2,1,0:T(8,128)(2,1)} custom-call(s32[2]{0:T(128)S(1)} %pad_add_fusion.where_ref, s32[1152]{0:T(1024)S(1)} %get-tuple-element.10.index_ref, bf16[8,12,16,128]{3,2,1,0:T(8,128)(2,1)} %collective-permute-done.1.refs_0_, bf16[8,12,16,128]{3,2,1,0:T(8,128)(2,1)S(1)} %pad_maximum_fusion.refs_1_.refs_4_, ...), custom_call_target="tpu_custom_call" | custom-call | flops 603979776 | bytes 3145728 | tf_op jit(solution)/shard_map/pallas_call | solution.py:96
  97.2 7.4 %collective-permute-start.10 = (bf16[8,12,16,128]{3,2,1,0:T(8,128)(2,1)}, bf16[8,12,16,128]{3,2,1,0:T(8,128)(2,1)}, u32[]{:S(2)}, u32[]{:S(2)}) collective-permute-start(bf16[8,12,16,128]{3,2,1,0:T(8,128)(2,1)} %shard_map.37.refs_1_), channel_id=1, source_target_pairs={{0,1009},{1,16},{2,1011},{3,18},{4,1013},{5,20},{6,1015},{7,22},{8... | collective-permute-start | bytes 1179656 | tf_op jit(solution)/shard_map/ppermute | solution.py:146
  104.7 5.4 %shard_map.38.refs_2_ = bf16[8,12,16,128]{3,2,1,0:T(8,128)(2,1)} custom-call(s32[2]{0:T(128)S(1)} %pad_add_fusion.where_ref, s32[1152]{0:T(1024)S(1)} %get-tuple-element.9.index_ref, bf16[8,12,16,128]{3,2,1,0:T(8,128)(2,1)} %collective-permute-done.1.refs_0_, bf16[8,12,16,128]{3,2,1,0:T(8,128)(2,1)S(1)} %pad_maximum_fusion.refs_1_.refs_4_, ...), custom_call_target="tpu_custom_call" | custom-call | flops 603979776 | bytes 3145728 | tf_op jit(solution)/shard_map/pallas_call | solution.py:96
  110.2 2.3 %collective-permute-start.19 = (bf16[8,12,16,128]{3,2,1,0:T(8,128)(2,1)}, bf16[8,12,16,128]{3,2,1,0:T(8,128)(2,1)}, u32[]{:S(2)}, u32[]{:S(2)}) collective-permute-start(bf16[8,12,16,128]{3,2,1,0:T(8,128)(2,1)} %shard_map.38.refs_2_), channel_id=1, source_target_pairs={{0,1},{1,0},{2,3},{3,2},{4,5},{5,4},{6,7},{7,6},{8,9},{9,8},{10,11... | collective-permute-start | bytes 1179656 | tf_op jit(solution)/shard_map/ppermute | solution.py:176
  118.8 7.7 %shard_map.39 = (bf16[16,12,8,128]{3,2,1,0:T(8,128)(2,1)S(1)}, bf16[16,12,8,128]{3,2,1,0:T(8,128)(2,1)S(1)}) custom-call(s32[2]{0:T(128)S(1)} %pad_add_fusion.where_ref, s32[2304]{0:T(1024)S(1)} %reshape.7.index_ref, bf16[8,12,16,128]{3,2,1,0:T(8,128)(2,1)} %collective-permute-done.10.refs_0_, bf16[8,12,16,128]{3,2,1,0:T(8,128)(2,1)} %shard_map.37.refs_1_, ...), custom_call_target="tpu_custom_call" | custom-call | flops 1207959552 | bytes 6291456 | tf_op jit(solution)/shard_map/pallas_call | solution.py:96
  126.6 3.6 %collective-permute-start.20 = (bf16[16,12,8,128]{3,2,1,0:T(8,128)(2,1)S(1)}, bf16[16,12,8,128]{3,2,1,0:T(8,128)(2,1)S(1)}, u32[]{:S(2)}, u32[]{:S(2)}) collective-permute-start(bf16[16,12,8,128]{3,2,1,0:T(8,128)(2,1)S(1)} %get-tuple-element.8), channel_id=1, source_target_pairs={{0,1},{1,0},{2,3},{3,2},{4,5},{5,4},{6,7},{7,6},{8,9},{9,8},{10,11... | collective-permute-start | bytes 1179656 | tf_op jit(solution)/shard_map/ppermute | solution.py:179
  (74 shorter events, 21.2 us)
Async XLA Ops:
  0.0 18.2 %collective-permute-start = (bf16[32,12,8,128]{3,2,1,0:T(8,128)(2,1)}, bf16[32,12,8,128]{3,2,1,0:T(8,128)(2,1)S(1)}, u32[]{:S(2)}, u32[]{:S(2)}) collective-permute-start(bf16[32,12,8,128]{3,2,1,0:T(8,128)(2,1)} %param.5), channel_id=1, source_target_pairs={{0,1},{1,0},{2,3},{3,2},{4,5},{5,4},{6,7},{7,6},{8,9},{9,8},{10,11... | collective-permute-start | bytes 2359304 | tf_op jit(solution)/shard_map/ppermute | solution.py:148
  20.2 13.0 %collective-permute-start.14 = (bf16[8,12,16,128]{3,2,1,0:T(8,128)(2,1)S(1)}, bf16[8,12,16,128]{3,2,1,0:T(8,128)(2,1)S(1)}, u32[]{:S(2)}, u32[]{:S(2)}) collective-permute-start(bf16[8,12,16,128]{3,2,1,0:T(8,128)(2,1)S(1)} %pad_maximum_fusion.1.refs_2_.refs_4_.refs_13_), channel_id=1, source_target_pairs={{2,0},{3,1},{4,2},{5,3},{6,4},{7,5},{8,6},{9,7},{10,8},{11,9},{12,... | collective-permute-start | bytes 1179656 | tf_op jit(solution)/shard_map/ppermute | solution.py:121
  24.6 13.4 %collective-permute-start.11 = (bf16[8,12,16,128]{3,2,1,0:T(8,128)(2,1)S(1)}, bf16[8,12,16,128]{3,2,1,0:T(8,128)(2,1)S(1)}, u32[]{:S(2)}, u32[]{:S(2)}) collective-permute-start(bf16[8,12,16,128]{3,2,1,0:T(8,128)(2,1)S(1)} %pad_maximum_fusion.1.refs_2_.refs_4_.refs_13_), channel_id=1, source_target_pairs={{0,2},{1,3},{2,4},{3,5},{4,6},{5,7},{6,8},{7,9},{8,10},{9,11},{10,... | collective-permute-start | bytes 1179656 | tf_op jit(solution)/shard_map/ppermute | solution.py:120
  26.5 21.9 %copy-start.13 = (s32[32,12,12]{0,2,1:T(8,128)S(1)}, s32[32,12,12]{0,2,1:T(8,128)}, u32[]{:S(2)}) copy-start(s32[32,12,12]{0,2,1:T(8,128)} %param.4) | copy-start | bytes 55300
  26.6 14.5 %collective-permute-start.5 = (bf16[8,12,16,128]{3,2,1,0:T(8,128)(2,1)S(1)}, bf16[8,12,16,128]{3,2,1,0:T(8,128)(2,1)S(1)}, u32[]{:S(2)}, u32[]{:S(2)}) collective-permute-start(bf16[8,12,16,128]{3,2,1,0:T(8,128)(2,1)S(1)} %pad_maximum_fusion.refs_1_.refs_4_), channel_id=1, source_target_pairs={{2,0},{3,1},{4,2},{5,3},{6,4},{7,5},{8,6},{9,7},{10,8},{11,9},{12,... | collective-permute-start | bytes 1179656 | tf_op jit(solution)/shard_map/ppermute | solution.py:121
  31.2 15.2 %collective-permute-start.2 = (bf16[8,12,16,128]{3,2,1,0:T(8,128)(2,1)S(1)}, bf16[8,12,16,128]{3,2,1,0:T(8,128)(2,1)S(1)}, u32[]{:S(2)}, u32[]{:S(2)}) collective-permute-start(bf16[8,12,16,128]{3,2,1,0:T(8,128)(2,1)S(1)} %pad_maximum_fusion.refs_1_.refs_4_), channel_id=1, source_target_pairs={{0,2},{1,3},{2,4},{3,5},{4,6},{5,7},{6,8},{7,9},{8,10},{9,11},{10,... | collective-permute-start | bytes 1179656 | tf_op jit(solution)/shard_map/ppermute | solution.py:120
  33.2 24.7 %collective-permute-start.15 = (bf16[8,12,16,128]{3,2,1,0:T(8,128)(2,1)S(1)}, bf16[8,12,16,128]{3,2,1,0:T(8,128)(2,1)}, u32[]{:S(2)}, u32[]{:S(2)}) collective-permute-start(bf16[8,12,16,128]{3,2,1,0:T(8,128)(2,1)S(1)} %collective-permute-done.14.refs_8_.refs_17_), channel_id=1, source_target_pairs={{2,0},{3,1},{4,2},{5,3},{6,4},{7,5},{8,6},{9,7},{10,8},{11,9},{12,... | collective-permute-start | bytes 1179656 | tf_op jit(solution)/shard_map/ppermute | solution.py:121
  38.0 24.8 %collective-permute-start.12 = (bf16[8,12,16,128]{3,2,1,0:T(8,128)(2,1)S(1)}, bf16[8,12,16,128]{3,2,1,0:T(8,128)(2,1)}, u32[]{:S(2)}, u32[]{:S(2)}) collective-permute-start(bf16[8,12,16,128]{3,2,1,0:T(8,128)(2,1)S(1)} %collective-permute-done.11.refs_5_.refs_14_), channel_id=1, source_target_pairs={{0,2},{1,3},{2,4},{3,5},{4,6},{5,7},{6,8},{7,9},{8,10},{9,11},{10,... | collective-permute-start | bytes 1179656 | tf_op jit(solution)/shard_map/ppermute | solution.py:120
  41.1 23.6 %collective-permute-start.6 = (bf16[8,12,16,128]{3,2,1,0:T(8,128)(2,1)S(1)}, bf16[8,12,16,128]{3,2,1,0:T(8,128)(2,1)}, u32[]{:S(2)}, u32[]{:S(2)}) collective-permute-start(bf16[8,12,16,128]{3,2,1,0:T(8,128)(2,1)S(1)} %collective-permute-done.5.refs_8_), channel_id=1, source_target_pairs={{2,0},{3,1},{4,2},{5,3},{6,4},{7,5},{8,6},{9,7},{10,8},{11,9},{12,... | collective-permute-start | bytes 1179656 | tf_op jit(solution)/shard_map/ppermute | solution.py:121
  46.4 22.9 %collective-permute-start.3 = (bf16[8,12,16,128]{3,2,1,0:T(8,128)(2,1)S(1)}, bf16[8,12,16,128]{3,2,1,0:T(8,128)(2,1)}, u32[]{:S(2)}, u32[]{:S(2)}) collective-permute-start(bf16[8,12,16,128]{3,2,1,0:T(8,128)(2,1)S(1)} %collective-permute-done.2.refs_5_), channel_id=1, source_target_pairs={{0,2},{1,3},{2,4},{3,5},{4,6},{5,7},{6,8},{7,9},{8,10},{9,11},{10,... | collective-permute-start | bytes 1179656 | tf_op jit(solution)/shard_map/ppermute | solution.py:120
  52.6 33.4 %collective-permute-start.1 = (bf16[8,12,16,128]{3,2,1,0:T(8,128)(2,1)S(1)}, bf16[8,12,16,128]{3,2,1,0:T(8,128)(2,1)}, u32[]{:S(2)}, u32[]{:S(2)}) collective-permute-start(bf16[8,12,16,128]{3,2,1,0:T(8,128)(2,1)S(1)} %pad_maximum_fusion.refs_1_.refs_4_), channel_id=1, source_target_pairs={{0,1009},{1,16},{2,1011},{3,18},{4,1013},{5,20},{6,1015},{7,22},{8... | collective-permute-start | bytes 1179656 | tf_op jit(solution)/shard_map/ppermute | solution.py:146
  57.9 14.6 %collective-permute-start.16 = (bf16[8,12,16,128]{3,2,1,0:T(8,128)(2,1)}, bf16[8,12,16,128]{3,2,1,0:T(8,128)(2,1)S(1)}, u32[]{:S(2)}, u32[]{:S(2)}) collective-permute-start(bf16[8,12,16,128]{3,2,1,0:T(8,128)(2,1)} %collective-permute-done.15.refs_9_.refs_18_), channel_id=1, source_target_pairs={{2,0},{3,1},{4,2},{5,3},{6,4},{7,5},{8,6},{9,7},{10,8},{11,9},{12,... | collective-permute-start | bytes 1179656 | tf_op jit(solution)/shard_map/ppermute | solution.py:121
  62.8 14.4 %collective-permute-start.13 = (bf16[8,12,16,128]{3,2,1,0:T(8,128)(2,1)}, bf16[8,12,16,128]{3,2,1,0:T(8,128)(2,1)S(1)}, u32[]{:S(2)}, u32[]{:S(2)}) collective-permute-start(bf16[8,12,16,128]{3,2,1,0:T(8,128)(2,1)} %collective-permute-done.12.refs_6_.refs_15_), channel_id=1, source_target_pairs={{0,2},{1,3},{2,4},{3,5},{4,6},{5,7},{6,8},{7,9},{8,10},{9,11},{10,... | collective-permute-start | bytes 1179656 | tf_op jit(solution)/shard_map/ppermute | solution.py:120
  64.7 14.4 %collective-permute-start.7 = (bf16[8,12,16,128]{3,2,1,0:T(8,128)(2,1)}, bf16[8,12,16,128]{3,2,1,0:T(8,128)(2,1)S(1)}, u32[]{:S(2)}, u32[]{:S(2)}) collective-permute-start(bf16[8,12,16,128]{3,2,1,0:T(8,128)(2,1)} %collective-permute-done.6.refs_9_), channel_id=1, source_target_pairs={{2,0},{3,1},{4,2},{5,3},{6,4},{7,5},{8,6},{9,7},{10,8},{11,9},{12,... | collective-permute-start | bytes 1179656 | tf_op jit(solution)/shard_map/ppermute | solution.py:121
  69.3 14.6 %collective-permute-start.4 = (bf16[8,12,16,128]{3,2,1,0:T(8,128)(2,1)}, bf16[8,12,16,128]{3,2,1,0:T(8,128)(2,1)S(1)}, u32[]{:S(2)}, u32[]{:S(2)}) collective-permute-start(bf16[8,12,16,128]{3,2,1,0:T(8,128)(2,1)} %collective-permute-done.3.refs_6_), channel_id=1, source_target_pairs={{0,2},{1,3},{2,4},{3,5},{4,6},{5,7},{6,8},{7,9},{8,10},{9,11},{10,... | collective-permute-start | bytes 1179656 | tf_op jit(solution)/shard_map/ppermute | solution.py:120
  72.6 32.1 %collective-permute-start.18 = (bf16[4,12,16,128]{3,2,1,0:T(8,128)(2,1)S(1)}, bf16[4,12,16,128]{3,2,1,0:T(8,128)(2,1)S(1)}, u32[]{:S(2)}, u32[]{:S(2)}) collective-permute-start(bf16[4,12,16,128]{3,2,1,0:T(8,128)(2,1)S(1)} %slice.47), channel_id=1, source_target_pairs={{2,0},{3,1},{4,2},{5,3},{6,4},{7,5},{8,6},{9,7},{10,8},{11,9},{12,... | collective-permute-start | bytes 589832 | tf_op jit(solution)/shard_map/ppermute | solution.py:126
  77.2 27.5 %collective-permute-start.17 = (bf16[4,12,16,128]{3,2,1,0:T(8,128)(2,1)S(1)}, bf16[4,12,16,128]{3,2,1,0:T(8,128)(2,1)S(1)}, u32[]{:S(2)}, u32[]{:S(2)}) collective-permute-start(bf16[4,12,16,128]{3,2,1,0:T(8,128)(2,1)S(1)} %slice.46), channel_id=1, source_target_pairs={{0,2},{1,3},{2,4},{3,5},{4,6},{5,7},{6,8},{7,9},{8,10},{9,11},{10,... | collective-permute-start | bytes 589832 | tf_op jit(solution)/shard_map/ppermute | solution.py:125
  79.1 6.8 %copy-start.11 = (bf16[8,12,8,128]{3,2,1,0:T(8,128)(2,1)S(1)}, bf16[8,12,8,128]{3,2,1,0:T(8,128)(2,1)}, u32[]{:S(2)}) copy-start(bf16[8,12,8,128]{3,2,1,0:T(8,128)(2,1)} %get-tuple-element.11) | copy-start | bytes 589828
  79.2 7.5 %collective-permute-start.9 = (bf16[4,12,16,128]{3,2,1,0:T(8,128)(2,1)S(1)}, bf16[4,12,16,128]{3,2,1,0:T(8,128)(2,1)S(1)}, u32[]{:S(2)}, u32[]{:S(2)}) collective-permute-start(bf16[4,12,16,128]{3,2,1,0:T(8,128)(2,1)S(1)} %slice.44), channel_id=1, source_target_pairs={{2,0},{3,1},{4,2},{5,3},{6,4},{7,5},{8,6},{9,7},{10,8},{11,9},{12,... | collective-permute-start | bytes 589832 | tf_op jit(solution)/shard_map/ppermute | solution.py:126
  83.9 7.9 %collective-permute-start.8 = (bf16[4,12,16,128]{3,2,1,0:T(8,128)(2,1)S(1)}, bf16[4,12,16,128]{3,2,1,0:T(8,128)(2,1)S(1)}, u32[]{:S(2)}, u32[]{:S(2)}) collective-permute-start(bf16[4,12,16,128]{3,2,1,0:T(8,128)(2,1)S(1)} %slice.43), channel_id=1, source_target_pairs={{0,2},{1,3},{2,4},{3,5},{4,6},{5,7},{6,8},{7,9},{8,10},{9,11},{10,... | collective-permute-start | bytes 589832 | tf_op jit(solution)/shard_map/ppermute | solution.py:125
  86.6 10.6 %copy-start.7 = (bf16[4,12,16,128]{3,2,1,0:T(8,128)(2,1)}, bf16[4,12,16,128]{3,2,1,0:T(8,128)(2,1)S(1)}, u32[]{:S(2)}) copy-start(bf16[4,12,16,128]{3,2,1,0:T(8,128)(2,1)S(1)} %collective-permute-done.9.refs_12_) | copy-start | bytes 589828
  97.2 15.9 %collective-permute-start.10 = (bf16[8,12,16,128]{3,2,1,0:T(8,128)(2,1)}, bf16[8,12,16,128]{3,2,1,0:T(8,128)(2,1)}, u32[]{:S(2)}, u32[]{:S(2)}) collective-permute-start(bf16[8,12,16,128]{3,2,1,0:T(8,128)(2,1)} %shard_map.37.refs_1_), channel_id=1, source_target_pairs={{0,1009},{1,16},{2,1011},{3,18},{4,1013},{5,20},{6,1015},{7,22},{8... | collective-permute-start | bytes 1179656 | tf_op jit(solution)/shard_map/ppermute | solution.py:146
  110.2 4.0 %collective-permute-start.19 = (bf16[8,12,16,128]{3,2,1,0:T(8,128)(2,1)}, bf16[8,12,16,128]{3,2,1,0:T(8,128)(2,1)}, u32[]{:S(2)}, u32[]{:S(2)}) collective-permute-start(bf16[8,12,16,128]{3,2,1,0:T(8,128)(2,1)} %shard_map.38.refs_2_), channel_id=1, source_target_pairs={{0,1},{1,0},{2,3},{3,2},{4,5},{5,4},{6,7},{7,6},{8,9},{9,8},{10,11... | collective-permute-start | bytes 1179656 | tf_op jit(solution)/shard_map/ppermute | solution.py:176
  126.6 5.0 %collective-permute-start.20 = (bf16[16,12,8,128]{3,2,1,0:T(8,128)(2,1)S(1)}, bf16[16,12,8,128]{3,2,1,0:T(8,128)(2,1)S(1)}, u32[]{:S(2)}, u32[]{:S(2)}) collective-permute-start(bf16[16,12,8,128]{3,2,1,0:T(8,128)(2,1)S(1)} %get-tuple-element.8), channel_id=1, source_target_pairs={{0,1},{1,0},{2,3},{3,2},{4,5},{5,4},{6,7},{7,6},{8,9},{9,8},{10,11... | collective-permute-start | bytes 1179656 | tf_op jit(solution)/shard_map/ppermute | solution.py:179
  (13 other events, 43.0 us)

commit v2 on v1

v2 whole, which is shorter than its diff:
```python
import functools

import jax
import jax.numpy as jnp
from jax import lax
from jax.experimental import pallas as pl
from jax.experimental.pallas import tpu as pltpu
from jax.sharding import PartitionSpec as P

GROUP = 4
COST = 10


def product_kernel(first_block, is_first, scale, extra, where_ref, index_ref, *refs):
    parts, pieces = refs[:3], refs[3:12]
    outs, (window, left, window_sem, left_sem) = refs[12 + extra:-4], refs[-4:]
    rows, slots, width, size = parts[0].shape
    ring = size // width
    z, core = where_ref[0], where_ref[1]
    first_row = rows * where_ref[2 + first_block]

    window_copies = []
    for k, part in enumerate(parts):
        to = window.at[pl.ds(rows * (first_block + k), rows), pl.ds(0, slots)]
        window_copies.append(pltpu.make_async_copy(part, to, window_sem.at[k]))
    left_copies = []
    for g in range(2):
        group_copies = []
        for k in range(ring):
            away = (0, -1, -2, -3, 1, 2, 3, 4)[k]
            source = pieces[8] if k == 7 and g == 1 else pieces[k]
            from_rows = pl.ds(0 if k == 7 else GROUP * g, GROUP)
            slot = lax.rem(z + away + ring, ring)
            to = left.at[pl.ds(GROUP * g, GROUP), :, slot]
            group_copies.append(pltpu.make_async_copy(source.at[from_rows], to, left_sem.at[g, k]))
        left_copies.append(group_copies)
    for copy in window_copies + left_copies[0] + left_copies[1]:
        copy.start()
    window[4 * rows, 0] = jnp.zeros((width, size), window.dtype)
    tile_at = window.reshape(window.shape[0] * window.shape[1], width, size)
    for copy in window_copies:
        copy.wait()

    def one_row(i, carry):
        total = jnp.zeros((slots * width, size), jnp.float32)
        for t in range(0, slots, 2):
            columns = []
            for u in (t, t + 1):
                tiles = [tile_at[lax.shift_right_logical(index_ref[u % 4, s, first_row + i], 10 * (u // 4)) & 1023] for s in range(slots)]
                columns.append(jnp.concatenate(tiles, axis=0))
            picked = jnp.concatenate(columns, axis=1)
            blocks = left[i, pl.ds(t, 2)].reshape(2 * size, size)
            total += jnp.dot(picked, blocks, preferred_element_type=jnp.float32)
        total = (total * scale).reshape(slots, width, size)
        if is_first:
            (out,) = outs
            out[i] = (-total).astype(out.dtype)
            line = lax.broadcasted_iota(jnp.int32, (width, size), 0)
            lane = lax.broadcasted_iota(jnp.int32, (width, size), 1)
            diagonal = jnp.where(lane == line + z * width, 3.0, 0.0)
            out[i, 0] = (diagonal - total[0]).astype(out.dtype)
        else:
            keep, send = outs
            low, high = total[:, :width // 2], total[:, width // 2:]
            keep[i] = jnp.where(core == 0, low, high).astype(keep.dtype)
            send[i] = jnp.where(core == 0, high, low).astype(send.dtype)
        return carry

    for g in range(2):
        for copy in left_copies[g]:
            copy.wait()
        lax.fori_loop(GROUP * g, GROUP * (g + 1), one_row, 0, unroll=GROUP)


def product(first_block, is_first, scale, where, index, parts, pieces, after=()):
    rows, slots, width, size = parts[0].shape
    dtype = parts[0].dtype
    if is_first:
        outs = jax.ShapeDtypeStruct((rows, slots, width, size), dtype)
        out_specs = pl.BlockSpec(memory_space=pltpu.VMEM)
    else:
        outs = [jax.ShapeDtypeStruct((rows, slots, width // 2, size), dtype)] * 2
        out_specs = [pl.BlockSpec(memory_space=pltpu.VMEM)] * 2
    flops = 2 * rows * slots * slots * width * size * size
    return pl.pallas_call(
        functools.partial(product_kernel, first_block, is_first, scale, len(after)),
        out_shape=outs,
        in_specs=[pl.BlockSpec(memory_space=pltpu.SMEM)] * 2 + [pl.BlockSpec(memory_space=pl.ANY)] * (12 + len(after)),
        out_specs=out_specs,
        scratch_shapes=[
            pltpu.VMEM((4 * rows + 1, 16, width, size), dtype),
            pltpu.VMEM((rows, slots, size // width, width, size), dtype),
            pltpu.SemaphoreType.DMA((3,)),
            pltpu.SemaphoreType.DMA((2, size // width)),
        ],
        compiler_params=pltpu.CompilerParams(vmem_limit_bytes=12 * 2**20),
        cost_estimate=pl.CostEstimate(flops=COST * flops, bytes_accessed=rows * slots * size * size * 2, transcendentals=0),
    )(where, index, *parts, *pieces, *after)


def gather_ring(streams, ring):
    count = 2 * ring
    up = [(i, (i + 2) % count) for i in range(count)]
    down = [((i + 2) % count, i) for i in range(count)]
    risen = [[piece] for piece in streams]
    fallen = [[piece] for piece in streams]
    for step in range(ring // 2 - 1):
        for k in range(len(streams)):
            risen[k].append(lax.ppermute(risen[k][-1], "cols", up))
            fallen[k].append(lax.ppermute(fallen[k][-1], "cols", down))
    gathered = []
    for k in range(len(streams)):
        half = streams[k].shape[0] // 2
        last_up = lax.ppermute(risen[k][-1][:half], "cols", up)
        last_down = lax.ppermute(fallen[k][-1][half:], "cols", down)
        gathered.append(risen[k] + fallen[k][1:] + [last_up, last_down])
    return gathered


def local(columns, fetch, values):
    rows_here, slots, half_width, size = values.shape
    cols = lax.axis_size("cols")
    count = lax.axis_size("rows")
    col = lax.axis_index("cols")
    z, core = col // 2, col % 2
    first = core == 0
    swap = [(i, i ^ 1) for i in range(cols)]

    def outward(piece):
        pairs = []
        for r in range(count):
            for c in range(cols):
                to = ((r - 1) % count, c + 1) if c % 2 == 0 else ((r + 1) % count, c - 1)
                pairs.append((r * cols + c, to[0] * cols + to[1]))
        return lax.ppermute(piece, ("rows", "cols"), pairs)

    other = lax.ppermute(values, "cols", swap)

    def joined(number):
        start = jnp.where(first, 8 * number, 24 - 8 * number)
        mine = lax.dynamic_slice_in_dim(values, start, 8, 0)
        theirs = lax.dynamic_slice_in_dim(other, start, 8, 0)
        low = jnp.where(first, mine, theirs)
        high = jnp.where(first, theirs, mine)
        return jnp.concatenate([low, high], axis=2)

    outer_rows, inner_rows, beyond = joined(0), joined(1), joined(2)
    outer_pieces, inner_pieces = gather_ring([outer_rows, inner_rows], cols // 2)

    origin = lax.axis_index("rows") * rows_here + core * 16
    total = rows_here * count
    away = (columns - origin + total // 2) % total - total // 2 + 8
    part = jnp.where(first, away // 8, 3 - away // 8)
    place = (part * 8 + away % 8) * 16
    index = jnp.where(fetch >= 0, place[:, :, None] + fetch, 32 * 16).transpose(1, 2, 0)
    index = index[:4] + index[4:8] * 1024 + index[8:] * 1024**2
    where = jnp.stack([z, core, 3 * core, 1 + core]).astype(jnp.int32)

    scale = 1.0 / (slots * size)
    shifted_outer = product(0, True, scale, where, index, (outward(outer_rows), outer_rows, inner_rows), outer_pieces)
    shifted_outward = outward(shifted_outer)
    shifted_inner = product(1, True, scale, where, index, (outer_rows, inner_rows, beyond), inner_pieces, [shifted_outer])
    shifted_beyond = lax.ppermute(shifted_inner, "cols", swap)
    keep_outer, send_outer = product(
        0, False, 0.5, where, index, (shifted_outward, shifted_outer, shifted_inner), outer_pieces
    )
    got_outer = lax.ppermute(send_outer, "cols", swap)
    keep_inner, send_inner = product(
        1, False, 0.5, where, index, (shifted_outer, shifted_inner, shifted_beyond), inner_pieces, [keep_outer]
    )
    got_inner = lax.ppermute(send_inner, "cols", swap)
    for_first = jnp.concatenate([keep_outer, keep_inner, got_inner, got_outer])
    for_second = jnp.concatenate([got_outer, got_inner, keep_inner, keep_outer])
    return jnp.where(first, for_first, for_second)


def solution(mesh):
    in_specs = (P("rows", None), P("rows", None, None), P("rows", None, "cols", None))
    out_specs = P("rows", None, "cols", None)
    return jax.shard_map(local, mesh=mesh, in_specs=in_specs, out_specs=out_specs, check_vma=False)
```

time: 134 us -> 119 us (0.89)
  local copies, waits for them, and re-layouts: 10.3 us -> 0.07 us
  waiting for transfers between devices: 11.4 us -> 7.62 us
  Pallas kernels: 18.6 us -> 15.4 us
  starting transfers between devices: 87.8 us -> 90.9 us
    unnamed x32 -> x2, local copies, waits for them, and re-layouts: 5.31 us -> 0.01 us
    ppermute x2, waiting for transfers between devices: 5.14 us -> 0.01 us  [gather_ring(): last_up = lax.ppermute(risen[k][-1][:half], 'cols', up)]
    ppermute x1 -> x2, starting transfers between devices: 3.62 us -> 7.73 us  [the longest x1 5.81 us: local(): got_outer = lax.ppermute(send_outer, 'cols', swap)]
    ppermute x6, waiting for transfers between devices: 0.02 us -> 4.11 us  [gather_ring(): risen[k].append(lax.ppermute(risen[k][-1], 'cols', up))]
    ppermute x1, starting transfers between devices: 2.26 us -> 6.19 us  [local(): shifted_beyond = lax.ppermute(shifted_inner, 'cols', swap)]
    ppermute x2, starting transfers between devices: 12.7 us -> 9 us  [outward(): return lax.ppermute(piece, ('rows', 'cols'), pairs)]
    pallas_call x3 -> x4, Pallas kernels: 18.6 us -> 15.4 us  [product(): pl.pallas_call(functools.partial(product_kernel, first_block, is_first, s...]
    rev x1 -> x0, local copies, waits for them, and re-layouts: 2.94 us -> none  [local(): index = jnp.where(first, index[:2], index[:1:-1])]
  transfers between devices with their start and end apart: 21 -> 22, of which waited for: 6 -> 5; matrix products, arithmetic and copies ran while one was open for 4% -> 1% of each run, Pallas kernels for 8% -> 13%
where the time goes in v2:
time: 119 us; the launch traced here: 118 us
  starting transfers between devices  90.9 us (76%)
  Pallas kernels  15.4 us (13%)
  waiting for transfers between devices  7.62 us (6%)
  other arithmetic  3.5 us (3%)
    ppermute x6, starting transfers between devices, gather_ring(): fallen[k].append(lax.ppermute(fallen[k][-1], 'cols', down))  27.4 us
    ppermute x1, starting transfers between devices, local(): other = lax.ppermute(values, 'cols', swap)  16.1 us
    pallas_call x4, Pallas kernels, product(): pl.pallas_call(functools.partial(product_kernel, first_block, is_first, s...  15.4 us
    ppermute x6, starting transfers between devices, gather_ring(): risen[k].append(lax.ppermute(risen[k][-1], 'cols', up))  11.5 us
    ppermute x2, starting transfers between devices, gather_ring(): last_down = lax.ppermute(fallen[k][-1][half:], 'cols', down)  9.15 us
    ppermute x2, starting transfers between devices, outward(): return lax.ppermute(piece, ('rows', 'cols'), pairs)  9 us
    ppermute x1, starting transfers between devices, local(): shifted_beyond = lax.ppermute(shifted_inner, 'cols', swap)  6.19 us
    ppermute x1, starting transfers between devices, local(): got_outer = lax.ppermute(send_outer, 'cols', swap)  5.81 us
  transfers between devices with their start and end apart: 22, of which 5 were waited for; matrix products, arithmetic and copies ran while one was open for 1% of the time, Pallas kernels for 13%

profile of v2, /device:TPU:1, one launch (start us, length us, event | category | flops | bytes accessed | tf_op | source)
XLA Modules:
  0.0 117.9 jit_solution(6037505668691051159)
XLA Ops:
  0.0 16.1 %collective-permute-start = (bf16[32,12,8,128]{3,2,1,0:T(8,128)(2,1)}, bf16[32,12,8,128]{3,2,1,0:T(8,128)(2,1)S(1)}, u32[]{:S(2)}, u32[]{:S(2)}) collective-permute-start(bf16[32,12,8,128]{3,2,1,0:T(8,128)(2,1)} %param.5), channel_id=1, source_target_pairs={{0,1},{1,0},{2,3},{3,2},{4,5},{5,4},{6,7},{7,6},{8,9},{9,8},{10,11... | collective-permute-start | bytes 2359304 | tf_op jit(solution)/shard_map/ppermute | solution.py:137
  16.1 2.1 %collective-permute-done = bf16[32,12,8,128]{3,2,1,0:T(8,128)(2,1)S(1)} collective-permute-done((bf16[32,12,8,128]{3,2,1,0:T(8,128)(2,1)}, bf16[32,12,8,128]{3,2,1,0:T(8,128)(2,1)S(1)}, u32[]{:S(2)}, u32[]{:S(2)}) %collective-permute-start) | collective-permute-done | bytes 786464 | tf_op jit(solution)/shard_map/ppermute | solution.py:137
  19.4 1.9 %collective-permute-start.2 = (bf16[8,12,16,128]{3,2,1,0:T(8,128)(2,1)S(1)}, bf16[8,12,16,128]{3,2,1,0:T(8,128)(2,1)S(1)}, u32[]{:S(2)}, u32[]{:S(2)}) collective-permute-start(bf16[8,12,16,128]{3,2,1,0:T(8,128)(2,1)S(1)} %pad_maximum_fusion.refs_1_.refs_3_.refs_0_), channel_id=1, source_target_pairs={{0,2},{1,3},{2,4},{3,5},{4,6},{5,7},{6,8},{7,9},{8,10},{9,11},{10,... | collective-permute-start | bytes 1179656 | tf_op jit(solution)/shard_map/ppermute | solution.py:109
  21.4 4.6 %collective-permute-start.5 = (bf16[8,12,16,128]{3,2,1,0:T(8,128)(2,1)S(1)}, bf16[8,12,16,128]{3,2,1,0:T(8,128)(2,1)S(1)}, u32[]{:S(2)}, u32[]{:S(2)}) collective-permute-start(bf16[8,12,16,128]{3,2,1,0:T(8,128)(2,1)S(1)} %pad_maximum_fusion.refs_1_.refs_3_.refs_0_), channel_id=1, source_target_pairs={{2,0},{3,1},{4,2},{5,3},{6,4},{7,5},{8,6},{9,7},{10,8},{11,9},{12,... | collective-permute-start | bytes 1179656 | tf_op jit(solution)/shard_map/ppermute | solution.py:110
  26.0 1.9 %collective-permute-start.11 = (bf16[8,12,16,128]{3,2,1,0:T(8,128)(2,1)S(1)}, bf16[8,12,16,128]{3,2,1,0:T(8,128)(2,1)S(1)}, u32[]{:S(2)}, u32[]{:S(2)}) collective-permute-start(bf16[8,12,16,128]{3,2,1,0:T(8,128)(2,1)S(1)} %pad_maximum_fusion.1.refs_2_.refs_1_.refs_3_), channel_id=1, source_target_pairs={{0,2},{1,3},{2,4},{3,5},{4,6},{5,7},{6,8},{7,9},{8,10},{9,11},{10,... | collective-permute-start | bytes 1179656 | tf_op jit(solution)/shard_map/ppermute | solution.py:109
  28.0 4.6 %collective-permute-start.14 = (bf16[8,12,16,128]{3,2,1,0:T(8,128)(2,1)S(1)}, bf16[8,12,16,128]{3,2,1,0:T(8,128)(2,1)S(1)}, u32[]{:S(2)}, u32[]{:S(2)}) collective-permute-start(bf16[8,12,16,128]{3,2,1,0:T(8,128)(2,1)S(1)} %pad_maximum_fusion.1.refs_2_.refs_1_.refs_3_), channel_id=1, source_target_pairs={{2,0},{3,1},{4,2},{5,3},{6,4},{7,5},{8,6},{9,7},{10,8},{11,9},{12,... | collective-permute-start | bytes 1179656 | tf_op jit(solution)/shard_map/ppermute | solution.py:110
  34.8 4.6 %collective-permute-start.6 = (bf16[8,12,16,128]{3,2,1,0:T(8,128)(2,1)S(1)}, bf16[8,12,16,128]{3,2,1,0:T(8,128)(2,1)S(1)}, u32[]{:S(2)}, u32[]{:S(2)}) collective-permute-start(bf16[8,12,16,128]{3,2,1,0:T(8,128)(2,1)S(1)} %collective-permute-done.5.refs_7_), channel_id=1, source_target_pairs={{2,0},{3,1},{4,2},{5,3},{6,4},{7,5},{8,6},{9,7},{10,8},{11,9},{12,... | collective-permute-start | bytes 1179656 | tf_op jit(solution)/shard_map/ppermute | solution.py:110
  43.2 4.6 %collective-permute-start.15 = (bf16[8,12,16,128]{3,2,1,0:T(8,128)(2,1)S(1)}, bf16[8,12,16,128]{3,2,1,0:T(8,128)(2,1)S(1)}, u32[]{:S(2)}, u32[]{:S(2)}) collective-permute-start(bf16[8,12,16,128]{3,2,1,0:T(8,128)(2,1)S(1)} %collective-permute-done.14.refs_7_), channel_id=1, source_target_pairs={{2,0},{3,1},{4,2},{5,3},{6,4},{7,5},{8,6},{9,7},{10,8},{11,9},{12,... | collective-permute-start | bytes 1179656 | tf_op jit(solution)/shard_map/ppermute | solution.py:110
  51.7 4.6 %collective-permute-start.7 = (bf16[8,12,16,128]{3,2,1,0:T(8,128)(2,1)S(1)}, bf16[8,12,16,128]{3,2,1,0:T(8,128)(2,1)S(1)}, u32[]{:S(2)}, u32[]{:S(2)}) collective-permute-start(bf16[8,12,16,128]{3,2,1,0:T(8,128)(2,1)S(1)} %collective-permute-done.6.refs_8_), channel_id=1, source_target_pairs={{2,0},{3,1},{4,2},{5,3},{6,4},{7,5},{8,6},{9,7},{10,8},{11,9},{12,... | collective-permute-start | bytes 1179656 | tf_op jit(solution)/shard_map/ppermute | solution.py:110
  57.1 5.1 %collective-permute-start.1 = (bf16[8,12,16,128]{3,2,1,0:T(8,128)(2,1)S(1)}, bf16[8,12,16,128]{3,2,1,0:T(8,128)(2,1)S(1)}, u32[]{:S(2)}, u32[]{:S(2)}) collective-permute-start(bf16[8,12,16,128]{3,2,1,0:T(8,128)(2,1)S(1)} %pad_maximum_fusion.refs_1_.refs_3_.refs_0_), channel_id=1, source_target_pairs={{0,1009},{1,16},{2,1011},{3,18},{4,1013},{5,20},{6,1015},{7,22},{8... | collective-permute-start | bytes 1179656 | tf_op jit(solution)/shard_map/ppermute | solution.py:135
  62.3 1.9 %collective-permute-start.13 = (bf16[8,12,16,128]{3,2,1,0:T(8,128)(2,1)S(1)}, bf16[8,12,16,128]{3,2,1,0:T(8,128)(2,1)S(1)}, u32[]{:S(2)}, u32[]{:S(2)}) collective-permute-start(bf16[8,12,16,128]{3,2,1,0:T(8,128)(2,1)S(1)} %collective-permute-done.12.refs_5_), channel_id=1, source_target_pairs={{0,2},{1,3},{2,4},{3,5},{4,6},{5,7},{6,8},{7,9},{8,10},{9,11},{10,... | collective-permute-start | bytes 1179656 | tf_op jit(solution)/shard_map/ppermute | solution.py:109
  64.2 4.6 %collective-permute-start.16 = (bf16[8,12,16,128]{3,2,1,0:T(8,128)(2,1)S(1)}, bf16[8,12,16,128]{3,2,1,0:T(8,128)(2,1)S(1)}, u32[]{:S(2)}, u32[]{:S(2)}) collective-permute-start(bf16[8,12,16,128]{3,2,1,0:T(8,128)(2,1)S(1)} %collective-permute-done.15.refs_8_), channel_id=1, source_target_pairs={{2,0},{3,1},{4,2},{5,3},{6,4},{7,5},{8,6},{9,7},{10,8},{11,9},{12,... | collective-permute-start | bytes 1179656 | tf_op jit(solution)/shard_map/ppermute | solution.py:110
  68.8 1.9 %collective-permute-start.8 = (bf16[4,12,16,128]{3,2,1,0:T(8,128)(2,1)S(1)}, bf16[4,12,16,128]{3,2,1,0:T(8,128)(2,1)S(1)}, u32[]{:S(2)}, u32[]{:S(2)}) collective-permute-start(bf16[4,12,16,128]{3,2,1,0:T(8,128)(2,1)S(1)} %slice.31), channel_id=1, source_target_pairs={{0,2},{1,3},{2,4},{3,5},{4,6},{5,7},{6,8},{7,9},{8,10},{9,11},{10,... | collective-permute-start | bytes 589832 | tf_op jit(solution)/shard_map/ppermute | solution.py:114
  70.8 4.6 %collective-permute-start.9 = (bf16[4,12,16,128]{3,2,1,0:T(8,128)(2,1)S(1)}, bf16[4,12,16,128]{3,2,1,0:T(8,128)(2,1)S(1)}, u32[]{:S(2)}, u32[]{:S(2)}) collective-permute-start(bf16[4,12,16,128]{3,2,1,0:T(8,128)(2,1)S(1)} %slice.32), channel_id=1, source_target_pairs={{2,0},{3,1},{4,2},{5,3},{6,4},{7,5},{8,6},{9,7},{10,8},{11,9},{12,... | collective-permute-start | bytes 589832 | tf_op jit(solution)/shard_map/ppermute | solution.py:115
  75.6 1.9 %collective-permute-start.17 = (bf16[4,12,16,128]{3,2,1,0:T(8,128)(2,1)S(1)}, bf16[4,12,16,128]{3,2,1,0:T(8,128)(2,1)S(1)}, u32[]{:S(2)}, u32[]{:S(2)}) collective-permute-start(bf16[4,12,16,128]{3,2,1,0:T(8,128)(2,1)S(1)} %slice.33), channel_id=1, source_target_pairs={{0,2},{1,3},{2,4},{3,5},{4,6},{5,7},{6,8},{7,9},{8,10},{9,11},{10,... | collective-permute-start | bytes 589832 | tf_op jit(solution)/shard_map/ppermute | solution.py:114
  77.5 4.6 %collective-permute-start.18 = (bf16[4,12,16,128]{3,2,1,0:T(8,128)(2,1)S(1)}, bf16[4,12,16,128]{3,2,1,0:T(8,128)(2,1)S(1)}, u32[]{:S(2)}, u32[]{:S(2)}) collective-permute-start(bf16[4,12,16,128]{3,2,1,0:T(8,128)(2,1)S(1)} %slice.34), channel_id=1, source_target_pairs={{2,0},{3,1},{4,2},{5,3},{6,4},{7,5},{8,6},{9,7},{10,8},{11,9},{12,... | collective-permute-start | bytes 589832 | tf_op jit(solution)/shard_map/ppermute | solution.py:115
  82.1 3.8 %shard_map.37.refs_12_.refs_1_.refs_0_ = bf16[8,12,16,128]{3,2,1,0:T(8,128)(2,1)S(1)} custom-call(s32[4]{0:T(128)S(1)} %pad_add_fusion.where_ref, s32[4,12,32]{2,1,0:T(8,128)S(1)} %fusion.index_ref, bf16[8,12,16,128]{3,2,1,0:T(8,128)(2,1)S(1)} %collective-permute-done.1.refs_0_, bf16[8,12,16,128]{3,2,1,0:T(8,128)(2,1)S(1)} %pad_maximum_fusion.refs_1_.refs_3_.refs_0_, ...), custom_call_target="tpu_custom_call" | custom-call | flops 6039797760 | bytes 3145728 | tf_op jit(solution)/shard_map/pallas_call | solution.py:85
  86.0 3.9 %collective-permute-start.10 = (bf16[8,12,16,128]{3,2,1,0:T(8,128)(2,1)S(1)}, bf16[8,12,16,128]{3,2,1,0:T(8,128)(2,1)S(1)}, u32[]{:S(2)}, u32[]{:S(2)}) collective-permute-start(bf16[8,12,16,128]{3,2,1,0:T(8,128)(2,1)S(1)} %shard_map.37.refs_12_.refs_1_.refs_0_), channel_id=1, source_target_pairs={{0,1009},{1,16},{2,1011},{3,18},{4,1013},{5,20},{6,1015},{7,22},{8... | collective-permute-start | bytes 1179656 | tf_op jit(solution)/shard_map/ppermute | solution.py:135
  89.9 3.8 %shard_map.38.refs_2_.refs_1_ = bf16[8,12,16,128]{3,2,1,0:T(8,128)(2,1)S(1)} custom-call(s32[4]{0:T(128)S(1)} %pad_add_fusion.where_ref, s32[4,12,32]{2,1,0:T(8,128)S(1)} %fusion.index_ref, bf16[8,12,16,128]{3,2,1,0:T(8,128)(2,1)S(1)} %pad_maximum_fusion.refs_1_.refs_3_.refs_0_, bf16[8,12,16,128]{3,2,1,0:T(8,128)(2,1)S(1)} %pad_maximum_fusion.1.refs_2_.refs_1_.refs_3_, ...), custom_call_target="tpu_custom_call" | custom-call | flops 6039797760 | bytes 3145728 | tf_op jit(solution)/shard_map/pallas_call | solution.py:85
  93.8 6.2 %collective-permute-start.19 = (bf16[8,12,16,128]{3,2,1,0:T(8,128)(2,1)S(1)}, bf16[8,12,16,128]{3,2,1,0:T(8,128)(2,1)S(1)}, u32[]{:S(2)}, u32[]{:S(2)}) collective-permute-start(bf16[8,12,16,128]{3,2,1,0:T(8,128)(2,1)S(1)} %shard_map.38.refs_2_.refs_1_), channel_id=1, source_target_pairs={{0,1},{1,0},{2,3},{3,2},{4,5},{5,4},{6,7},{7,6},{8,9},{9,8},{10,11... | collective-permute-start | bytes 1179656 | tf_op jit(solution)/shard_map/ppermute | solution.py:163
  100.0 3.8 %shard_map.39 = (bf16[8,12,8,128]{3,2,1,0:T(8,128)(2,1)S(1)}, bf16[8,12,8,128]{3,2,1,0:T(8,128)(2,1)S(1)}) custom-call(s32[4]{0:T(128)S(1)} %pad_add_fusion.where_ref, s32[4,12,32]{2,1,0:T(8,128)S(1)} %fusion.index_ref, bf16[8,12,16,128]{3,2,1,0:T(8,128)(2,1)S(1)} %collective-permute-done.10.refs_0_, ...), custom_call_target="tpu_custom_call" | custom-call | flops 6039797760 | bytes 3145728 | tf_op jit(solution)/shard_map/pallas_call | solution.py:85
  103.8 5.8 %collective-permute-start.21 = (bf16[8,12,8,128]{3,2,1,0:T(8,128)(2,1)S(1)}, bf16[8,12,8,128]{3,2,1,0:T(8,128)(2,1)S(1)}, u32[]{:S(2)}, u32[]{:S(2)}) collective-permute-start(bf16[8,12,8,128]{3,2,1,0:T(8,128)(2,1)S(1)} %get-tuple-element.12), channel_id=1, source_target_pairs={{0,1},{1,0},{2,3},{3,2},{4,5},{5,4},{6,7},{7,6},{8,9},{9,8},{10,11... | collective-permute-start | bytes 589832 | tf_op jit(solution)/shard_map/ppermute | solution.py:167
  109.6 3.8 %shard_map.40 = (bf16[8,12,8,128]{3,2,1,0:T(8,128)(2,1)S(1)}, bf16[8,12,8,128]{3,2,1,0:T(8,128)(2,1)S(1)}) custom-call(s32[4]{0:T(128)S(1)} %pad_add_fusion.where_ref, s32[4,12,32]{2,1,0:T(8,128)S(1)} %fusion.index_ref, bf16[8,12,16,128]{3,2,1,0:T(8,128)(2,1)S(1)} %shard_map.37.refs_12_.refs_1_.refs_0_, ...), custom_call_target="tpu_custom_call" | custom-call | flops 6039797760 | bytes 3145728 | tf_op jit(solution)/shard_map/pallas_call | solution.py:85
  113.5 1.9 %collective-permute-start.20 = (bf16[8,12,8,128]{3,2,1,0:T(8,128)(2,1)S(1)}, bf16[8,12,8,128]{3,2,1,0:T(8,128)(2,1)S(1)}, u32[]{:S(2)}, u32[]{:S(2)}) collective-permute-start(bf16[8,12,8,128]{3,2,1,0:T(8,128)(2,1)S(1)} %get-tuple-element.11), channel_id=1, source_target_pairs={{0,1},{1,0},{2,3},{3,2},{4,5},{5,4},{6,7},{7,6},{8,9},{9,8},{10,11... | collective-permute-start | bytes 589832 | tf_op jit(solution)/shard_map/ppermute | solution.py:171
  (39 shorter events, 14.8 us)
Async XLA Ops:
  0.0 18.2 %collective-permute-start = (bf16[32,12,8,128]{3,2,1,0:T(8,128)(2,1)}, bf16[32,12,8,128]{3,2,1,0:T(8,128)(2,1)S(1)}, u32[]{:S(2)}, u32[]{:S(2)}) collective-permute-start(bf16[32,12,8,128]{3,2,1,0:T(8,128)(2,1)} %param.5), channel_id=1, source_target_pairs={{0,1},{1,0},{2,3},{3,2},{4,5},{5,4},{6,7},{7,6},{8,9},{9,8},{10,11... | collective-permute-start | bytes 2359304 | tf_op jit(solution)/shard_map/ppermute | solution.py:137
  19.4 13.4 %collective-permute-start.2 = (bf16[8,12,16,128]{3,2,1,0:T(8,128)(2,1)S(1)}, bf16[8,12,16,128]{3,2,1,0:T(8,128)(2,1)S(1)}, u32[]{:S(2)}, u32[]{:S(2)}) collective-permute-start(bf16[8,12,16,128]{3,2,1,0:T(8,128)(2,1)S(1)} %pad_maximum_fusion.refs_1_.refs_3_.refs_0_), channel_id=1, source_target_pairs={{0,2},{1,3},{2,4},{3,5},{4,6},{5,7},{6,8},{7,9},{8,10},{9,11},{10,... | collective-permute-start | bytes 1179656 | tf_op jit(solution)/shard_map/ppermute | solution.py:109
  21.4 13.4 %collective-permute-start.5 = (bf16[8,12,16,128]{3,2,1,0:T(8,128)(2,1)S(1)}, bf16[8,12,16,128]{3,2,1,0:T(8,128)(2,1)S(1)}, u32[]{:S(2)}, u32[]{:S(2)}) collective-permute-start(bf16[8,12,16,128]{3,2,1,0:T(8,128)(2,1)S(1)} %pad_maximum_fusion.refs_1_.refs_3_.refs_0_), channel_id=1, source_target_pairs={{2,0},{3,1},{4,2},{5,3},{6,4},{7,5},{8,6},{9,7},{10,8},{11,9},{12,... | collective-permute-start | bytes 1179656 | tf_op jit(solution)/shard_map/ppermute | solution.py:110
  26.0 15.3 %collective-permute-start.11 = (bf16[8,12,16,128]{3,2,1,0:T(8,128)(2,1)S(1)}, bf16[8,12,16,128]{3,2,1,0:T(8,128)(2,1)S(1)}, u32[]{:S(2)}, u32[]{:S(2)}) collective-permute-start(bf16[8,12,16,128]{3,2,1,0:T(8,128)(2,1)S(1)} %pad_maximum_fusion.1.refs_2_.refs_1_.refs_3_), channel_id=1, source_target_pairs={{0,2},{1,3},{2,4},{3,5},{4,6},{5,7},{6,8},{7,9},{8,10},{9,11},{10,... | collective-permute-start | bytes 1179656 | tf_op jit(solution)/shard_map/ppermute | solution.py:109
  28.0 15.3 %collective-permute-start.14 = (bf16[8,12,16,128]{3,2,1,0:T(8,128)(2,1)S(1)}, bf16[8,12,16,128]{3,2,1,0:T(8,128)(2,1)S(1)}, u32[]{:S(2)}, u32[]{:S(2)}) collective-permute-start(bf16[8,12,16,128]{3,2,1,0:T(8,128)(2,1)S(1)} %pad_maximum_fusion.1.refs_2_.refs_1_.refs_3_), channel_id=1, source_target_pairs={{2,0},{3,1},{4,2},{5,3},{6,4},{7,5},{8,6},{9,7},{10,8},{11,9},{12,... | collective-permute-start | bytes 1179656 | tf_op jit(solution)/shard_map/ppermute | solution.py:110
  32.9 16.9 %collective-permute-start.3 = (bf16[8,12,16,128]{3,2,1,0:T(8,128)(2,1)S(1)}, bf16[8,12,16,128]{3,2,1,0:T(8,128)(2,1)S(1)}, u32[]{:S(2)}, u32[]{:S(2)}) collective-permute-start(bf16[8,12,16,128]{3,2,1,0:T(8,128)(2,1)S(1)} %collective-permute-done.2.refs_4_), channel_id=1, source_target_pairs={{0,2},{1,3},{2,4},{3,5},{4,6},{5,7},{6,8},{7,9},{8,10},{9,11},{10,... | collective-permute-start | bytes 1179656 | tf_op jit(solution)/shard_map/ppermute | solution.py:109
  34.8 16.8 %collective-permute-start.6 = (bf16[8,12,16,128]{3,2,1,0:T(8,128)(2,1)S(1)}, bf16[8,12,16,128]{3,2,1,0:T(8,128)(2,1)S(1)}, u32[]{:S(2)}, u32[]{:S(2)}) collective-permute-start(bf16[8,12,16,128]{3,2,1,0:T(8,128)(2,1)S(1)} %collective-permute-done.5.refs_7_), channel_id=1, source_target_pairs={{2,0},{3,1},{4,2},{5,3},{6,4},{7,5},{8,6},{9,7},{10,8},{11,9},{12,... | collective-permute-start | bytes 1179656 | tf_op jit(solution)/shard_map/ppermute | solution.py:110
  39.4 8.4 %copy-start = (s32[32,12]{0,1:T(8,128)S(1)}, s32[32,12]{0,1:T(8,128)}, u32[]{:S(2)}) copy-start(s32[32,12]{0,1:T(8,128)} %param.3) | copy-start | bytes 4612
  41.3 20.9 %collective-permute-start.12 = (bf16[8,12,16,128]{3,2,1,0:T(8,128)(2,1)S(1)}, bf16[8,12,16,128]{3,2,1,0:T(8,128)(2,1)S(1)}, u32[]{:S(2)}, u32[]{:S(2)}) collective-permute-start(bf16[8,12,16,128]{3,2,1,0:T(8,128)(2,1)S(1)} %collective-permute-done.11.refs_4_), channel_id=1, source_target_pairs={{0,2},{1,3},{2,4},{3,5},{4,6},{5,7},{6,8},{7,9},{8,10},{9,11},{10,... | collective-permute-start | bytes 1179656 | tf_op jit(solution)/shard_map/ppermute | solution.py:109
  43.2 21.0 %collective-permute-start.15 = (bf16[8,12,16,128]{3,2,1,0:T(8,128)(2,1)S(1)}, bf16[8,12,16,128]{3,2,1,0:T(8,128)(2,1)S(1)}, u32[]{:S(2)}, u32[]{:S(2)}) collective-permute-start(bf16[8,12,16,128]{3,2,1,0:T(8,128)(2,1)S(1)} %collective-permute-done.14.refs_7_), channel_id=1, source_target_pairs={{2,0},{3,1},{4,2},{5,3},{6,4},{7,5},{8,6},{9,7},{10,8},{11,9},{12,... | collective-permute-start | bytes 1179656 | tf_op jit(solution)/shard_map/ppermute | solution.py:110
  49.7 19.1 %collective-permute-start.4 = (bf16[8,12,16,128]{3,2,1,0:T(8,128)(2,1)S(1)}, bf16[8,12,16,128]{3,2,1,0:T(8,128)(2,1)S(1)}, u32[]{:S(2)}, u32[]{:S(2)}) collective-permute-start(bf16[8,12,16,128]{3,2,1,0:T(8,128)(2,1)S(1)} %collective-permute-done.3.refs_5_), channel_id=1, source_target_pairs={{0,2},{1,3},{2,4},{3,5},{4,6},{5,7},{6,8},{7,9},{8,10},{9,11},{10,... | collective-permute-start | bytes 1179656 | tf_op jit(solution)/shard_map/ppermute | solution.py:109
  51.7 19.1 %collective-permute-start.7 = (bf16[8,12,16,128]{3,2,1,0:T(8,128)(2,1)S(1)}, bf16[8,12,16,128]{3,2,1,0:T(8,128)(2,1)S(1)}, u32[]{:S(2)}, u32[]{:S(2)}) collective-permute-start(bf16[8,12,16,128]{3,2,1,0:T(8,128)(2,1)S(1)} %collective-permute-done.6.refs_8_), channel_id=1, source_target_pairs={{2,0},{3,1},{4,2},{5,3},{6,4},{7,5},{8,6},{9,7},{10,8},{11,9},{12,... | collective-permute-start | bytes 1179656 | tf_op jit(solution)/shard_map/ppermute | solution.py:110
  57.1 25.0 %collective-permute-start.1 = (bf16[8,12,16,128]{3,2,1,0:T(8,128)(2,1)S(1)}, bf16[8,12,16,128]{3,2,1,0:T(8,128)(2,1)S(1)}, u32[]{:S(2)}, u32[]{:S(2)}) collective-permute-start(bf16[8,12,16,128]{3,2,1,0:T(8,128)(2,1)S(1)} %pad_maximum_fusion.refs_1_.refs_3_.refs_0_), channel_id=1, source_target_pairs={{0,1009},{1,16},{2,1011},{3,18},{4,1013},{5,20},{6,1015},{7,22},{8... | collective-permute-start | bytes 1179656 | tf_op jit(solution)/shard_map/ppermute | solution.py:135
  62.3 13.3 %collective-permute-start.13 = (bf16[8,12,16,128]{3,2,1,0:T(8,128)(2,1)S(1)}, bf16[8,12,16,128]{3,2,1,0:T(8,128)(2,1)S(1)}, u32[]{:S(2)}, u32[]{:S(2)}) collective-permute-start(bf16[8,12,16,128]{3,2,1,0:T(8,128)(2,1)S(1)} %collective-permute-done.12.refs_5_), channel_id=1, source_target_pairs={{0,2},{1,3},{2,4},{3,5},{4,6},{5,7},{6,8},{7,9},{8,10},{9,11},{10,... | collective-permute-start | bytes 1179656 | tf_op jit(solution)/shard_map/ppermute | solution.py:109
  64.2 13.3 %collective-permute-start.16 = (bf16[8,12,16,128]{3,2,1,0:T(8,128)(2,1)S(1)}, bf16[8,12,16,128]{3,2,1,0:T(8,128)(2,1)S(1)}, u32[]{:S(2)}, u32[]{:S(2)}) collective-permute-start(bf16[8,12,16,128]{3,2,1,0:T(8,128)(2,1)S(1)} %collective-permute-done.15.refs_8_), channel_id=1, source_target_pairs={{2,0},{3,1},{4,2},{5,3},{6,4},{7,5},{8,6},{9,7},{10,8},{11,9},{12,... | collective-permute-start | bytes 1179656 | tf_op jit(solution)/shard_map/ppermute | solution.py:110
  68.8 13.3 %collective-permute-start.8 = (bf16[4,12,16,128]{3,2,1,0:T(8,128)(2,1)S(1)}, bf16[4,12,16,128]{3,2,1,0:T(8,128)(2,1)S(1)}, u32[]{:S(2)}, u32[]{:S(2)}) collective-permute-start(bf16[4,12,16,128]{3,2,1,0:T(8,128)(2,1)S(1)} %slice.31), channel_id=1, source_target_pairs={{0,2},{1,3},{2,4},{3,5},{4,6},{5,7},{6,8},{7,9},{8,10},{9,11},{10,... | collective-permute-start | bytes 589832 | tf_op jit(solution)/shard_map/ppermute | solution.py:114
  70.8 11.3 %collective-permute-start.9 = (bf16[4,12,16,128]{3,2,1,0:T(8,128)(2,1)S(1)}, bf16[4,12,16,128]{3,2,1,0:T(8,128)(2,1)S(1)}, u32[]{:S(2)}, u32[]{:S(2)}) collective-permute-start(bf16[4,12,16,128]{3,2,1,0:T(8,128)(2,1)S(1)} %slice.32), channel_id=1, source_target_pairs={{2,0},{3,1},{4,2},{5,3},{6,4},{7,5},{8,6},{9,7},{10,8},{11,9},{12,... | collective-permute-start | bytes 589832 | tf_op jit(solution)/shard_map/ppermute | solution.py:115
  75.6 14.4 %collective-permute-start.17 = (bf16[4,12,16,128]{3,2,1,0:T(8,128)(2,1)S(1)}, bf16[4,12,16,128]{3,2,1,0:T(8,128)(2,1)S(1)}, u32[]{:S(2)}, u32[]{:S(2)}) collective-permute-start(bf16[4,12,16,128]{3,2,1,0:T(8,128)(2,1)S(1)} %slice.33), channel_id=1, source_target_pairs={{0,2},{1,3},{2,4},{3,5},{4,6},{5,7},{6,8},{7,9},{8,10},{9,11},{10,... | collective-permute-start | bytes 589832 | tf_op jit(solution)/shard_map/ppermute | solution.py:114
  77.5 12.4 %collective-permute-start.18 = (bf16[4,12,16,128]{3,2,1,0:T(8,128)(2,1)S(1)}, bf16[4,12,16,128]{3,2,1,0:T(8,128)(2,1)S(1)}, u32[]{:S(2)}, u32[]{:S(2)}) collective-permute-start(bf16[4,12,16,128]{3,2,1,0:T(8,128)(2,1)S(1)} %slice.34), channel_id=1, source_target_pairs={{2,0},{3,1},{4,2},{5,3},{6,4},{7,5},{8,6},{9,7},{10,8},{11,9},{12,... | collective-permute-start | bytes 589832 | tf_op jit(solution)/shard_map/ppermute | solution.py:115
  86.0 14.0 %collective-permute-start.10 = (bf16[8,12,16,128]{3,2,1,0:T(8,128)(2,1)S(1)}, bf16[8,12,16,128]{3,2,1,0:T(8,128)(2,1)S(1)}, u32[]{:S(2)}, u32[]{:S(2)}) collective-permute-start(bf16[8,12,16,128]{3,2,1,0:T(8,128)(2,1)S(1)} %shard_map.37.refs_12_.refs_1_.refs_0_), channel_id=1, source_target_pairs={{0,1009},{1,16},{2,1011},{3,18},{4,1013},{5,20},{6,1015},{7,22},{8... | collective-permute-start | bytes 1179656 | tf_op jit(solution)/shard_map/ppermute | solution.py:135
  93.8 15.9 %collective-permute-start.19 = (bf16[8,12,16,128]{3,2,1,0:T(8,128)(2,1)S(1)}, bf16[8,12,16,128]{3,2,1,0:T(8,128)(2,1)S(1)}, u32[]{:S(2)}, u32[]{:S(2)}) collective-permute-start(bf16[8,12,16,128]{3,2,1,0:T(8,128)(2,1)S(1)} %shard_map.38.refs_2_.refs_1_), channel_id=1, source_target_pairs={{0,1},{1,0},{2,3},{3,2},{4,5},{5,4},{6,7},{7,6},{8,9},{9,8},{10,11... | collective-permute-start | bytes 1179656 | tf_op jit(solution)/shard_map/ppermute | solution.py:163
  103.8 11.6 %collective-permute-start.21 = (bf16[8,12,8,128]{3,2,1,0:T(8,128)(2,1)S(1)}, bf16[8,12,8,128]{3,2,1,0:T(8,128)(2,1)S(1)}, u32[]{:S(2)}, u32[]{:S(2)}) collective-permute-start(bf16[8,12,8,128]{3,2,1,0:T(8,128)(2,1)S(1)} %get-tuple-element.12), channel_id=1, source_target_pairs={{0,1},{1,0},{2,3},{3,2},{4,5},{5,4},{6,7},{7,6},{8,9},{9,8},{10,11... | collective-permute-start | bytes 589832 | tf_op jit(solution)/shard_map/ppermute | solution.py:167
  113.5 3.3 %collective-permute-start.20 = (bf16[8,12,8,128]{3,2,1,0:T(8,128)(2,1)S(1)}, bf16[8,12,8,128]{3,2,1,0:T(8,128)(2,1)S(1)}, u32[]{:S(2)}, u32[]{:S(2)}) collective-permute-start(bf16[8,12,8,128]{3,2,1,0:T(8,128)(2,1)S(1)} %get-tuple-element.11), channel_id=1, source_target_pairs={{0,1},{1,0},{2,3},{3,2},{4,5},{5,4},{6,7},{7,6},{8,9},{9,8},{10,11... | collective-permute-start | bytes 589832 | tf_op jit(solution)/shard_map/ppermute | solution.py:171

commit v3 on v2

v3 whole, which is shorter than its diff:
```python
import functools

import jax
import jax.numpy as jnp
from jax import lax
from jax.experimental import pallas as pl
from jax.experimental.pallas import tpu as pltpu
from jax.sharding import PartitionSpec as P

GROUP = 4
COST = 10


def product_kernel(first_block, is_first, scale, extra, index_from, *refs):
    parts, pieces = refs[:3], refs[3:12]
    outs, (window, index_ref, index_sem) = refs[12 + extra:-3], refs[-3:]
    rows, slots, width, size = parts[0].shape
    col = lax.axis_index("cols")
    z, core = col // 2, lax.rem(col, 2)
    first_row = rows * jnp.where(core == 0, first_block, 3 - first_block)

    index_copy = pltpu.make_async_copy(index_from, index_ref, index_sem)
    index_copy.start()
    turn = lax.rem(size - width * z, size)
    for k, part in enumerate(parts):
        for row in range(rows):
            window[rows * (first_block + k) + row, pl.ds(0, slots)] = pltpu.roll(part[row], turn, 2)
    window[4 * rows, 0] = jnp.zeros((width, size), window.dtype)
    index_copy.wait()
    tile_at = window.reshape(window.shape[0] * window.shape[1], width, size)

    offset = 0
    if extra == 2:
        offset = rows * (1 - core)
        for out, done in zip(outs, refs[12:14]):
            out[pl.ds(rows - offset, rows)] = done[...]

    def one_row(half, i, carry):
        total = jnp.zeros((slots * width, size), jnp.float32)
        for t in range(0, slots, 2):
            columns, blocks = [], []
            for u in (t, t + 1):
                tiles = []
                for s in range(slots):
                    word = index_ref[u % 4, s, first_row + i]
                    tiles.append(tile_at[lax.shift_right_logical(word, 10 * (u // 4)) & 1023])
                columns.append(jnp.concatenate(tiles, axis=0))
                blocks += [piece[i, u] for piece in pieces[:4]]
                blocks.append(pieces[4 + half][i - GROUP * half, u])
                blocks += [piece[i, u] for piece in pieces[6:]]
            picked = jnp.concatenate(columns, axis=1)
            total += jnp.dot(picked, jnp.concatenate(blocks, axis=0), preferred_element_type=jnp.float32)
        total = (total * scale).reshape(slots, width, size)
        if is_first:
            (out,) = outs
            out[i] = (-total).astype(out.dtype)
            line = lax.broadcasted_iota(jnp.int32, (width, size), 0)
            lane = lax.broadcasted_iota(jnp.int32, (width, size), 1)
            diagonal = jnp.where(lane == line + z * width, 3.0, 0.0)
            out[i, 0] = (diagonal - total[0]).astype(out.dtype)
        else:
            keep, send = outs
            to = i + offset
            low, high = total[:, :width // 2], total[:, width // 2:]
            keep[to] = jnp.where(core == 0, low, high).astype(keep.dtype)
            send[to] = jnp.where(core == 0, high, low).astype(send.dtype)
        return carry

    for half in range(2):
        lax.fori_loop(GROUP * half, GROUP * (half + 1), functools.partial(one_row, half), 0, unroll=GROUP)


def product(first_block, is_first, scale, index, parts, pieces, after=()):
    rows, slots, width, size = parts[0].shape
    dtype = parts[0].dtype
    if is_first:
        outs = jax.ShapeDtypeStruct((rows, slots, width, size), dtype)
        out_specs = pl.BlockSpec(memory_space=pltpu.VMEM)
    else:
        out_rows = 2 * rows if after else rows
        outs = [jax.ShapeDtypeStruct((out_rows, slots, width // 2, size), dtype)] * 2
        out_specs = [pl.BlockSpec(memory_space=pltpu.VMEM)] * 2
    flops = 2 * rows * slots * slots * width * size * size
    return pl.pallas_call(
        functools.partial(product_kernel, first_block, is_first, scale, len(after)),
        out_shape=outs,
        in_specs=[pl.BlockSpec(memory_space=pl.ANY)]
        + [pl.BlockSpec(memory_space=pltpu.VMEM)] * 12
        + [pl.BlockSpec(memory_space=pltpu.VMEM if len(after) == 2 else pl.ANY)] * len(after),
        out_specs=out_specs,
        scratch_shapes=[
            pltpu.VMEM((4 * rows + 1, 16, width, size), dtype),
            pltpu.SMEM(index.shape, index.dtype),
            pltpu.SemaphoreType.DMA,
        ],
        compiler_params=pltpu.CompilerParams(vmem_limit_bytes=8 * 2**20),
        cost_estimate=pl.CostEstimate(flops=COST * flops, bytes_accessed=rows * slots * size * size * 2, transcendentals=0),
    )(index, *parts, *pieces, *after)


def gather_ring(streams, ring):
    count = 2 * ring
    up = [(i, (i + 2) % count) for i in range(count)]
    down = [((i + 2) % count, i) for i in range(count)]
    risen = [[piece] for piece in streams]
    fallen = [[piece] for piece in streams]
    for step in range(ring // 2 - 1):
        for k in range(len(streams)):
            risen[k].append(lax.ppermute(risen[k][-1], "cols", up))
            fallen[k].append(lax.ppermute(fallen[k][-1], "cols", down))
    gathered = []
    for k in range(len(streams)):
        half = streams[k].shape[0] // 2
        last_up = lax.ppermute(risen[k][-1][:half], "cols", up)
        last_down = lax.ppermute(fallen[k][-1][half:], "cols", down)
        gathered.append(fallen[k] + [last_up, last_down] + risen[k][:0:-1])
    return gathered


def local(columns, fetch, values):
    rows_here, slots, half_width, size = values.shape
    cols = lax.axis_size("cols")
    count = lax.axis_size("rows")
    col = lax.axis_index("cols")
    core = col % 2
    first = core == 0
    swap = [(i, i ^ 1) for i in range(cols)]

    def outward(piece):
        pairs = []
        for r in range(count):
            for c in range(cols):
                to = ((r - 1) % count, c + 1) if c % 2 == 0 else ((r + 1) % count, c - 1)
                pairs.append((r * cols + c, to[0] * cols + to[1]))
        return lax.ppermute(piece, ("rows", "cols"), pairs)

    origin = lax.axis_index("rows") * rows_here + core * 16
    total = rows_here * count
    away = (columns - origin + total // 2) % total - total // 2 + 8
    part = jnp.where(first, away // 8, 3 - away // 8)
    place = (part * 8 + away % 8) * 16
    index = jnp.where(fetch >= 0, place[:, :, None] + fetch, 32 * 16).transpose(1, 2, 0)
    index = index[:4] + index[4:8] * 1024 + index[8:] * 1024**2

    other = lax.ppermute(values, "cols", swap)
    other, index = lax.optimization_barrier((other, index))

    def joined(number):
        start = jnp.where(first, 8 * number, 24 - 8 * number)
        mine = lax.dynamic_slice_in_dim(values, start, 8, 0)
        theirs = lax.dynamic_slice_in_dim(other, start, 8, 0)
        low = jnp.where(first, mine, theirs)
        high = jnp.where(first, theirs, mine)
        return jnp.concatenate([low, high], axis=2)

    outer_rows, inner_rows, beyond = joined(0), joined(1), joined(2)
    outer_halo = outward(outer_rows)
    outer_pieces, inner_pieces = gather_ring([outer_rows, inner_rows], cols // 2)

    scale = 1.0 / (slots * size)
    shifted_outer = product(0, True, scale, index, (outer_halo, outer_rows, inner_rows), outer_pieces)
    shifted_outward = outward(shifted_outer)
    shifted_inner = product(1, True, scale, index, (outer_rows, inner_rows, beyond), inner_pieces, [shifted_outer])
    shifted_beyond = lax.ppermute(shifted_inner, "cols", swap)
    parts = (shifted_outward, shifted_outer, shifted_inner)
    done_outer = product(0, False, 0.5, index, parts, outer_pieces)
    parts = (shifted_outer, shifted_inner, shifted_beyond)
    keep, send = product(1, False, 0.5, index, parts, inner_pieces, done_outer)
    got = lax.ppermute(send, "cols", swap)
    return jnp.where(first, jnp.concatenate([keep, got]), jnp.concatenate([got, keep]))


def solution(mesh):
    in_specs = (P("rows", None), P("rows", None, None), P("rows", None, "cols", None))
    out_specs = P("rows", None, "cols", None)
    return jax.shard_map(local, mesh=mesh, in_specs=in_specs, out_specs=out_specs, check_vma=False)
```

time: 119 us -> 115 us (0.966)
  Pallas kernels: 15.4 us -> 12.6 us
  starting transfers between devices: 90.9 us -> 88.9 us
    pallas_call x4, Pallas kernels: 15.4 us -> 12.6 us  [product(): pl.pallas_call(functools.partial(product_kernel, first_block, is_first, s...]
    ppermute x6, waiting for transfers between devices: 4.11 us -> 6.1 us  [gather_ring(): risen[k].append(lax.ppermute(risen[k][-1], 'cols', up))]
    ppermute x1, waiting for transfers between devices: 2.08 us -> 0.43 us  [local(): other = lax.ppermute(values, 'cols', swap)]
    ppermute x2 -> x1, starting transfers between devices: 7.73 us -> 6.67 us  [local(): got = lax.ppermute(send, 'cols', swap)]
  transfers between devices with their start and end apart: 22 -> 21, of which waited for: 5 -> 6; matrix products, arithmetic and copies ran while one was open for 1% -> 1% of each run, Pallas kernels for 13% -> 8%
where the time goes in v3:
time: 115 us; the launch traced here: 114 us
  starting transfers between devices  88.9 us (77%)
  Pallas kernels  12.6 us (11%)
  waiting for transfers between devices  7.89 us (7%)
  other arithmetic  3.35 us (3%)
    ppermute x6, starting transfers between devices, gather_ring(): fallen[k].append(lax.ppermute(fallen[k][-1], 'cols', down))  27.4 us
    ppermute x1, starting transfers between devices, local(): other = lax.ppermute(values, 'cols', swap)  16.1 us
    pallas_call x4, Pallas kernels, product(): pl.pallas_call(functools.partial(product_kernel, first_block, is_first, s...  12.6 us
    ppermute x6, starting transfers between devices, gather_ring(): risen[k].append(lax.ppermute(risen[k][-1], 'cols', up))  11.5 us
    ppermute x2, starting transfers between devices, gather_ring(): last_down = lax.ppermute(fallen[k][-1][half:], 'cols', down)  9.15 us
    ppermute x2, starting transfers between devices, outward(): return lax.ppermute(piece, ('rows', 'cols'), pairs)  8.24 us
    ppermute x1, starting transfers between devices, local(): got = lax.ppermute(send, 'cols', swap)  6.67 us
    ppermute x6, waiting for transfers between devices, gather_ring(): risen[k].append(lax.ppermute(risen[k][-1], 'cols', up))  6.1 us
  transfers between devices with their start and end apart: 21, of which 6 were waited for; matrix products, arithmetic and copies ran while one was open for 1% of the time, Pallas kernels for 8%

profile of v3, /device:TPU:1, one launch (start us, length us, event | category | flops | bytes accessed | tf_op | source)
XLA Modules:
  0.0 113.9 jit_solution(17160351294022752228)
XLA Ops:
  0.0 16.1 %collective-permute-start = (bf16[32,12,8,128]{3,2,1,0:T(8,128)(2,1)}, bf16[32,12,8,128]{3,2,1,0:T(8,128)(2,1)S(1)}, u32[]{:S(2)}, u32[]{:S(2)}) collective-permute-start(bf16[32,12,8,128]{3,2,1,0:T(8,128)(2,1)} %param.5), channel_id=1, source_target_pairs={{0,1},{1,0},{2,3},{3,2},{4,5},{5,4},{6,7},{7,6},{8,9},{9,8},{10,11... | collective-permute-start | bytes 2359304 | tf_op jit(solution)/shard_map/ppermute | solution.py:145
  19.4 1.9 %collective-permute-start.5 = (bf16[8,12,16,128]{3,2,1,0:T(8,128)(2,1)S(1)}, bf16[8,12,16,128]{3,2,1,0:T(8,128)(2,1)S(1)}, u32[]{:S(2)}, u32[]{:S(2)}) collective-permute-start(bf16[8,12,16,128]{3,2,1,0:T(8,128)(2,1)S(1)} %pad_maximum_fusion.refs_1_.refs_3_.refs_0_), channel_id=1, source_target_pairs={{0,2},{1,3},{2,4},{3,5},{4,6},{5,7},{6,8},{7,9},{8,10},{9,11},{10,... | collective-permute-start | bytes 1179656 | tf_op jit(solution)/shard_map/ppermute | solution.py:109
  21.4 4.6 %collective-permute-start.2 = (bf16[8,12,16,128]{3,2,1,0:T(8,128)(2,1)S(1)}, bf16[8,12,16,128]{3,2,1,0:T(8,128)(2,1)S(1)}, u32[]{:S(2)}, u32[]{:S(2)}) collective-permute-start(bf16[8,12,16,128]{3,2,1,0:T(8,128)(2,1)S(1)} %pad_maximum_fusion.refs_1_.refs_3_.refs_0_), channel_id=1, source_target_pairs={{2,0},{3,1},{4,2},{5,3},{6,4},{7,5},{8,6},{9,7},{10,8},{11,9},{12,... | collective-permute-start | bytes 1179656 | tf_op jit(solution)/shard_map/ppermute | solution.py:110
  26.0 1.9 %collective-permute-start.13 = (bf16[8,12,16,128]{3,2,1,0:T(8,128)(2,1)S(1)}, bf16[8,12,16,128]{3,2,1,0:T(8,128)(2,1)S(1)}, u32[]{:S(2)}, u32[]{:S(2)}) collective-permute-start(bf16[8,12,16,128]{3,2,1,0:T(8,128)(2,1)S(1)} %pad_maximum_fusion.1.refs_2_.refs_1_.refs_3_), channel_id=1, source_target_pairs={{0,2},{1,3},{2,4},{3,5},{4,6},{5,7},{6,8},{7,9},{8,10},{9,11},{10,... | collective-permute-start | bytes 1179656 | tf_op jit(solution)/shard_map/ppermute | solution.py:109
  28.0 4.6 %collective-permute-start.10 = (bf16[8,12,16,128]{3,2,1,0:T(8,128)(2,1)S(1)}, bf16[8,12,16,128]{3,2,1,0:T(8,128)(2,1)S(1)}, u32[]{:S(2)}, u32[]{:S(2)}) collective-permute-start(bf16[8,12,16,128]{3,2,1,0:T(8,128)(2,1)S(1)} %pad_maximum_fusion.1.refs_2_.refs_1_.refs_3_), channel_id=1, source_target_pairs={{2,0},{3,1},{4,2},{5,3},{6,4},{7,5},{8,6},{9,7},{10,8},{11,9},{12,... | collective-permute-start | bytes 1179656 | tf_op jit(solution)/shard_map/ppermute | solution.py:110
  34.8 4.6 %collective-permute-start.3 = (bf16[8,12,16,128]{3,2,1,0:T(8,128)(2,1)S(1)}, bf16[8,12,16,128]{3,2,1,0:T(8,128)(2,1)S(1)}, u32[]{:S(2)}, u32[]{:S(2)}) collective-permute-start(bf16[8,12,16,128]{3,2,1,0:T(8,128)(2,1)S(1)} %collective-permute-done.2.refs_4_), channel_id=1, source_target_pairs={{2,0},{3,1},{4,2},{5,3},{6,4},{7,5},{8,6},{9,7},{10,8},{11,9},{12,... | collective-permute-start | bytes 1179656 | tf_op jit(solution)/shard_map/ppermute | solution.py:110
  39.4 1.9 %collective-permute-done.13.refs_11_ = bf16[8,12,16,128]{3,2,1,0:T(8,128)(2,1)S(1)} collective-permute-done((bf16[8,12,16,128]{3,2,1,0:T(8,128)(2,1)S(1)}, bf16[8,12,16,128]{3,2,1,0:T(8,128)(2,1)S(1)}, u32[]{:S(2)}, u32[]{:S(2)}) %collective-permute-start.13) | collective-permute-done | bytes 393248 | tf_op jit(solution)/shard_map/ppermute | solution.py:109
  43.2 4.6 %collective-permute-start.11 = (bf16[8,12,16,128]{3,2,1,0:T(8,128)(2,1)S(1)}, bf16[8,12,16,128]{3,2,1,0:T(8,128)(2,1)S(1)}, u32[]{:S(2)}, u32[]{:S(2)}) collective-permute-start(bf16[8,12,16,128]{3,2,1,0:T(8,128)(2,1)S(1)} %collective-permute-done.10.refs_4_), channel_id=1, source_target_pairs={{2,0},{3,1},{4,2},{5,3},{6,4},{7,5},{8,6},{9,7},{10,8},{11,9},{12,... | collective-permute-start | bytes 1179656 | tf_op jit(solution)/shard_map/ppermute | solution.py:110
  47.8 1.9 %collective-permute-done.6.refs_10_ = bf16[8,12,16,128]{3,2,1,0:T(8,128)(2,1)S(1)} collective-permute-done((bf16[8,12,16,128]{3,2,1,0:T(8,128)(2,1)S(1)}, bf16[8,12,16,128]{3,2,1,0:T(8,128)(2,1)S(1)}, u32[]{:S(2)}, u32[]{:S(2)}) %collective-permute-start.6) | collective-permute-done | bytes 393248 | tf_op jit(solution)/shard_map/ppermute | solution.py:109
  51.7 4.6 %collective-permute-start.4 = (bf16[8,12,16,128]{3,2,1,0:T(8,128)(2,1)S(1)}, bf16[8,12,16,128]{3,2,1,0:T(8,128)(2,1)S(1)}, u32[]{:S(2)}, u32[]{:S(2)}) collective-permute-start(bf16[8,12,16,128]{3,2,1,0:T(8,128)(2,1)S(1)} %collective-permute-done.3.refs_5_), channel_id=1, source_target_pairs={{2,0},{3,1},{4,2},{5,3},{6,4},{7,5},{8,6},{9,7},{10,8},{11,9},{12,... | collective-permute-start | bytes 1179656 | tf_op jit(solution)/shard_map/ppermute | solution.py:110
  56.2 1.9 %collective-permute-done.14.refs_10_ = bf16[8,12,16,128]{3,2,1,0:T(8,128)(2,1)S(1)} collective-permute-done((bf16[8,12,16,128]{3,2,1,0:T(8,128)(2,1)S(1)}, bf16[8,12,16,128]{3,2,1,0:T(8,128)(2,1)S(1)}, u32[]{:S(2)}, u32[]{:S(2)}) %collective-permute-start.14) | collective-permute-done | bytes 393248 | tf_op jit(solution)/shard_map/ppermute | solution.py:109
  60.1 4.6 %collective-permute-start.12 = (bf16[8,12,16,128]{3,2,1,0:T(8,128)(2,1)S(1)}, bf16[8,12,16,128]{3,2,1,0:T(8,128)(2,1)S(1)}, u32[]{:S(2)}, u32[]{:S(2)}) collective-permute-start(bf16[8,12,16,128]{3,2,1,0:T(8,128)(2,1)S(1)} %collective-permute-done.11.refs_5_), channel_id=1, source_target_pairs={{2,0},{3,1},{4,2},{5,3},{6,4},{7,5},{8,6},{9,7},{10,8},{11,9},{12,... | collective-permute-start | bytes 1179656 | tf_op jit(solution)/shard_map/ppermute | solution.py:110
  64.7 5.1 %collective-permute-start.1 = (bf16[8,12,16,128]{3,2,1,0:T(8,128)(2,1)S(1)}, bf16[8,12,16,128]{3,2,1,0:T(8,128)(2,1)S(1)}, u32[]{:S(2)}, u32[]{:S(2)}) collective-permute-start(bf16[8,12,16,128]{3,2,1,0:T(8,128)(2,1)S(1)} %pad_maximum_fusion.refs_1_.refs_3_.refs_0_), channel_id=1, source_target_pairs={{0,1009},{1,16},{2,1011},{3,18},{4,1013},{5,20},{6,1015},{7,22},{8... | collective-permute-start | bytes 1179656 | tf_op jit(solution)/shard_map/ppermute | solution.py:135
  69.8 1.9 %collective-permute-start.8 = (bf16[4,12,16,128]{3,2,1,0:T(8,128)(2,1)S(1)}, bf16[4,12,16,128]{3,2,1,0:T(8,128)(2,1)S(1)}, u32[]{:S(2)}, u32[]{:S(2)}) collective-permute-start(bf16[4,12,16,128]{3,2,1,0:T(8,128)(2,1)S(1)} %slice.31), channel_id=1, source_target_pairs={{0,2},{1,3},{2,4},{3,5},{4,6},{5,7},{6,8},{7,9},{8,10},{9,11},{10,... | collective-permute-start | bytes 589832 | tf_op jit(solution)/shard_map/ppermute | solution.py:114
  71.8 4.6 %collective-permute-start.9 = (bf16[4,12,16,128]{3,2,1,0:T(8,128)(2,1)S(1)}, bf16[4,12,16,128]{3,2,1,0:T(8,128)(2,1)S(1)}, u32[]{:S(2)}, u32[]{:S(2)}) collective-permute-start(bf16[4,12,16,128]{3,2,1,0:T(8,128)(2,1)S(1)} %slice.32), channel_id=1, source_target_pairs={{2,0},{3,1},{4,2},{5,3},{6,4},{7,5},{8,6},{9,7},{10,8},{11,9},{12,... | collective-permute-start | bytes 589832 | tf_op jit(solution)/shard_map/ppermute | solution.py:115
  76.4 1.9 %collective-permute-start.16 = (bf16[4,12,16,128]{3,2,1,0:T(8,128)(2,1)S(1)}, bf16[4,12,16,128]{3,2,1,0:T(8,128)(2,1)S(1)}, u32[]{:S(2)}, u32[]{:S(2)}) collective-permute-start(bf16[4,12,16,128]{3,2,1,0:T(8,128)(2,1)S(1)} %slice.33), channel_id=1, source_target_pairs={{0,2},{1,3},{2,4},{3,5},{4,6},{5,7},{6,8},{7,9},{8,10},{9,11},{10,... | collective-permute-start | bytes 589832 | tf_op jit(solution)/shard_map/ppermute | solution.py:114
  78.4 4.6 %collective-permute-start.17 = (bf16[4,12,16,128]{3,2,1,0:T(8,128)(2,1)S(1)}, bf16[4,12,16,128]{3,2,1,0:T(8,128)(2,1)S(1)}, u32[]{:S(2)}, u32[]{:S(2)}) collective-permute-start(bf16[4,12,16,128]{3,2,1,0:T(8,128)(2,1)S(1)} %slice.34), channel_id=1, source_target_pairs={{2,0},{3,1},{4,2},{5,3},{6,4},{7,5},{8,6},{9,7},{10,8},{11,9},{12,... | collective-permute-start | bytes 589832 | tf_op jit(solution)/shard_map/ppermute | solution.py:115
  83.0 3.1 %shard_map.37.refs_12_.refs_1_.refs_0_ = bf16[8,12,16,128]{3,2,1,0:T(8,128)(2,1)S(1)} custom-call(s32[4,12,32]{2,1,0:T(8,128)S(1)} %fusion.index_from, bf16[8,12,16,128]{3,2,1,0:T(8,128)(2,1)S(1)} %collective-permute-done.1.refs_0_, bf16[8,12,16,128]{3,2,1,0:T(8,128)(2,1)S(1)} %pad_maximum_fusion.refs_1_.refs_3_.refs_0_, ...), custom_call_target="tpu_custom_call" | custom-call | flops 6039797760 | bytes 3145728 | tf_op jit(solution)/shard_map/pallas_call | solution.py:84
  86.2 3.2 %collective-permute-start.19 = (bf16[8,12,16,128]{3,2,1,0:T(8,128)(2,1)S(1)}, bf16[8,12,16,128]{3,2,1,0:T(8,128)(2,1)S(1)}, u32[]{:S(2)}, u32[]{:S(2)}) collective-permute-start(bf16[8,12,16,128]{3,2,1,0:T(8,128)(2,1)S(1)} %shard_map.37.refs_12_.refs_1_.refs_0_), channel_id=1, source_target_pairs={{0,1009},{1,16},{2,1011},{3,18},{4,1013},{5,20},{6,1015},{7,22},{8... | collective-permute-start | bytes 1179656 | tf_op jit(solution)/shard_map/ppermute | solution.py:135
  89.3 3.1 %shard_map.38.refs_2_.refs_1_ = bf16[8,12,16,128]{3,2,1,0:T(8,128)(2,1)S(1)} custom-call(s32[4,12,32]{2,1,0:T(8,128)S(1)} %fusion.index_from, bf16[8,12,16,128]{3,2,1,0:T(8,128)(2,1)S(1)} %pad_maximum_fusion.refs_1_.refs_3_.refs_0_, bf16[8,12,16,128]{3,2,1,0:T(8,128)(2,1)S(1)} %pad_maximum_fusion.1.refs_2_.refs_1_.refs_3_, ...), custom_call_target="tpu_custom_call" | custom-call | flops 6039797760 | bytes 3145728 | tf_op jit(solution)/shard_map/pallas_call | solution.py:84
  92.5 6.1 %collective-permute-start.18 = (bf16[8,12,16,128]{3,2,1,0:T(8,128)(2,1)S(1)}, bf16[8,12,16,128]{3,2,1,0:T(8,128)(2,1)S(1)}, u32[]{:S(2)}, u32[]{:S(2)}) collective-permute-start(bf16[8,12,16,128]{3,2,1,0:T(8,128)(2,1)S(1)} %shard_map.38.refs_2_.refs_1_), channel_id=1, source_target_pairs={{0,1},{1,0},{2,3},{3,2},{4,5},{5,4},{6,7},{7,6},{8,9},{9,8},{10,11... | collective-permute-start | bytes 1179656 | tf_op jit(solution)/shard_map/ppermute | solution.py:164
  98.6 3.1 %shard_map.39 = (bf16[8,12,8,128]{3,2,1,0:T(8,128)(2,1)S(1)}, bf16[8,12,8,128]{3,2,1,0:T(8,128)(2,1)S(1)}) custom-call(s32[4,12,32]{2,1,0:T(8,128)S(1)} %fusion.index_from, bf16[8,12,16,128]{3,2,1,0:T(8,128)(2,1)S(1)} %collective-permute-done.19.refs_0_, bf16[8,12,16,128]{3,2,1,0:T(8,128)(2,1)S(1)} %shard_map.37.refs_12_.refs_1_.refs_0_, ...), custom_call_target="tpu_custom_call" | custom-call | flops 6039797760 | bytes 3145728 | tf_op jit(solution)/shard_map/pallas_call | solution.py:84
  101.7 3.2 %shard_map.40 = (bf16[16,12,8,128]{3,2,1,0:T(8,128)(2,1)S(1)}, bf16[16,12,8,128]{3,2,1,0:T(8,128)(2,1)S(1)}) custom-call(s32[4,12,32]{2,1,0:T(8,128)S(1)} %fusion.index_from, bf16[8,12,16,128]{3,2,1,0:T(8,128)(2,1)S(1)} %shard_map.37.refs_12_.refs_1_.refs_0_, bf16[8,12,16,128]{3,2,1,0:T(8,128)(2,1)S(1)} %shard_map.38.refs_2_.refs_1_, ...), custom_call_target="tpu_custom_call" | custom-call | flops 6039797760 | bytes 3145728 | tf_op jit(solution)/shard_map/pallas_call | solution.py:84
  104.9 6.7 %collective-permute-start.20 = (bf16[16,12,8,128]{3,2,1,0:T(8,128)(2,1)S(1)}, bf16[16,12,8,128]{3,2,1,0:T(8,128)(2,1)S(1)}, u32[]{:S(2)}, u32[]{:S(2)}) collective-permute-start(bf16[16,12,8,128]{3,2,1,0:T(8,128)(2,1)S(1)} %get-tuple-element.16), channel_id=1, source_target_pairs={{0,1},{1,0},{2,3},{3,2},{4,5},{5,4},{6,7},{7,6},{8,9},{9,8},{10,11... | collective-permute-start | bytes 1179656 | tf_op jit(solution)/shard_map/ppermute | solution.py:169
  (36 shorter events, 13.9 us)
Async XLA Ops:
  0.0 18.2 %collective-permute-start = (bf16[32,12,8,128]{3,2,1,0:T(8,128)(2,1)}, bf16[32,12,8,128]{3,2,1,0:T(8,128)(2,1)S(1)}, u32[]{:S(2)}, u32[]{:S(2)}) collective-permute-start(bf16[32,12,8,128]{3,2,1,0:T(8,128)(2,1)} %param.5), channel_id=1, source_target_pairs={{0,1},{1,0},{2,3},{3,2},{4,5},{5,4},{6,7},{7,6},{8,9},{9,8},{10,11... | collective-permute-start | bytes 2359304 | tf_op jit(solution)/shard_map/ppermute | solution.py:145
  16.1 0.7 copy-start
  19.4 13.4 %collective-permute-start.5 = (bf16[8,12,16,128]{3,2,1,0:T(8,128)(2,1)S(1)}, bf16[8,12,16,128]{3,2,1,0:T(8,128)(2,1)S(1)}, u32[]{:S(2)}, u32[]{:S(2)}) collective-permute-start(bf16[8,12,16,128]{3,2,1,0:T(8,128)(2,1)S(1)} %pad_maximum_fusion.refs_1_.refs_3_.refs_0_), channel_id=1, source_target_pairs={{0,2},{1,3},{2,4},{3,5},{4,6},{5,7},{6,8},{7,9},{8,10},{9,11},{10,... | collective-permute-start | bytes 1179656 | tf_op jit(solution)/shard_map/ppermute | solution.py:109
  21.4 13.4 %collective-permute-start.2 = (bf16[8,12,16,128]{3,2,1,0:T(8,128)(2,1)S(1)}, bf16[8,12,16,128]{3,2,1,0:T(8,128)(2,1)S(1)}, u32[]{:S(2)}, u32[]{:S(2)}) collective-permute-start(bf16[8,12,16,128]{3,2,1,0:T(8,128)(2,1)S(1)} %pad_maximum_fusion.refs_1_.refs_3_.refs_0_), channel_id=1, source_target_pairs={{2,0},{3,1},{4,2},{5,3},{6,4},{7,5},{8,6},{9,7},{10,8},{11,9},{12,... | collective-permute-start | bytes 1179656 | tf_op jit(solution)/shard_map/ppermute | solution.py:110
  26.0 15.3 %collective-permute-start.13 = (bf16[8,12,16,128]{3,2,1,0:T(8,128)(2,1)S(1)}, bf16[8,12,16,128]{3,2,1,0:T(8,128)(2,1)S(1)}, u32[]{:S(2)}, u32[]{:S(2)}) collective-permute-start(bf16[8,12,16,128]{3,2,1,0:T(8,128)(2,1)S(1)} %pad_maximum_fusion.1.refs_2_.refs_1_.refs_3_), channel_id=1, source_target_pairs={{0,2},{1,3},{2,4},{3,5},{4,6},{5,7},{6,8},{7,9},{8,10},{9,11},{10,... | collective-permute-start | bytes 1179656 | tf_op jit(solution)/shard_map/ppermute | solution.py:109
  28.0 15.3 %collective-permute-start.10 = (bf16[8,12,16,128]{3,2,1,0:T(8,128)(2,1)S(1)}, bf16[8,12,16,128]{3,2,1,0:T(8,128)(2,1)S(1)}, u32[]{:S(2)}, u32[]{:S(2)}) collective-permute-start(bf16[8,12,16,128]{3,2,1,0:T(8,128)(2,1)S(1)} %pad_maximum_fusion.1.refs_2_.refs_1_.refs_3_), channel_id=1, source_target_pairs={{2,0},{3,1},{4,2},{5,3},{6,4},{7,5},{8,6},{9,7},{10,8},{11,9},{12,... | collective-permute-start | bytes 1179656 | tf_op jit(solution)/shard_map/ppermute | solution.py:110
  32.9 16.9 %collective-permute-start.6 = (bf16[8,12,16,128]{3,2,1,0:T(8,128)(2,1)S(1)}, bf16[8,12,16,128]{3,2,1,0:T(8,128)(2,1)S(1)}, u32[]{:S(2)}, u32[]{:S(2)}) collective-permute-start(bf16[8,12,16,128]{3,2,1,0:T(8,128)(2,1)S(1)} %collective-permute-done.5.refs_11_), channel_id=1, source_target_pairs={{0,2},{1,3},{2,4},{3,5},{4,6},{5,7},{6,8},{7,9},{8,10},{9,11},{10,... | collective-permute-start | bytes 1179656 | tf_op jit(solution)/shard_map/ppermute | solution.py:109
  34.8 16.8 %collective-permute-start.3 = (bf16[8,12,16,128]{3,2,1,0:T(8,128)(2,1)S(1)}, bf16[8,12,16,128]{3,2,1,0:T(8,128)(2,1)S(1)}, u32[]{:S(2)}, u32[]{:S(2)}) collective-permute-start(bf16[8,12,16,128]{3,2,1,0:T(8,128)(2,1)S(1)} %collective-permute-done.2.refs_4_), channel_id=1, source_target_pairs={{2,0},{3,1},{4,2},{5,3},{6,4},{7,5},{8,6},{9,7},{10,8},{11,9},{12,... | collective-permute-start | bytes 1179656 | tf_op jit(solution)/shard_map/ppermute | solution.py:110
  41.3 16.9 %collective-permute-start.14 = (bf16[8,12,16,128]{3,2,1,0:T(8,128)(2,1)S(1)}, bf16[8,12,16,128]{3,2,1,0:T(8,128)(2,1)S(1)}, u32[]{:S(2)}, u32[]{:S(2)}) collective-permute-start(bf16[8,12,16,128]{3,2,1,0:T(8,128)(2,1)S(1)} %collective-permute-done.13.refs_11_), channel_id=1, source_target_pairs={{0,2},{1,3},{2,4},{3,5},{4,6},{5,7},{6,8},{7,9},{8,10},{9,11},{10,... | collective-permute-start | bytes 1179656 | tf_op jit(solution)/shard_map/ppermute | solution.py:109
  43.2 16.8 %collective-permute-start.11 = (bf16[8,12,16,128]{3,2,1,0:T(8,128)(2,1)S(1)}, bf16[8,12,16,128]{3,2,1,0:T(8,128)(2,1)S(1)}, u32[]{:S(2)}, u32[]{:S(2)}) collective-permute-start(bf16[8,12,16,128]{3,2,1,0:T(8,128)(2,1)S(1)} %collective-permute-done.10.refs_4_), channel_id=1, source_target_pairs={{2,0},{3,1},{4,2},{5,3},{6,4},{7,5},{8,6},{9,7},{10,8},{11,9},{12,... | collective-permute-start | bytes 1179656 | tf_op jit(solution)/shard_map/ppermute | solution.py:110
  49.7 20.0 %collective-permute-start.7 = (bf16[8,12,16,128]{3,2,1,0:T(8,128)(2,1)S(1)}, bf16[8,12,16,128]{3,2,1,0:T(8,128)(2,1)S(1)}, u32[]{:S(2)}, u32[]{:S(2)}) collective-permute-start(bf16[8,12,16,128]{3,2,1,0:T(8,128)(2,1)S(1)} %collective-permute-done.6.refs_10_), channel_id=1, source_target_pairs={{0,2},{1,3},{2,4},{3,5},{4,6},{5,7},{6,8},{7,9},{8,10},{9,11},{10,... | collective-permute-start | bytes 1179656 | tf_op jit(solution)/shard_map/ppermute | solution.py:109
  51.7 20.1 %collective-permute-start.4 = (bf16[8,12,16,128]{3,2,1,0:T(8,128)(2,1)S(1)}, bf16[8,12,16,128]{3,2,1,0:T(8,128)(2,1)S(1)}, u32[]{:S(2)}, u32[]{:S(2)}) collective-permute-start(bf16[8,12,16,128]{3,2,1,0:T(8,128)(2,1)S(1)} %collective-permute-done.3.refs_5_), channel_id=1, source_target_pairs={{2,0},{3,1},{4,2},{5,3},{6,4},{7,5},{8,6},{9,7},{10,8},{11,9},{12,... | collective-permute-start | bytes 1179656 | tf_op jit(solution)/shard_map/ppermute | solution.py:110
  58.2 18.3 %collective-permute-start.15 = (bf16[8,12,16,128]{3,2,1,0:T(8,128)(2,1)S(1)}, bf16[8,12,16,128]{3,2,1,0:T(8,128)(2,1)S(1)}, u32[]{:S(2)}, u32[]{:S(2)}) collective-permute-start(bf16[8,12,16,128]{3,2,1,0:T(8,128)(2,1)S(1)} %collective-permute-done.14.refs_10_), channel_id=1, source_target_pairs={{0,2},{1,3},{2,4},{3,5},{4,6},{5,7},{6,8},{7,9},{8,10},{9,11},{10,... | collective-permute-start | bytes 1179656 | tf_op jit(solution)/shard_map/ppermute | solution.py:109
  60.1 18.3 %collective-permute-start.12 = (bf16[8,12,16,128]{3,2,1,0:T(8,128)(2,1)S(1)}, bf16[8,12,16,128]{3,2,1,0:T(8,128)(2,1)S(1)}, u32[]{:S(2)}, u32[]{:S(2)}) collective-permute-start(bf16[8,12,16,128]{3,2,1,0:T(8,128)(2,1)S(1)} %collective-permute-done.11.refs_5_), channel_id=1, source_target_pairs={{2,0},{3,1},{4,2},{5,3},{6,4},{7,5},{8,6},{9,7},{10,8},{11,9},{12,... | collective-permute-start | bytes 1179656 | tf_op jit(solution)/shard_map/ppermute | solution.py:110
  64.7 18.3 %collective-permute-start.1 = (bf16[8,12,16,128]{3,2,1,0:T(8,128)(2,1)S(1)}, bf16[8,12,16,128]{3,2,1,0:T(8,128)(2,1)S(1)}, u32[]{:S(2)}, u32[]{:S(2)}) collective-permute-start(bf16[8,12,16,128]{3,2,1,0:T(8,128)(2,1)S(1)} %pad_maximum_fusion.refs_1_.refs_3_.refs_0_), channel_id=1, source_target_pairs={{0,1009},{1,16},{2,1011},{3,18},{4,1013},{5,20},{6,1015},{7,22},{8... | collective-permute-start | bytes 1179656 | tf_op jit(solution)/shard_map/ppermute | solution.py:135
  69.8 13.2 %collective-permute-start.8 = (bf16[4,12,16,128]{3,2,1,0:T(8,128)(2,1)S(1)}, bf16[4,12,16,128]{3,2,1,0:T(8,128)(2,1)S(1)}, u32[]{:S(2)}, u32[]{:S(2)}) collective-permute-start(bf16[4,12,16,128]{3,2,1,0:T(8,128)(2,1)S(1)} %slice.31), channel_id=1, source_target_pairs={{0,2},{1,3},{2,4},{3,5},{4,6},{5,7},{6,8},{7,9},{8,10},{9,11},{10,... | collective-permute-start | bytes 589832 | tf_op jit(solution)/shard_map/ppermute | solution.py:114
  71.8 11.3 %collective-permute-start.9 = (bf16[4,12,16,128]{3,2,1,0:T(8,128)(2,1)S(1)}, bf16[4,12,16,128]{3,2,1,0:T(8,128)(2,1)S(1)}, u32[]{:S(2)}, u32[]{:S(2)}) collective-permute-start(bf16[4,12,16,128]{3,2,1,0:T(8,128)(2,1)S(1)} %slice.32), channel_id=1, source_target_pairs={{2,0},{3,1},{4,2},{5,3},{6,4},{7,5},{8,6},{9,7},{10,8},{11,9},{12,... | collective-permute-start | bytes 589832 | tf_op jit(solution)/shard_map/ppermute | solution.py:115
  76.4 12.9 %collective-permute-start.16 = (bf16[4,12,16,128]{3,2,1,0:T(8,128)(2,1)S(1)}, bf16[4,12,16,128]{3,2,1,0:T(8,128)(2,1)S(1)}, u32[]{:S(2)}, u32[]{:S(2)}) collective-permute-start(bf16[4,12,16,128]{3,2,1,0:T(8,128)(2,1)S(1)} %slice.33), channel_id=1, source_target_pairs={{0,2},{1,3},{2,4},{3,5},{4,6},{5,7},{6,8},{7,9},{8,10},{9,11},{10,... | collective-permute-start | bytes 589832 | tf_op jit(solution)/shard_map/ppermute | solution.py:114
  78.4 10.9 %collective-permute-start.17 = (bf16[4,12,16,128]{3,2,1,0:T(8,128)(2,1)S(1)}, bf16[4,12,16,128]{3,2,1,0:T(8,128)(2,1)S(1)}, u32[]{:S(2)}, u32[]{:S(2)}) collective-permute-start(bf16[4,12,16,128]{3,2,1,0:T(8,128)(2,1)S(1)} %slice.34), channel_id=1, source_target_pairs={{2,0},{3,1},{4,2},{5,3},{6,4},{7,5},{8,6},{9,7},{10,8},{11,9},{12,... | collective-permute-start | bytes 589832 | tf_op jit(solution)/shard_map/ppermute | solution.py:115
  86.2 12.4 %collective-permute-start.19 = (bf16[8,12,16,128]{3,2,1,0:T(8,128)(2,1)S(1)}, bf16[8,12,16,128]{3,2,1,0:T(8,128)(2,1)S(1)}, u32[]{:S(2)}, u32[]{:S(2)}) collective-permute-start(bf16[8,12,16,128]{3,2,1,0:T(8,128)(2,1)S(1)} %shard_map.37.refs_12_.refs_1_.refs_0_), channel_id=1, source_target_pairs={{0,1009},{1,16},{2,1011},{3,18},{4,1013},{5,20},{6,1015},{7,22},{8... | collective-permute-start | bytes 1179656 | tf_op jit(solution)/shard_map/ppermute | solution.py:135
  92.5 9.2 %collective-permute-start.18 = (bf16[8,12,16,128]{3,2,1,0:T(8,128)(2,1)S(1)}, bf16[8,12,16,128]{3,2,1,0:T(8,128)(2,1)S(1)}, u32[]{:S(2)}, u32[]{:S(2)}) collective-permute-start(bf16[8,12,16,128]{3,2,1,0:T(8,128)(2,1)S(1)} %shard_map.38.refs_2_.refs_1_), channel_id=1, source_target_pairs={{0,1},{1,0},{2,3},{3,2},{4,5},{5,4},{6,7},{7,6},{8,9},{9,8},{10,11... | collective-permute-start | bytes 1179656 | tf_op jit(solution)/shard_map/ppermute | solution.py:164
  104.9 8.0 %collective-permute-start.20 = (bf16[16,12,8,128]{3,2,1,0:T(8,128)(2,1)S(1)}, bf16[16,12,8,128]{3,2,1,0:T(8,128)(2,1)S(1)}, u32[]{:S(2)}, u32[]{:S(2)}) collective-permute-start(bf16[16,12,8,128]{3,2,1,0:T(8,128)(2,1)S(1)} %get-tuple-element.16), channel_id=1, source_target_pairs={{0,1},{1,0},{2,3},{3,2},{4,5},{5,4},{6,7},{7,6},{8,9},{9,8},{10,11... | collective-permute-start | bytes 1179656 | tf_op jit(solution)/shard_map/ppermute | solution.py:169

commit v4 on v3

--- a/solution.py
+++ b/solution.py
@@ -7,13 +7,12 @@
 from jax.experimental.pallas import tpu as pltpu
 from jax.sharding import PartitionSpec as P
 
-GROUP = 4
-COST = 10
+UNROLL = 8
 
 
 def product_kernel(first_block, is_first, scale, extra, index_from, *refs):
-    parts, pieces = refs[:3], refs[3:12]
-    outs, (window, index_ref, index_sem) = refs[12 + extra:-3], refs[-3:]
+    parts, pieces = refs[:3], refs[3:11]
+    outs, (window, index_ref, index_sem) = refs[11 + extra:-3], refs[-3:]
     rows, slots, width, size = parts[0].shape
     col = lax.axis_index("cols")
     z, core = col // 2, lax.rem(col, 2)
@@ -23,36 +22,35 @@
     index_copy.start()
     turn = lax.rem(size - width * z, size)
     for k, part in enumerate(parts):
-        for row in range(rows):
-            window[rows * (first_block + k) + row, pl.ds(0, slots)] = pltpu.roll(part[row], turn, 2)
+        to = rows * (first_block + k) + (core if part.shape[0] < rows else 0)
+        for row in range(part.shape[0]):
+            window[to + row, pl.ds(0, slots)] = pltpu.roll(part[row], turn, 2)
     window[4 * rows, 0] = jnp.zeros((width, size), window.dtype)
     index_copy.wait()
     tile_at = window.reshape(window.shape[0] * window.shape[1], width, size)
 
     offset = 0
     if extra == 2:
-        offset = rows * (1 - core)
-        for out, done in zip(outs, refs[12:14]):
+        offset = rows * core
+        for out, done in zip(outs, refs[11:13]):
             out[pl.ds(rows - offset, rows)] = done[...]
 
-    def one_row(half, i, carry):
+    def one_row(i, carry):
         total = jnp.zeros((slots * width, size), jnp.float32)
-        for t in range(0, slots, 2):
+        for t in range(0, slots, 6):
             columns, blocks = [], []
-            for u in (t, t + 1):
+            for u in range(t, t + 6):
                 tiles = []
                 for s in range(slots):
                     word = index_ref[u % 4, s, first_row + i]
                     tiles.append(tile_at[lax.shift_right_logical(word, 10 * (u // 4)) & 1023])
                 columns.append(jnp.concatenate(tiles, axis=0))
-                blocks += [piece[i, u] for piece in pieces[:4]]
-                blocks.append(pieces[4 + half][i - GROUP * half, u])
-                blocks += [piece[i, u] for piece in pieces[6:]]
+                blocks += [piece[i, u] for piece in pieces]
             picked = jnp.concatenate(columns, axis=1)
             total += jnp.dot(picked, jnp.concatenate(blocks, axis=0), preferred_element_type=jnp.float32)
         total = (total * scale).reshape(slots, width, size)
         if is_first:
-            (out,) = outs
+            out = outs[0]
             out[i] = (-total).astype(out.dtype)
             line = lax.broadcasted_iota(jnp.int32, (width, size), 0)
             lane = lax.broadcasted_iota(jnp.int32, (width, size), 1)
@@ -66,16 +64,17 @@
             send[to] = jnp.where(core == 0, high, low).astype(send.dtype)
         return carry
 
-    for half in range(2):
-        lax.fori_loop(GROUP * half, GROUP * (half + 1), functools.partial(one_row, half), 0, unroll=GROUP)
+    lax.fori_loop(0, rows, one_row, 0, unroll=UNROLL)
+    if is_first and first_block == 1:
+        outs[1][...] = outs[0][pl.ds(1 - core, rows - 1)]
 
 
-def product(first_block, is_first, scale, index, parts, pieces, after=()):
+def product(first_block, is_first, scale, index, parts, pieces, after=(), cost=10):
     rows, slots, width, size = parts[0].shape
     dtype = parts[0].dtype
     if is_first:
-        outs = jax.ShapeDtypeStruct((rows, slots, width, size), dtype)
-        out_specs = pl.BlockSpec(memory_space=pltpu.VMEM)
+        outs = [jax.ShapeDtypeStruct((rows - k, slots, width, size), dtype) for k in range(1 + first_block)]
+        out_specs = [pl.BlockSpec(memory_space=pltpu.VMEM)] * (1 + first_block)
     else:
         out_rows = 2 * rows if after else rows
         outs = [jax.ShapeDtypeStruct((out_rows, slots, width // 2, size), dtype)] * 2
@@ -85,7 +84,7 @@
         functools.partial(product_kernel, first_block, is_first, scale, len(after)),
         out_shape=outs,
         in_specs=[pl.BlockSpec(memory_space=pl.ANY)]
-        + [pl.BlockSpec(memory_space=pltpu.VMEM)] * 12
+        + [pl.BlockSpec(memory_space=pltpu.VMEM)] * 11
         + [pl.BlockSpec(memory_space=pltpu.VMEM if len(after) == 2 else pl.ANY)] * len(after),
         out_specs=out_specs,
         scratch_shapes=[
@@ -94,7 +93,7 @@
             pltpu.SemaphoreType.DMA,
         ],
         compiler_params=pltpu.CompilerParams(vmem_limit_bytes=8 * 2**20),
-        cost_estimate=pl.CostEstimate(flops=COST * flops, bytes_accessed=rows * slots * size * size * 2, transcendentals=0),
+        cost_estimate=pl.CostEstimate(flops=int(cost * flops), bytes_accessed=rows * slots * size * size * 2, transcendentals=0),
     )(index, *parts, *pieces, *after)
 
 
@@ -108,12 +107,12 @@
         for k in range(len(streams)):
             risen[k].append(lax.ppermute(risen[k][-1], "cols", up))
             fallen[k].append(lax.ppermute(fallen[k][-1], "cols", down))
+    first = lax.axis_index("cols") % 2 == 0
+    outward = [(i, (i + 2) % count if i % 2 == 0 else (i - 2) % count) for i in range(count)]
     gathered = []
     for k in range(len(streams)):
-        half = streams[k].shape[0] // 2
-        last_up = lax.ppermute(risen[k][-1][:half], "cols", up)
-        last_down = lax.ppermute(fallen[k][-1][half:], "cols", down)
-        gathered.append(fallen[k] + [last_up, last_down] + risen[k][:0:-1])
+        farthest = lax.ppermute(jnp.where(first, risen[k][-1], fallen[k][-1]), "cols", outward)
+        gathered.append(fallen[k] + [farthest] + risen[k][:0:-1])
     return gathered
 
 
@@ -158,14 +157,14 @@
     outer_pieces, inner_pieces = gather_ring([outer_rows, inner_rows], cols // 2)
 
     scale = 1.0 / (slots * size)
-    shifted_outer = product(0, True, scale, index, (outer_halo, outer_rows, inner_rows), outer_pieces)
+    (shifted_outer,) = product(0, True, scale, index, (outer_halo, outer_rows, inner_rows), outer_pieces)
     shifted_outward = outward(shifted_outer)
-    shifted_inner = product(1, True, scale, index, (outer_rows, inner_rows, beyond), inner_pieces, [shifted_outer])
-    shifted_beyond = lax.ppermute(shifted_inner, "cols", swap)
+    shifted_inner, inner_edge = product(1, True, scale, index, (outer_rows, inner_rows, beyond), inner_pieces, [shifted_outer])
+    shifted_beyond = lax.ppermute(inner_edge, "cols", swap)
+    parts = (shifted_outer, shifted_inner, shifted_beyond)
+    done_inner = product(1, False, 0.5, index, parts, inner_pieces, cost=0.01)
     parts = (shifted_outward, shifted_outer, shifted_inner)
-    done_outer = product(0, False, 0.5, index, parts, outer_pieces)
-    parts = (shifted_outer, shifted_inner, shifted_beyond)
-    keep, send = product(1, False, 0.5, index, parts, inner_pieces, done_outer)
+    keep, send = product(0, False, 0.5, index, parts, outer_pieces, done_inner)
     got = lax.ppermute(send, "cols", swap)
     return jnp.where(first, jnp.concatenate([keep, got]), jnp.concatenate([got, keep]))
 

time: 115 us -> 111 us (0.965)
  starting transfers between devices: 88.9 us -> 82.8 us
  waiting for transfers between devices: 7.89 us -> 10.6 us
    ppermute x5 -> x3, waiting for transfers between devices: 0.01 us -> 4.6 us  [the longest x2 3.34 us: gather_ring(): lax.ppermute(jnp.where(first, risen[k][-1], fallen[k][-1]), 'cols', outward)]
    ppermute x1, starting transfers between devices: 6.67 us -> 2.29 us  [local(): got = lax.ppermute(send, 'cols', swap)]
    ppermute x6, waiting for transfers between devices: 6.1 us -> 4.18 us  [gather_ring(): risen[k].append(lax.ppermute(risen[k][-1], 'cols', up))]
    ppermute x5 -> x3, starting transfers between devices: 19 us -> 18.5 us  [the longest x2 9.76 us: gather_ring(): lax.ppermute(jnp.where(first, risen[k][-1], fallen[k][-1]), 'cols', outward)]
  transfers between devices with their start and end apart: 21 -> 19, of which waited for: 6 -> 7; matrix products, arithmetic and copies ran while one was open for 1% -> 1% of each run, Pallas kernels for 8% -> 9%
where the time goes in v4:
time: 111 us; the launch traced here: 110 us
  starting transfers between devices  82.8 us (75%)
  Pallas kernels  12.6 us (11%)
  waiting for transfers between devices  10.6 us (10%)
  other arithmetic  3.44 us (3%)
    ppermute x6, starting transfers between devices, gather_ring(): fallen[k].append(lax.ppermute(fallen[k][-1], 'cols', down))  27.4 us
    ppermute x1, starting transfers between devices, local(): other = lax.ppermute(values, 'cols', swap)  16.1 us
    pallas_call x4, Pallas kernels, product(): pl.pallas_call(functools.partial(product_kernel, first_block, is_first, s...  12.6 us
    ppermute x6, starting transfers between devices, gather_ring(): risen[k].append(lax.ppermute(risen[k][-1], 'cols', up))  11.5 us
    ppermute x2, starting transfers between devices, gather_ring(): lax.ppermute(jnp.where(first, risen[k][-1], fallen[k][-1]), 'cols', outward)  9.76 us
    ppermute x1, starting transfers between devices, local(): shifted_beyond = lax.ppermute(inner_edge, 'cols', swap)  8.7 us
    ppermute x2, starting transfers between devices, outward(): return lax.ppermute(piece, ('rows', 'cols'), pairs)  7.11 us
    ppermute x6, waiting for transfers between devices, gather_ring(): risen[k].append(lax.ppermute(risen[k][-1], 'cols', up))  4.18 us
  transfers between devices with their start and end apart: 19, of which 7 were waited for; matrix products, arithmetic and copies ran while one was open for 1% of the time, Pallas kernels for 9%

profile of v4, /device:TPU:1, one launch (start us, length us, event | category | flops | bytes accessed | tf_op | source)
XLA Modules:
  0.0 110.5 jit_solution(10796861199011670174)
XLA Ops:
  0.0 16.1 %collective-permute-start = (bf16[32,12,8,128]{3,2,1,0:T(8,128)(2,1)}, bf16[32,12,8,128]{3,2,1,0:T(8,128)(2,1)S(1)}, u32[]{:S(2)}, u32[]{:S(2)}) collective-permute-start(bf16[32,12,8,128]{3,2,1,0:T(8,128)(2,1)} %param.5), channel_id=1, source_target_pairs={{0,1},{1,0},{2,3},{3,2},{4,5},{5,4},{6,7},{7,6},{8,9},{9,8},{10,11... | collective-permute-start | bytes 2359304 | tf_op jit(solution)/shard_map/ppermute | solution.py:144
  19.4 1.9 %collective-permute-start.5 = (bf16[8,12,16,128]{3,2,1,0:T(8,128)(2,1)S(1)}, bf16[8,12,16,128]{3,2,1,0:T(8,128)(2,1)S(1)}, u32[]{:S(2)}, u32[]{:S(2)}) collective-permute-start(bf16[8,12,16,128]{3,2,1,0:T(8,128)(2,1)S(1)} %pad_maximum_fusion.refs_1_.refs_3_.refs_0_), channel_id=1, source_target_pairs={{0,2},{1,3},{2,4},{3,5},{4,6},{5,7},{6,8},{7,9},{8,10},{9,11},{10,... | collective-permute-start | bytes 1179656 | tf_op jit(solution)/shard_map/ppermute | solution.py:108
  21.4 4.6 %collective-permute-start.2 = (bf16[8,12,16,128]{3,2,1,0:T(8,128)(2,1)S(1)}, bf16[8,12,16,128]{3,2,1,0:T(8,128)(2,1)S(1)}, u32[]{:S(2)}, u32[]{:S(2)}) collective-permute-start(bf16[8,12,16,128]{3,2,1,0:T(8,128)(2,1)S(1)} %pad_maximum_fusion.refs_1_.refs_3_.refs_0_), channel_id=1, source_target_pairs={{2,0},{3,1},{4,2},{5,3},{6,4},{7,5},{8,6},{9,7},{10,8},{11,9},{12,... | collective-permute-start | bytes 1179656 | tf_op jit(solution)/shard_map/ppermute | solution.py:109
  26.0 1.9 %collective-permute-start.13 = (bf16[8,12,16,128]{3,2,1,0:T(8,128)(2,1)S(1)}, bf16[8,12,16,128]{3,2,1,0:T(8,128)(2,1)S(1)}, u32[]{:S(2)}, u32[]{:S(2)}) collective-permute-start(bf16[8,12,16,128]{3,2,1,0:T(8,128)(2,1)S(1)} %pad_maximum_fusion.1.refs_2_.refs_1_.refs_3_), channel_id=1, source_target_pairs={{0,2},{1,3},{2,4},{3,5},{4,6},{5,7},{6,8},{7,9},{8,10},{9,11},{10,... | collective-permute-start | bytes 1179656 | tf_op jit(solution)/shard_map/ppermute | solution.py:108
  28.0 4.6 %collective-permute-start.10 = (bf16[8,12,16,128]{3,2,1,0:T(8,128)(2,1)S(1)}, bf16[8,12,16,128]{3,2,1,0:T(8,128)(2,1)S(1)}, u32[]{:S(2)}, u32[]{:S(2)}) collective-permute-start(bf16[8,12,16,128]{3,2,1,0:T(8,128)(2,1)S(1)} %pad_maximum_fusion.1.refs_2_.refs_1_.refs_3_), channel_id=1, source_target_pairs={{2,0},{3,1},{4,2},{5,3},{6,4},{7,5},{8,6},{9,7},{10,8},{11,9},{12,... | collective-permute-start | bytes 1179656 | tf_op jit(solution)/shard_map/ppermute | solution.py:109
  32.9 1.9 %collective-permute-start.6 = (bf16[8,12,16,128]{3,2,1,0:T(8,128)(2,1)S(1)}, bf16[8,12,16,128]{3,2,1,0:T(8,128)(2,1)S(1)}, u32[]{:S(2)}, u32[]{:S(2)}) collective-permute-start(bf16[8,12,16,128]{3,2,1,0:T(8,128)(2,1)S(1)} %collective-permute-done.5.refs_10_), channel_id=1, source_target_pairs={{0,2},{1,3},{2,4},{3,5},{4,6},{5,7},{6,8},{7,9},{8,10},{9,11},{10,... | collective-permute-start | bytes 1179656 | tf_op jit(solution)/shard_map/ppermute | solution.py:108
  34.8 4.6 %collective-permute-start.3 = (bf16[8,12,16,128]{3,2,1,0:T(8,128)(2,1)S(1)}, bf16[8,12,16,128]{3,2,1,0:T(8,128)(2,1)S(1)}, u32[]{:S(2)}, u32[]{:S(2)}) collective-permute-start(bf16[8,12,16,128]{3,2,1,0:T(8,128)(2,1)S(1)} %collective-permute-done.2.refs_4_), channel_id=1, source_target_pairs={{2,0},{3,1},{4,2},{5,3},{6,4},{7,5},{8,6},{9,7},{10,8},{11,9},{12,... | collective-permute-start | bytes 1179656 | tf_op jit(solution)/shard_map/ppermute | solution.py:109
  39.4 1.9 %collective-permute-done.13.refs_10_ = bf16[8,12,16,128]{3,2,1,0:T(8,128)(2,1)S(1)} collective-permute-done((bf16[8,12,16,128]{3,2,1,0:T(8,128)(2,1)S(1)}, bf16[8,12,16,128]{3,2,1,0:T(8,128)(2,1)S(1)}, u32[]{:S(2)}, u32[]{:S(2)}) %collective-permute-start.13) | collective-permute-done | bytes 393248 | tf_op jit(solution)/shard_map/ppermute | solution.py:108
  43.2 4.6 %collective-permute-start.11 = (bf16[8,12,16,128]{3,2,1,0:T(8,128)(2,1)S(1)}, bf16[8,12,16,128]{3,2,1,0:T(8,128)(2,1)S(1)}, u32[]{:S(2)}, u32[]{:S(2)}) collective-permute-start(bf16[8,12,16,128]{3,2,1,0:T(8,128)(2,1)S(1)} %collective-permute-done.10.refs_4_), channel_id=1, source_target_pairs={{2,0},{3,1},{4,2},{5,3},{6,4},{7,5},{8,6},{9,7},{10,8},{11,9},{12,... | collective-permute-start | bytes 1179656 | tf_op jit(solution)/shard_map/ppermute | solution.py:109
  47.8 1.9 %collective-permute-done.6.refs_9_ = bf16[8,12,16,128]{3,2,1,0:T(8,128)(2,1)S(1)} collective-permute-done((bf16[8,12,16,128]{3,2,1,0:T(8,128)(2,1)S(1)}, bf16[8,12,16,128]{3,2,1,0:T(8,128)(2,1)S(1)}, u32[]{:S(2)}, u32[]{:S(2)}) %collective-permute-start.6) | collective-permute-done | bytes 393248 | tf_op jit(solution)/shard_map/ppermute | solution.py:108
  51.7 4.6 %collective-permute-start.4 = (bf16[8,12,16,128]{3,2,1,0:T(8,128)(2,1)S(1)}, bf16[8,12,16,128]{3,2,1,0:T(8,128)(2,1)S(1)}, u32[]{:S(2)}, u32[]{:S(2)}) collective-permute-start(bf16[8,12,16,128]{3,2,1,0:T(8,128)(2,1)S(1)} %collective-permute-done.3.refs_5_), channel_id=1, source_target_pairs={{2,0},{3,1},{4,2},{5,3},{6,4},{7,5},{8,6},{9,7},{10,8},{11,9},{12,... | collective-permute-start | bytes 1179656 | tf_op jit(solution)/shard_map/ppermute | solution.py:109
  56.2 5.1 %collective-permute-start.1 = (bf16[8,12,16,128]{3,2,1,0:T(8,128)(2,1)S(1)}, bf16[8,12,16,128]{3,2,1,0:T(8,128)(2,1)S(1)}, u32[]{:S(2)}, u32[]{:S(2)}) collective-permute-start(bf16[8,12,16,128]{3,2,1,0:T(8,128)(2,1)S(1)} %pad_maximum_fusion.refs_1_.refs_3_.refs_0_), channel_id=1, source_target_pairs={{0,1009},{1,16},{2,1011},{3,18},{4,1013},{5,20},{6,1015},{7,22},{8... | collective-permute-start | bytes 1179656 | tf_op jit(solution)/shard_map/ppermute | solution.py:134
  61.3 1.9 %collective-permute-start.15 = (bf16[8,12,16,128]{3,2,1,0:T(8,128)(2,1)S(1)}, bf16[8,12,16,128]{3,2,1,0:T(8,128)(2,1)S(1)}, u32[]{:S(2)}, u32[]{:S(2)}) collective-permute-start(bf16[8,12,16,128]{3,2,1,0:T(8,128)(2,1)S(1)} %collective-permute-done.14.refs_9_), channel_id=1, source_target_pairs={{0,2},{1,3},{2,4},{3,5},{4,6},{5,7},{6,8},{7,9},{8,10},{9,11},{10,... | collective-permute-start | bytes 1179656 | tf_op jit(solution)/shard_map/ppermute | solution.py:108
  63.3 4.6 %collective-permute-start.12 = (bf16[8,12,16,128]{3,2,1,0:T(8,128)(2,1)S(1)}, bf16[8,12,16,128]{3,2,1,0:T(8,128)(2,1)S(1)}, u32[]{:S(2)}, u32[]{:S(2)}) collective-permute-start(bf16[8,12,16,128]{3,2,1,0:T(8,128)(2,1)S(1)} %collective-permute-done.11.refs_5_), channel_id=1, source_target_pairs={{2,0},{3,1},{4,2},{5,3},{6,4},{7,5},{8,6},{9,7},{10,8},{11,9},{12,... | collective-permute-start | bytes 1179656 | tf_op jit(solution)/shard_map/ppermute | solution.py:109
  67.9 4.9 %collective-permute-start.8 = (bf16[8,12,16,128]{3,2,1,0:T(8,128)(2,1)S(1)}, bf16[8,12,16,128]{3,2,1,0:T(8,128)(2,1)S(1)}, u32[]{:S(2)}, u32[]{:S(2)}) collective-permute-start(bf16[8,12,16,128]{3,2,1,0:T(8,128)(2,1)S(1)} %broadcast_select_fusion.1), channel_id=1, source_target_pairs={{0,2},{1,15},{2,4},{3,1},{4,6},{5,3},{6,8},{7,5},{8,10},{9,7},{10,... | collective-permute-start | bytes 1179656 | tf_op jit(solution)/shard_map/ppermute | solution.py:114
  73.0 4.9 %collective-permute-start.16 = (bf16[8,12,16,128]{3,2,1,0:T(8,128)(2,1)S(1)}, bf16[8,12,16,128]{3,2,1,0:T(8,128)(2,1)S(1)}, u32[]{:S(2)}, u32[]{:S(2)}) collective-permute-start(bf16[8,12,16,128]{3,2,1,0:T(8,128)(2,1)S(1)} %broadcast_select_fusion), channel_id=1, source_target_pairs={{0,2},{1,15},{2,4},{3,1},{4,6},{5,3},{6,8},{7,5},{8,10},{9,7},{10,... | collective-permute-start | bytes 1179656 | tf_op jit(solution)/shard_map/ppermute | solution.py:114
  77.9 3.3 %collective-permute-done.8.refs_7_ = bf16[8,12,16,128]{3,2,1,0:T(8,128)(2,1)S(1)} collective-permute-done((bf16[8,12,16,128]{3,2,1,0:T(8,128)(2,1)S(1)}, bf16[8,12,16,128]{3,2,1,0:T(8,128)(2,1)S(1)}, u32[]{:S(2)}, u32[]{:S(2)}) %collective-permute-start.8) | collective-permute-done | bytes 393248 | tf_op jit(solution)/shard_map/ppermute | solution.py:114
  81.2 3.1 %shard_map.37.refs_11_.refs_0_.refs_1_ = bf16[8,12,16,128]{3,2,1,0:T(8,128)(2,1)S(1)} custom-call(s32[4,12,32]{2,1,0:T(8,128)S(1)} %fusion.index_from, bf16[8,12,16,128]{3,2,1,0:T(8,128)(2,1)S(1)} %collective-permute-done.1.refs_0_, bf16[8,12,16,128]{3,2,1,0:T(8,128)(2,1)S(1)} %pad_maximum_fusion.refs_1_.refs_3_.refs_0_, ...), custom_call_target="tpu_custom_call" | custom-call | flops 6039797760 | bytes 3145728 | tf_op jit(solution)/shard_map/pallas_call | solution.py:83
  84.4 2.0 %collective-permute-start.9 = (bf16[8,12,16,128]{3,2,1,0:T(8,128)(2,1)S(1)}, bf16[8,12,16,128]{3,2,1,0:T(8,128)(2,1)S(1)}, u32[]{:S(2)}, u32[]{:S(2)}) collective-permute-start(bf16[8,12,16,128]{3,2,1,0:T(8,128)(2,1)S(1)} %shard_map.37.refs_11_.refs_0_.refs_1_), channel_id=1, source_target_pairs={{0,1009},{1,16},{2,1011},{3,18},{4,1013},{5,20},{6,1015},{7,22},{8... | collective-permute-start | bytes 1179656 | tf_op jit(solution)/shard_map/ppermute | solution.py:134
  86.4 3.2 %shard_map.38 = (bf16[8,12,16,128]{3,2,1,0:T(8,128)(2,1)S(1)}, bf16[7,12,16,128]{3,2,1,0:T(8,128)(2,1)S(1)}) custom-call(s32[4,12,32]{2,1,0:T(8,128)S(1)} %fusion.index_from, bf16[8,12,16,128]{3,2,1,0:T(8,128)(2,1)S(1)} %pad_maximum_fusion.refs_1_.refs_3_.refs_0_, bf16[8,12,16,128]{3,2,1,0:T(8,128)(2,1)S(1)} %pad_maximum_fusion.1.refs_2_.refs_1_.refs_3_, ...), custom_call_target="tpu_custom_call" | custom-call | flops 6039797760 | bytes 3145728 | tf_op jit(solution)/shard_map/pallas_call | solution.py:83
  89.6 8.7 %collective-permute-start.17 = (bf16[7,12,16,128]{3,2,1,0:T(8,128)(2,1)S(1)}, bf16[7,12,16,128]{3,2,1,0:T(8,128)(2,1)S(1)}, u32[]{:S(2)}, u32[]{:S(2)}) collective-permute-start(bf16[7,12,16,128]{3,2,1,0:T(8,128)(2,1)S(1)} %get-tuple-element.16), channel_id=1, source_target_pairs={{0,1},{1,0},{2,3},{3,2},{4,5},{5,4},{6,7},{7,6},{8,9},{9,8},{10,11... | collective-permute-start | bytes 1032200 | tf_op jit(solution)/shard_map/ppermute | solution.py:163
  99.5 3.1 %shard_map.39 = (bf16[8,12,8,128]{3,2,1,0:T(8,128)(2,1)S(1)}, bf16[8,12,8,128]{3,2,1,0:T(8,128)(2,1)S(1)}) custom-call(s32[4,12,32]{2,1,0:T(8,128)S(1)} %fusion.index_from, bf16[8,12,16,128]{3,2,1,0:T(8,128)(2,1)S(1)} %shard_map.37.refs_11_.refs_0_.refs_1_, bf16[8,12,16,128]{3,2,1,0:T(8,128)(2,1)S(1)} %get-tuple-element.15.refs_1_.refs_2_, ...), custom_call_target="tpu_custom_call" | custom-call | flops 6039797 | bytes 3145728 | tf_op jit(solution)/shard_map/pallas_call | solution.py:83
  102.7 3.2 %shard_map.40 = (bf16[16,12,8,128]{3,2,1,0:T(8,128)(2,1)S(1)}, bf16[16,12,8,128]{3,2,1,0:T(8,128)(2,1)S(1)}) custom-call(s32[4,12,32]{2,1,0:T(8,128)S(1)} %fusion.index_from, bf16[8,12,16,128]{3,2,1,0:T(8,128)(2,1)S(1)} %collective-permute-done.9.refs_0_, bf16[8,12,16,128]{3,2,1,0:T(8,128)(2,1)S(1)} %shard_map.37.refs_11_.refs_0_.refs_1_, ...), custom_call_target="tpu_custom_call" | custom-call | flops 6039797760 | bytes 3145728 | tf_op jit(solution)/shard_map/pallas_call | solution.py:83
  105.8 2.3 %collective-permute-start.18 = (bf16[16,12,8,128]{3,2,1,0:T(8,128)(2,1)S(1)}, bf16[16,12,8,128]{3,2,1,0:T(8,128)(2,1)S(1)}, u32[]{:S(2)}, u32[]{:S(2)}) collective-permute-start(bf16[16,12,8,128]{3,2,1,0:T(8,128)(2,1)S(1)} %get-tuple-element.20), channel_id=1, source_target_pairs={{0,1},{1,0},{2,3},{3,2},{4,5},{5,4},{6,7},{7,6},{8,9},{9,8},{10,11... | collective-permute-start | bytes 1179656 | tf_op jit(solution)/shard_map/ppermute | solution.py:168
  (30 shorter events, 11.3 us)
Async XLA Ops:
  0.0 18.2 %collective-permute-start = (bf16[32,12,8,128]{3,2,1,0:T(8,128)(2,1)}, bf16[32,12,8,128]{3,2,1,0:T(8,128)(2,1)S(1)}, u32[]{:S(2)}, u32[]{:S(2)}) collective-permute-start(bf16[32,12,8,128]{3,2,1,0:T(8,128)(2,1)} %param.5), channel_id=1, source_target_pairs={{0,1},{1,0},{2,3},{3,2},{4,5},{5,4},{6,7},{7,6},{8,9},{9,8},{10,11... | collective-permute-start | bytes 2359304 | tf_op jit(solution)/shard_map/ppermute | solution.py:144
  16.1 0.7 copy-start
  19.4 13.4 %collective-permute-start.5 = (bf16[8,12,16,128]{3,2,1,0:T(8,128)(2,1)S(1)}, bf16[8,12,16,128]{3,2,1,0:T(8,128)(2,1)S(1)}, u32[]{:S(2)}, u32[]{:S(2)}) collective-permute-start(bf16[8,12,16,128]{3,2,1,0:T(8,128)(2,1)S(1)} %pad_maximum_fusion.refs_1_.refs_3_.refs_0_), channel_id=1, source_target_pairs={{0,2},{1,3},{2,4},{3,5},{4,6},{5,7},{6,8},{7,9},{8,10},{9,11},{10,... | collective-permute-start | bytes 1179656 | tf_op jit(solution)/shard_map/ppermute | solution.py:108
  21.4 13.4 %collective-permute-start.2 = (bf16[8,12,16,128]{3,2,1,0:T(8,128)(2,1)S(1)}, bf16[8,12,16,128]{3,2,1,0:T(8,128)(2,1)S(1)}, u32[]{:S(2)}, u32[]{:S(2)}) collective-permute-start(bf16[8,12,16,128]{3,2,1,0:T(8,128)(2,1)S(1)} %pad_maximum_fusion.refs_1_.refs_3_.refs_0_), channel_id=1, source_target_pairs={{2,0},{3,1},{4,2},{5,3},{6,4},{7,5},{8,6},{9,7},{10,8},{11,9},{12,... | collective-permute-start | bytes 1179656 | tf_op jit(solution)/shard_map/ppermute | solution.py:109
  26.0 15.3 %collective-permute-start.13 = (bf16[8,12,16,128]{3,2,1,0:T(8,128)(2,1)S(1)}, bf16[8,12,16,128]{3,2,1,0:T(8,128)(2,1)S(1)}, u32[]{:S(2)}, u32[]{:S(2)}) collective-permute-start(bf16[8,12,16,128]{3,2,1,0:T(8,128)(2,1)S(1)} %pad_maximum_fusion.1.refs_2_.refs_1_.refs_3_), channel_id=1, source_target_pairs={{0,2},{1,3},{2,4},{3,5},{4,6},{5,7},{6,8},{7,9},{8,10},{9,11},{10,... | collective-permute-start | bytes 1179656 | tf_op jit(solution)/shard_map/ppermute | solution.py:108
  28.0 15.3 %collective-permute-start.10 = (bf16[8,12,16,128]{3,2,1,0:T(8,128)(2,1)S(1)}, bf16[8,12,16,128]{3,2,1,0:T(8,128)(2,1)S(1)}, u32[]{:S(2)}, u32[]{:S(2)}) collective-permute-start(bf16[8,12,16,128]{3,2,1,0:T(8,128)(2,1)S(1)} %pad_maximum_fusion.1.refs_2_.refs_1_.refs_3_), channel_id=1, source_target_pairs={{2,0},{3,1},{4,2},{5,3},{6,4},{7,5},{8,6},{9,7},{10,8},{11,9},{12,... | collective-permute-start | bytes 1179656 | tf_op jit(solution)/shard_map/ppermute | solution.py:109
  32.9 16.9 %collective-permute-start.6 = (bf16[8,12,16,128]{3,2,1,0:T(8,128)(2,1)S(1)}, bf16[8,12,16,128]{3,2,1,0:T(8,128)(2,1)S(1)}, u32[]{:S(2)}, u32[]{:S(2)}) collective-permute-start(bf16[8,12,16,128]{3,2,1,0:T(8,128)(2,1)S(1)} %collective-permute-done.5.refs_10_), channel_id=1, source_target_pairs={{0,2},{1,3},{2,4},{3,5},{4,6},{5,7},{6,8},{7,9},{8,10},{9,11},{10,... | collective-permute-start | bytes 1179656 | tf_op jit(solution)/shard_map/ppermute | solution.py:108
  34.8 16.8 %collective-permute-start.3 = (bf16[8,12,16,128]{3,2,1,0:T(8,128)(2,1)S(1)}, bf16[8,12,16,128]{3,2,1,0:T(8,128)(2,1)S(1)}, u32[]{:S(2)}, u32[]{:S(2)}) collective-permute-start(bf16[8,12,16,128]{3,2,1,0:T(8,128)(2,1)S(1)} %collective-permute-done.2.refs_4_), channel_id=1, source_target_pairs={{2,0},{3,1},{4,2},{5,3},{6,4},{7,5},{8,6},{9,7},{10,8},{11,9},{12,... | collective-permute-start | bytes 1179656 | tf_op jit(solution)/shard_map/ppermute | solution.py:109
  41.3 20.0 %collective-permute-start.14 = (bf16[8,12,16,128]{3,2,1,0:T(8,128)(2,1)S(1)}, bf16[8,12,16,128]{3,2,1,0:T(8,128)(2,1)S(1)}, u32[]{:S(2)}, u32[]{:S(2)}) collective-permute-start(bf16[8,12,16,128]{3,2,1,0:T(8,128)(2,1)S(1)} %collective-permute-done.13.refs_10_), channel_id=1, source_target_pairs={{0,2},{1,3},{2,4},{3,5},{4,6},{5,7},{6,8},{7,9},{8,10},{9,11},{10,... | collective-permute-start | bytes 1179656 | tf_op jit(solution)/shard_map/ppermute | solution.py:108
  43.2 20.0 %collective-permute-start.11 = (bf16[8,12,16,128]{3,2,1,0:T(8,128)(2,1)S(1)}, bf16[8,12,16,128]{3,2,1,0:T(8,128)(2,1)S(1)}, u32[]{:S(2)}, u32[]{:S(2)}) collective-permute-start(bf16[8,12,16,128]{3,2,1,0:T(8,128)(2,1)S(1)} %collective-permute-done.10.refs_4_), channel_id=1, source_target_pairs={{2,0},{3,1},{4,2},{5,3},{6,4},{7,5},{8,6},{9,7},{10,8},{11,9},{12,... | collective-permute-start | bytes 1179656 | tf_op jit(solution)/shard_map/ppermute | solution.py:109
  49.7 18.1 %collective-permute-start.7 = (bf16[8,12,16,128]{3,2,1,0:T(8,128)(2,1)S(1)}, bf16[8,12,16,128]{3,2,1,0:T(8,128)(2,1)S(1)}, u32[]{:S(2)}, u32[]{:S(2)}) collective-permute-start(bf16[8,12,16,128]{3,2,1,0:T(8,128)(2,1)S(1)} %collective-permute-done.6.refs_9_), channel_id=1, source_target_pairs={{0,2},{1,3},{2,4},{3,5},{4,6},{5,7},{6,8},{7,9},{8,10},{9,11},{10,... | collective-permute-start | bytes 1179656 | tf_op jit(solution)/shard_map/ppermute | solution.py:108
  51.7 16.2 %collective-permute-start.4 = (bf16[8,12,16,128]{3,2,1,0:T(8,128)(2,1)S(1)}, bf16[8,12,16,128]{3,2,1,0:T(8,128)(2,1)S(1)}, u32[]{:S(2)}, u32[]{:S(2)}) collective-permute-start(bf16[8,12,16,128]{3,2,1,0:T(8,128)(2,1)S(1)} %collective-permute-done.3.refs_5_), channel_id=1, source_target_pairs={{2,0},{3,1},{4,2},{5,3},{6,4},{7,5},{8,6},{9,7},{10,8},{11,9},{12,... | collective-permute-start | bytes 1179656 | tf_op jit(solution)/shard_map/ppermute | solution.py:109
  56.2 21.6 %collective-permute-start.1 = (bf16[8,12,16,128]{3,2,1,0:T(8,128)(2,1)S(1)}, bf16[8,12,16,128]{3,2,1,0:T(8,128)(2,1)S(1)}, u32[]{:S(2)}, u32[]{:S(2)}) collective-permute-start(bf16[8,12,16,128]{3,2,1,0:T(8,128)(2,1)S(1)} %pad_maximum_fusion.refs_1_.refs_3_.refs_0_), channel_id=1, source_target_pairs={{0,1009},{1,16},{2,1011},{3,18},{4,1013},{5,20},{6,1015},{7,22},{8... | collective-permute-start | bytes 1179656 | tf_op jit(solution)/shard_map/ppermute | solution.py:134
  61.3 11.6 %collective-permute-start.15 = (bf16[8,12,16,128]{3,2,1,0:T(8,128)(2,1)S(1)}, bf16[8,12,16,128]{3,2,1,0:T(8,128)(2,1)S(1)}, u32[]{:S(2)}, u32[]{:S(2)}) collective-permute-start(bf16[8,12,16,128]{3,2,1,0:T(8,128)(2,1)S(1)} %collective-permute-done.14.refs_9_), channel_id=1, source_target_pairs={{0,2},{1,3},{2,4},{3,5},{4,6},{5,7},{6,8},{7,9},{8,10},{9,11},{10,... | collective-permute-start | bytes 1179656 | tf_op jit(solution)/shard_map/ppermute | solution.py:108
  63.3 9.6 %collective-permute-start.12 = (bf16[8,12,16,128]{3,2,1,0:T(8,128)(2,1)S(1)}, bf16[8,12,16,128]{3,2,1,0:T(8,128)(2,1)S(1)}, u32[]{:S(2)}, u32[]{:S(2)}) collective-permute-start(bf16[8,12,16,128]{3,2,1,0:T(8,128)(2,1)S(1)} %collective-permute-done.11.refs_5_), channel_id=1, source_target_pairs={{2,0},{3,1},{4,2},{5,3},{6,4},{7,5},{8,6},{9,7},{10,8},{11,9},{12,... | collective-permute-start | bytes 1179656 | tf_op jit(solution)/shard_map/ppermute | solution.py:109
  67.9 13.3 %collective-permute-start.8 = (bf16[8,12,16,128]{3,2,1,0:T(8,128)(2,1)S(1)}, bf16[8,12,16,128]{3,2,1,0:T(8,128)(2,1)S(1)}, u32[]{:S(2)}, u32[]{:S(2)}) collective-permute-start(bf16[8,12,16,128]{3,2,1,0:T(8,128)(2,1)S(1)} %broadcast_select_fusion.1), channel_id=1, source_target_pairs={{0,2},{1,15},{2,4},{3,1},{4,6},{5,3},{6,8},{7,5},{8,10},{9,7},{10,... | collective-permute-start | bytes 1179656 | tf_op jit(solution)/shard_map/ppermute | solution.py:114
  73.0 13.4 %collective-permute-start.16 = (bf16[8,12,16,128]{3,2,1,0:T(8,128)(2,1)S(1)}, bf16[8,12,16,128]{3,2,1,0:T(8,128)(2,1)S(1)}, u32[]{:S(2)}, u32[]{:S(2)}) collective-permute-start(bf16[8,12,16,128]{3,2,1,0:T(8,128)(2,1)S(1)} %broadcast_select_fusion), channel_id=1, source_target_pairs={{0,2},{1,15},{2,4},{3,1},{4,6},{5,3},{6,8},{7,5},{8,10},{9,7},{10,... | collective-permute-start | bytes 1179656 | tf_op jit(solution)/shard_map/ppermute | solution.py:114
  84.4 18.3 %collective-permute-start.9 = (bf16[8,12,16,128]{3,2,1,0:T(8,128)(2,1)S(1)}, bf16[8,12,16,128]{3,2,1,0:T(8,128)(2,1)S(1)}, u32[]{:S(2)}, u32[]{:S(2)}) collective-permute-start(bf16[8,12,16,128]{3,2,1,0:T(8,128)(2,1)S(1)} %shard_map.37.refs_11_.refs_0_.refs_1_), channel_id=1, source_target_pairs={{0,1009},{1,16},{2,1011},{3,18},{4,1013},{5,20},{6,1015},{7,22},{8... | collective-permute-start | bytes 1179656 | tf_op jit(solution)/shard_map/ppermute | solution.py:134
  89.6 10.0 %collective-permute-start.17 = (bf16[7,12,16,128]{3,2,1,0:T(8,128)(2,1)S(1)}, bf16[7,12,16,128]{3,2,1,0:T(8,128)(2,1)S(1)}, u32[]{:S(2)}, u32[]{:S(2)}) collective-permute-start(bf16[7,12,16,128]{3,2,1,0:T(8,128)(2,1)S(1)} %get-tuple-element.16), channel_id=1, source_target_pairs={{0,1},{1,0},{2,3},{3,2},{4,5},{5,4},{6,7},{7,6},{8,9},{9,8},{10,11... | collective-permute-start | bytes 1032200 | tf_op jit(solution)/shard_map/ppermute | solution.py:163
  105.8 3.6 %collective-permute-start.18 = (bf16[16,12,8,128]{3,2,1,0:T(8,128)(2,1)S(1)}, bf16[16,12,8,128]{3,2,1,0:T(8,128)(2,1)S(1)}, u32[]{:S(2)}, u32[]{:S(2)}) collective-permute-start(bf16[16,12,8,128]{3,2,1,0:T(8,128)(2,1)S(1)} %get-tuple-element.20), channel_id=1, source_target_pairs={{0,1},{1,0},{2,3},{3,2},{4,5},{5,4},{6,7},{7,6},{8,9},{9,8},{10,11... | collective-permute-start | bytes 1179656 | tf_op jit(solution)/shard_map/ppermute | solution.py:168

commit v5 on v4

--- a/solution.py
+++ b/solution.py
@@ -14,17 +14,22 @@
     parts, pieces = refs[:3], refs[3:11]
     outs, (window, index_ref, index_sem) = refs[11 + extra:-3], refs[-3:]
     rows, slots, width, size = parts[0].shape
+    ring = size // width
     col = lax.axis_index("cols")
     z, core = col // 2, lax.rem(col, 2)
     first_row = rows * jnp.where(core == 0, first_block, 3 - first_block)
 
     index_copy = pltpu.make_async_copy(index_from, index_ref, index_sem)
     index_copy.start()
-    turn = lax.rem(size - width * z, size)
+    lane = lax.broadcasted_iota(jnp.int32, (size, size), 1)
+    away = jnp.where(core == 0, z + lane // width, z - lane // width + ring) & (ring - 1)
+    turned = lax.broadcasted_iota(jnp.int32, (size, size), 0) == away * width + (lane & (width - 1))
+    turned = turned.astype(jnp.float32).astype(window.dtype)
     for k, part in enumerate(parts):
         to = rows * (first_block + k) + (core if part.shape[0] < rows else 0)
         for row in range(part.shape[0]):
-            window[to + row, pl.ds(0, slots)] = pltpu.roll(part[row], turn, 2)
+            lines = jnp.dot(part[row].reshape(slots * width, size), turned, preferred_element_type=jnp.float32)
+            window[to + row, pl.ds(0, slots)] = lines.astype(window.dtype).reshape(slots, width, size)
     window[4 * rows, 0] = jnp.zeros((width, size), window.dtype)
     index_copy.wait()
     tile_at = window.reshape(window.shape[0] * window.shape[1], width, size)
@@ -99,21 +104,15 @@
 
 def gather_ring(streams, ring):
     count = 2 * ring
-    up = [(i, (i + 2) % count) for i in range(count)]
-    down = [((i + 2) % count, i) for i in range(count)]
-    risen = [[piece] for piece in streams]
-    fallen = [[piece] for piece in streams]
+    ahead = [(i, (i + 2) % count if i % 2 == 0 else (i - 2) % count) for i in range(count)]
+    back = [(to, i) for i, to in ahead]
+    gone = [[piece] for piece in streams]
+    come = [[piece] for piece in streams]
     for step in range(ring // 2 - 1):
         for k in range(len(streams)):
-            risen[k].append(lax.ppermute(risen[k][-1], "cols", up))
-            fallen[k].append(lax.ppermute(fallen[k][-1], "cols", down))
-    first = lax.axis_index("cols") % 2 == 0
-    outward = [(i, (i + 2) % count if i % 2 == 0 else (i - 2) % count) for i in range(count)]
-    gathered = []
-    for k in range(len(streams)):
-        farthest = lax.ppermute(jnp.where(first, risen[k][-1], fallen[k][-1]), "cols", outward)
-        gathered.append(fallen[k] + [farthest] + risen[k][:0:-1])
-    return gathered
+            gone[k].append(lax.ppermute(gone[k][-1], "cols", ahead))
+            come[k].append(lax.ppermute(come[k][-1], "cols", back))
+    return [come[k] + [lax.ppermute(gone[k][-1], "cols", ahead)] + gone[k][:0:-1] for k in range(len(streams))]
 
 
 def local(columns, fetch, values):

time: 111 us -> 105 us (0.946)
  waiting for transfers between devices: 10.6 us -> 8 us
  starting transfers between devices: 82.8 us -> 80.4 us
    ppermute x1, starting transfers between devices: 8.7 us -> 4.27 us  [local(): shifted_beyond = lax.ppermute(inner_edge, 'cols', swap)]
    ppermute x2, starting transfers between devices: 7.11 us -> 10.3 us  [outward(): return lax.ppermute(piece, ('rows', 'cols'), pairs)]
    ppermute x14, waiting for transfers between devices: 7.54 us -> 4.98 us  [the longest x6 2.61 us: gather_ring(): gone[k].append(lax.ppermute(gone[k][-1], 'cols', ahead))]
    ppermute x14, starting transfers between devices: 48.7 us -> 47.5 us  [the longest x6 25.4 us: gather_ring(): gone[k].append(lax.ppermute(gone[k][-1], 'cols', ahead))]
  transfers between devices with their start and end apart: 19 -> 19, of which waited for: 7 -> 6; matrix products, arithmetic and copies ran while one was open for 1% -> 1% of each run, Pallas kernels for 9% -> 8%
where the time goes in v5:
time: 105 us
  starting transfers between devices  80.4 us (77%)
  Pallas kernels  11.9 us (11%)
  waiting for transfers between devices  8 us (8%)
  other arithmetic  3.35 us (3%)
    ppermute x6, starting transfers between devices, gather_ring(): gone[k].append(lax.ppermute(gone[k][-1], 'cols', ahead))  25.4 us
    ppermute x1, starting transfers between devices, local(): other = lax.ppermute(values, 'cols', swap)  16.1 us
    ppermute x6, starting transfers between devices, gather_ring(): come[k].append(lax.ppermute(come[k][-1], 'cols', back))  13 us
    pallas_call x4, Pallas kernels, product(): pl.pallas_call(functools.partial(product_kernel, first_block, is_first, s...  11.9 us
    ppermute x2, starting transfers between devices, outward(): return lax.ppermute(piece, ('rows', 'cols'), pairs)  10.3 us
    ppermute x2, starting transfers between devices, gather_ring(): lax.ppermute(gone[k][-1], 'cols', ahead)  9.15 us
    ppermute x1, starting transfers between devices, local(): shifted_beyond = lax.ppermute(inner_edge, 'cols', swap)  4.27 us
    ppermute x6, waiting for transfers between devices, gather_ring(): gone[k].append(lax.ppermute(gone[k][-1], 'cols', ahead))  2.61 us
  transfers between devices with their start and end apart: 19, of which 6 were waited for; matrix products, arithmetic and copies ran while one was open for 1% of the time, Pallas kernels for 8%

profile of v5, /device:TPU:1, one launch (start us, length us, event | category | flops | bytes accessed | tf_op | source)
XLA Modules:
  0.0 104.7 jit_solution(2019808010610418254)
XLA Ops:
  0.0 16.1 %collective-permute-start = (bf16[32,12,8,128]{3,2,1,0:T(8,128)(2,1)}, bf16[32,12,8,128]{3,2,1,0:T(8,128)(2,1)S(1)}, u32[]{:S(2)}, u32[]{:S(2)}) collective-permute-start(bf16[32,12,8,128]{3,2,1,0:T(8,128)(2,1)} %param.5), channel_id=1, source_target_pairs={{0,1},{1,0},{2,3},{3,2},{4,5},{5,4},{6,7},{7,6},{8,9},{9,8},{10,11... | collective-permute-start | bytes 2359304 | tf_op jit(solution)/shard_map/ppermute | solution.py:143
  19.4 4.4 %collective-permute-start.5 = (bf16[8,12,16,128]{3,2,1,0:T(8,128)(2,1)S(1)}, bf16[8,12,16,128]{3,2,1,0:T(8,128)(2,1)S(1)}, u32[]{:S(2)}, u32[]{:S(2)}) collective-permute-start(bf16[8,12,16,128]{3,2,1,0:T(8,128)(2,1)S(1)} %pad_maximum_fusion.refs_1_.refs_3_.refs_0_), channel_id=1, source_target_pairs={{0,2},{1,15},{2,4},{3,1},{4,6},{5,3},{6,8},{7,5},{8,10},{9,7},{10,... | collective-permute-start | bytes 1179656 | tf_op jit(solution)/shard_map/ppermute | solution.py:113
  23.9 1.9 %collective-permute-start.13 = (bf16[8,12,16,128]{3,2,1,0:T(8,128)(2,1)S(1)}, bf16[8,12,16,128]{3,2,1,0:T(8,128)(2,1)S(1)}, u32[]{:S(2)}, u32[]{:S(2)}) collective-permute-start(bf16[8,12,16,128]{3,2,1,0:T(8,128)(2,1)S(1)} %pad_maximum_fusion.1.refs_2_.refs_1_.refs_3_), channel_id=1, source_target_pairs={{0,2},{1,15},{2,4},{3,1},{4,6},{5,3},{6,8},{7,5},{8,10},{9,7},{10,... | collective-permute-start | bytes 1179656 | tf_op jit(solution)/shard_map/ppermute | solution.py:113
  25.8 3.4 %collective-permute-start.2 = (bf16[8,12,16,128]{3,2,1,0:T(8,128)(2,1)S(1)}, bf16[8,12,16,128]{3,2,1,0:T(8,128)(2,1)S(1)}, u32[]{:S(2)}, u32[]{:S(2)}) collective-permute-start(bf16[8,12,16,128]{3,2,1,0:T(8,128)(2,1)S(1)} %pad_maximum_fusion.refs_1_.refs_3_.refs_0_), channel_id=1, source_target_pairs={{2,0},{15,1},{4,2},{1,3},{6,4},{3,5},{8,6},{5,7},{10,8},{7,9},{12,... | collective-permute-start | bytes 1179656 | tf_op jit(solution)/shard_map/ppermute | solution.py:114
  29.2 4.3 %collective-permute-start.6 = (bf16[8,12,16,128]{3,2,1,0:T(8,128)(2,1)S(1)}, bf16[8,12,16,128]{3,2,1,0:T(8,128)(2,1)S(1)}, u32[]{:S(2)}, u32[]{:S(2)}) collective-permute-start(bf16[8,12,16,128]{3,2,1,0:T(8,128)(2,1)S(1)} %collective-permute-done.5.refs_10_), channel_id=1, source_target_pairs={{0,2},{1,15},{2,4},{3,1},{4,6},{5,3},{6,8},{7,5},{8,10},{9,7},{10,... | collective-permute-start | bytes 1179656 | tf_op jit(solution)/shard_map/ppermute | solution.py:113
  33.6 1.9 %collective-permute-start.10 = (bf16[8,12,16,128]{3,2,1,0:T(8,128)(2,1)S(1)}, bf16[8,12,16,128]{3,2,1,0:T(8,128)(2,1)S(1)}, u32[]{:S(2)}, u32[]{:S(2)}) collective-permute-start(bf16[8,12,16,128]{3,2,1,0:T(8,128)(2,1)S(1)} %pad_maximum_fusion.1.refs_2_.refs_1_.refs_3_), channel_id=1, source_target_pairs={{2,0},{15,1},{4,2},{1,3},{6,4},{3,5},{8,6},{5,7},{10,8},{7,9},{12,... | collective-permute-start | bytes 1179656 | tf_op jit(solution)/shard_map/ppermute | solution.py:114
  36.6 4.5 %collective-permute-start.14 = (bf16[8,12,16,128]{3,2,1,0:T(8,128)(2,1)S(1)}, bf16[8,12,16,128]{3,2,1,0:T(8,128)(2,1)S(1)}, u32[]{:S(2)}, u32[]{:S(2)}) collective-permute-start(bf16[8,12,16,128]{3,2,1,0:T(8,128)(2,1)S(1)} %collective-permute-done.13.refs_10_), channel_id=1, source_target_pairs={{0,2},{1,15},{2,4},{3,1},{4,6},{5,3},{6,8},{7,5},{8,10},{9,7},{10,... | collective-permute-start | bytes 1179656 | tf_op jit(solution)/shard_map/ppermute | solution.py:113
  41.2 1.9 %collective-permute-start.3 = (bf16[8,12,16,128]{3,2,1,0:T(8,128)(2,1)S(1)}, bf16[8,12,16,128]{3,2,1,0:T(8,128)(2,1)S(1)}, u32[]{:S(2)}, u32[]{:S(2)}) collective-permute-start(bf16[8,12,16,128]{3,2,1,0:T(8,128)(2,1)S(1)} %collective-permute-done.2.refs_4_), channel_id=1, source_target_pairs={{2,0},{15,1},{4,2},{1,3},{6,4},{3,5},{8,6},{5,7},{10,8},{7,9},{12,... | collective-permute-start | bytes 1179656 | tf_op jit(solution)/shard_map/ppermute | solution.py:114
  44.6 4.6 %collective-permute-start.7 = (bf16[8,12,16,128]{3,2,1,0:T(8,128)(2,1)S(1)}, bf16[8,12,16,128]{3,2,1,0:T(8,128)(2,1)S(1)}, u32[]{:S(2)}, u32[]{:S(2)}) collective-permute-start(bf16[8,12,16,128]{3,2,1,0:T(8,128)(2,1)S(1)} %collective-permute-done.6.refs_9_), channel_id=1, source_target_pairs={{0,2},{1,15},{2,4},{3,1},{4,6},{5,3},{6,8},{7,5},{8,10},{9,7},{10,... | collective-permute-start | bytes 1179656 | tf_op jit(solution)/shard_map/ppermute | solution.py:113
  49.2 1.9 %collective-permute-start.1 = (bf16[8,12,16,128]{3,2,1,0:T(8,128)(2,1)S(1)}, bf16[8,12,16,128]{3,2,1,0:T(8,128)(2,1)S(1)}, u32[]{:S(2)}, u32[]{:S(2)}) collective-permute-start(bf16[8,12,16,128]{3,2,1,0:T(8,128)(2,1)S(1)} %pad_maximum_fusion.refs_1_.refs_3_.refs_0_), channel_id=1, source_target_pairs={{0,1009},{1,16},{2,1011},{3,18},{4,1013},{5,20},{6,1015},{7,22},{8... | collective-permute-start | bytes 1179656 | tf_op jit(solution)/shard_map/ppermute | solution.py:133
  51.1 1.9 %collective-permute-start.11 = (bf16[8,12,16,128]{3,2,1,0:T(8,128)(2,1)S(1)}, bf16[8,12,16,128]{3,2,1,0:T(8,128)(2,1)S(1)}, u32[]{:S(2)}, u32[]{:S(2)}) collective-permute-start(bf16[8,12,16,128]{3,2,1,0:T(8,128)(2,1)S(1)} %collective-permute-done.10.refs_4_), channel_id=1, source_target_pairs={{2,0},{15,1},{4,2},{1,3},{6,4},{3,5},{8,6},{5,7},{10,8},{7,9},{12,... | collective-permute-start | bytes 1179656 | tf_op jit(solution)/shard_map/ppermute | solution.py:114
  53.0 5.6 %collective-permute-start.15 = (bf16[8,12,16,128]{3,2,1,0:T(8,128)(2,1)S(1)}, bf16[8,12,16,128]{3,2,1,0:T(8,128)(2,1)S(1)}, u32[]{:S(2)}, u32[]{:S(2)}) collective-permute-start(bf16[8,12,16,128]{3,2,1,0:T(8,128)(2,1)S(1)} %collective-permute-done.14.refs_9_), channel_id=1, source_target_pairs={{0,2},{1,15},{2,4},{3,1},{4,6},{5,3},{6,8},{7,5},{8,10},{9,7},{10,... | collective-permute-start | bytes 1179656 | tf_op jit(solution)/shard_map/ppermute | solution.py:113
  58.7 1.9 %collective-permute-start.4 = (bf16[8,12,16,128]{3,2,1,0:T(8,128)(2,1)S(1)}, bf16[8,12,16,128]{3,2,1,0:T(8,128)(2,1)S(1)}, u32[]{:S(2)}, u32[]{:S(2)}) collective-permute-start(bf16[8,12,16,128]{3,2,1,0:T(8,128)(2,1)S(1)} %collective-permute-done.3.refs_5_), channel_id=1, source_target_pairs={{2,0},{15,1},{4,2},{1,3},{6,4},{3,5},{8,6},{5,7},{10,8},{7,9},{12,... | collective-permute-start | bytes 1179656 | tf_op jit(solution)/shard_map/ppermute | solution.py:114
  60.6 4.6 %collective-permute-start.8 = (bf16[8,12,16,128]{3,2,1,0:T(8,128)(2,1)S(1)}, bf16[8,12,16,128]{3,2,1,0:T(8,128)(2,1)S(1)}, u32[]{:S(2)}, u32[]{:S(2)}) collective-permute-start(bf16[8,12,16,128]{3,2,1,0:T(8,128)(2,1)S(1)} %collective-permute-done.7.refs_8_), channel_id=1, source_target_pairs={{0,2},{1,15},{2,4},{3,1},{4,6},{5,3},{6,8},{7,5},{8,10},{9,7},{10,... | collective-permute-start | bytes 1179656 | tf_op jit(solution)/shard_map/ppermute | solution.py:115
  65.3 1.9 %collective-permute-start.12 = (bf16[8,12,16,128]{3,2,1,0:T(8,128)(2,1)S(1)}, bf16[8,12,16,128]{3,2,1,0:T(8,128)(2,1)S(1)}, u32[]{:S(2)}, u32[]{:S(2)}) collective-permute-start(bf16[8,12,16,128]{3,2,1,0:T(8,128)(2,1)S(1)} %collective-permute-done.11.refs_5_), channel_id=1, source_target_pairs={{2,0},{15,1},{4,2},{1,3},{6,4},{3,5},{8,6},{5,7},{10,8},{7,9},{12,... | collective-permute-start | bytes 1179656 | tf_op jit(solution)/shard_map/ppermute | solution.py:114
  67.2 4.6 %collective-permute-start.16 = (bf16[8,12,16,128]{3,2,1,0:T(8,128)(2,1)S(1)}, bf16[8,12,16,128]{3,2,1,0:T(8,128)(2,1)S(1)}, u32[]{:S(2)}, u32[]{:S(2)}) collective-permute-start(bf16[8,12,16,128]{3,2,1,0:T(8,128)(2,1)S(1)} %collective-permute-done.15.refs_8_), channel_id=1, source_target_pairs={{0,2},{1,15},{2,4},{3,1},{4,6},{5,3},{6,8},{7,5},{8,10},{9,7},{10,... | collective-permute-start | bytes 1179656 | tf_op jit(solution)/shard_map/ppermute | solution.py:115
  71.8 2.3 %collective-permute-done.8.refs_7_ = bf16[8,12,16,128]{3,2,1,0:T(8,128)(2,1)S(1)} collective-permute-done((bf16[8,12,16,128]{3,2,1,0:T(8,128)(2,1)S(1)}, bf16[8,12,16,128]{3,2,1,0:T(8,128)(2,1)S(1)}, u32[]{:S(2)}, u32[]{:S(2)}) %collective-permute-start.8) | collective-permute-done | bytes 393248 | tf_op jit(solution)/shard_map/ppermute | solution.py:115
  74.2 2.9 %shard_map.37.refs_11_.refs_0_.refs_1_ = bf16[8,12,16,128]{3,2,1,0:T(8,128)(2,1)S(1)} custom-call(s32[4,12,32]{2,1,0:T(8,128)S(1)} %fusion.index_from, bf16[8,12,16,128]{3,2,1,0:T(8,128)(2,1)S(1)} %collective-permute-done.1.refs_0_, bf16[8,12,16,128]{3,2,1,0:T(8,128)(2,1)S(1)} %pad_maximum_fusion.refs_1_.refs_3_.refs_0_, ...), custom_call_target="tpu_custom_call" | custom-call | flops 6039797760 | bytes 3145728 | tf_op jit(solution)/shard_map/pallas_call | solution.py:88
  77.0 8.4 %collective-permute-start.9 = (bf16[8,12,16,128]{3,2,1,0:T(8,128)(2,1)S(1)}, bf16[8,12,16,128]{3,2,1,0:T(8,128)(2,1)S(1)}, u32[]{:S(2)}, u32[]{:S(2)}) collective-permute-start(bf16[8,12,16,128]{3,2,1,0:T(8,128)(2,1)S(1)} %shard_map.37.refs_11_.refs_0_.refs_1_), channel_id=1, source_target_pairs={{0,1009},{1,16},{2,1011},{3,18},{4,1013},{5,20},{6,1015},{7,22},{8... | collective-permute-start | bytes 1179656 | tf_op jit(solution)/shard_map/ppermute | solution.py:133
  85.4 3.1 %shard_map.38 = (bf16[8,12,16,128]{3,2,1,0:T(8,128)(2,1)S(1)}, bf16[7,12,16,128]{3,2,1,0:T(8,128)(2,1)S(1)}) custom-call(s32[4,12,32]{2,1,0:T(8,128)S(1)} %fusion.index_from, bf16[8,12,16,128]{3,2,1,0:T(8,128)(2,1)S(1)} %pad_maximum_fusion.refs_1_.refs_3_.refs_0_, bf16[8,12,16,128]{3,2,1,0:T(8,128)(2,1)S(1)} %pad_maximum_fusion.1.refs_2_.refs_1_.refs_3_, ...), custom_call_target="tpu_custom_call" | custom-call | flops 6039797760 | bytes 3145728 | tf_op jit(solution)/shard_map/pallas_call | solution.py:88
  88.5 4.3 %collective-permute-start.17 = (bf16[7,12,16,128]{3,2,1,0:T(8,128)(2,1)S(1)}, bf16[7,12,16,128]{3,2,1,0:T(8,128)(2,1)S(1)}, u32[]{:S(2)}, u32[]{:S(2)}) collective-permute-start(bf16[7,12,16,128]{3,2,1,0:T(8,128)(2,1)S(1)} %get-tuple-element.16), channel_id=1, source_target_pairs={{0,1},{1,0},{2,3},{3,2},{4,5},{5,4},{6,7},{7,6},{8,9},{9,8},{10,11... | collective-permute-start | bytes 1032200 | tf_op jit(solution)/shard_map/ppermute | solution.py:162
  94.1 2.9 %shard_map.39 = (bf16[8,12,8,128]{3,2,1,0:T(8,128)(2,1)S(1)}, bf16[8,12,8,128]{3,2,1,0:T(8,128)(2,1)S(1)}) custom-call(s32[4,12,32]{2,1,0:T(8,128)S(1)} %fusion.index_from, bf16[8,12,16,128]{3,2,1,0:T(8,128)(2,1)S(1)} %shard_map.37.refs_11_.refs_0_.refs_1_, bf16[8,12,16,128]{3,2,1,0:T(8,128)(2,1)S(1)} %get-tuple-element.15.refs_1_.refs_2_, ...), custom_call_target="tpu_custom_call" | custom-call | flops 6039797 | bytes 3145728 | tf_op jit(solution)/shard_map/pallas_call | solution.py:88
  97.0 3.1 %shard_map.40 = (bf16[16,12,8,128]{3,2,1,0:T(8,128)(2,1)S(1)}, bf16[16,12,8,128]{3,2,1,0:T(8,128)(2,1)S(1)}) custom-call(s32[4,12,32]{2,1,0:T(8,128)S(1)} %fusion.index_from, bf16[8,12,16,128]{3,2,1,0:T(8,128)(2,1)S(1)} %collective-permute-done.9.refs_0_, bf16[8,12,16,128]{3,2,1,0:T(8,128)(2,1)S(1)} %shard_map.37.refs_11_.refs_0_.refs_1_, ...), custom_call_target="tpu_custom_call" | custom-call | flops 6039797760 | bytes 3145728 | tf_op jit(solution)/shard_map/pallas_call | solution.py:88
  100.1 2.3 %collective-permute-start.18 = (bf16[16,12,8,128]{3,2,1,0:T(8,128)(2,1)S(1)}, bf16[16,12,8,128]{3,2,1,0:T(8,128)(2,1)S(1)}, u32[]{:S(2)}, u32[]{:S(2)}) collective-permute-start(bf16[16,12,8,128]{3,2,1,0:T(8,128)(2,1)S(1)} %get-tuple-element.20), channel_id=1, source_target_pairs={{0,1},{1,0},{2,3},{3,2},{4,5},{5,4},{6,7},{7,6},{8,9},{9,8},{10,11... | collective-permute-start | bytes 1179656 | tf_op jit(solution)/shard_map/ppermute | solution.py:167
  (28 shorter events, 9.7 us)
Async XLA Ops:
  0.0 18.2 %collective-permute-start = (bf16[32,12,8,128]{3,2,1,0:T(8,128)(2,1)}, bf16[32,12,8,128]{3,2,1,0:T(8,128)(2,1)S(1)}, u32[]{:S(2)}, u32[]{:S(2)}) collective-permute-start(bf16[32,12,8,128]{3,2,1,0:T(8,128)(2,1)} %param.5), channel_id=1, source_target_pairs={{0,1},{1,0},{2,3},{3,2},{4,5},{5,4},{6,7},{7,6},{8,9},{9,8},{10,11... | collective-permute-start | bytes 2359304 | tf_op jit(solution)/shard_map/ppermute | solution.py:143
  16.1 0.7 copy-start
  19.4 9.8 %collective-permute-start.5 = (bf16[8,12,16,128]{3,2,1,0:T(8,128)(2,1)S(1)}, bf16[8,12,16,128]{3,2,1,0:T(8,128)(2,1)S(1)}, u32[]{:S(2)}, u32[]{:S(2)}) collective-permute-start(bf16[8,12,16,128]{3,2,1,0:T(8,128)(2,1)S(1)} %pad_maximum_fusion.refs_1_.refs_3_.refs_0_), channel_id=1, source_target_pairs={{0,2},{1,15},{2,4},{3,1},{4,6},{5,3},{6,8},{7,5},{8,10},{9,7},{10,... | collective-permute-start | bytes 1179656 | tf_op jit(solution)/shard_map/ppermute | solution.py:113
  23.9 12.7 %collective-permute-start.13 = (bf16[8,12,16,128]{3,2,1,0:T(8,128)(2,1)S(1)}, bf16[8,12,16,128]{3,2,1,0:T(8,128)(2,1)S(1)}, u32[]{:S(2)}, u32[]{:S(2)}) collective-permute-start(bf16[8,12,16,128]{3,2,1,0:T(8,128)(2,1)S(1)} %pad_maximum_fusion.1.refs_2_.refs_1_.refs_3_), channel_id=1, source_target_pairs={{0,2},{1,15},{2,4},{3,1},{4,6},{5,3},{6,8},{7,5},{8,10},{9,7},{10,... | collective-permute-start | bytes 1179656 | tf_op jit(solution)/shard_map/ppermute | solution.py:113
  25.8 15.3 %collective-permute-start.2 = (bf16[8,12,16,128]{3,2,1,0:T(8,128)(2,1)S(1)}, bf16[8,12,16,128]{3,2,1,0:T(8,128)(2,1)S(1)}, u32[]{:S(2)}, u32[]{:S(2)}) collective-permute-start(bf16[8,12,16,128]{3,2,1,0:T(8,128)(2,1)S(1)} %pad_maximum_fusion.refs_1_.refs_3_.refs_0_), channel_id=1, source_target_pairs={{2,0},{15,1},{4,2},{1,3},{6,4},{3,5},{8,6},{5,7},{10,8},{7,9},{12,... | collective-permute-start | bytes 1179656 | tf_op jit(solution)/shard_map/ppermute | solution.py:114
  29.2 15.3 %collective-permute-start.6 = (bf16[8,12,16,128]{3,2,1,0:T(8,128)(2,1)S(1)}, bf16[8,12,16,128]{3,2,1,0:T(8,128)(2,1)S(1)}, u32[]{:S(2)}, u32[]{:S(2)}) collective-permute-start(bf16[8,12,16,128]{3,2,1,0:T(8,128)(2,1)S(1)} %collective-permute-done.5.refs_10_), channel_id=1, source_target_pairs={{0,2},{1,15},{2,4},{3,1},{4,6},{5,3},{6,8},{7,5},{8,10},{9,7},{10,... | collective-permute-start | bytes 1179656 | tf_op jit(solution)/shard_map/ppermute | solution.py:113
  33.6 17.5 %collective-permute-start.10 = (bf16[8,12,16,128]{3,2,1,0:T(8,128)(2,1)S(1)}, bf16[8,12,16,128]{3,2,1,0:T(8,128)(2,1)S(1)}, u32[]{:S(2)}, u32[]{:S(2)}) collective-permute-start(bf16[8,12,16,128]{3,2,1,0:T(8,128)(2,1)S(1)} %pad_maximum_fusion.1.refs_2_.refs_1_.refs_3_), channel_id=1, source_target_pairs={{2,0},{15,1},{4,2},{1,3},{6,4},{3,5},{8,6},{5,7},{10,8},{7,9},{12,... | collective-permute-start | bytes 1179656 | tf_op jit(solution)/shard_map/ppermute | solution.py:114
  36.6 16.4 %collective-permute-start.14 = (bf16[8,12,16,128]{3,2,1,0:T(8,128)(2,1)S(1)}, bf16[8,12,16,128]{3,2,1,0:T(8,128)(2,1)S(1)}, u32[]{:S(2)}, u32[]{:S(2)}) collective-permute-start(bf16[8,12,16,128]{3,2,1,0:T(8,128)(2,1)S(1)} %collective-permute-done.13.refs_10_), channel_id=1, source_target_pairs={{0,2},{1,15},{2,4},{3,1},{4,6},{5,3},{6,8},{7,5},{8,10},{9,7},{10,... | collective-permute-start | bytes 1179656 | tf_op jit(solution)/shard_map/ppermute | solution.py:113
  41.2 17.5 %collective-permute-start.3 = (bf16[8,12,16,128]{3,2,1,0:T(8,128)(2,1)S(1)}, bf16[8,12,16,128]{3,2,1,0:T(8,128)(2,1)S(1)}, u32[]{:S(2)}, u32[]{:S(2)}) collective-permute-start(bf16[8,12,16,128]{3,2,1,0:T(8,128)(2,1)S(1)} %collective-permute-done.2.refs_4_), channel_id=1, source_target_pairs={{2,0},{15,1},{4,2},{1,3},{6,4},{3,5},{8,6},{5,7},{10,8},{7,9},{12,... | collective-permute-start | bytes 1179656 | tf_op jit(solution)/shard_map/ppermute | solution.py:114
  44.6 16.0 %collective-permute-start.7 = (bf16[8,12,16,128]{3,2,1,0:T(8,128)(2,1)S(1)}, bf16[8,12,16,128]{3,2,1,0:T(8,128)(2,1)S(1)}, u32[]{:S(2)}, u32[]{:S(2)}) collective-permute-start(bf16[8,12,16,128]{3,2,1,0:T(8,128)(2,1)S(1)} %collective-permute-done.6.refs_9_), channel_id=1, source_target_pairs={{0,2},{1,15},{2,4},{3,1},{4,6},{5,3},{6,8},{7,5},{8,10},{9,7},{10,... | collective-permute-start | bytes 1179656 | tf_op jit(solution)/shard_map/ppermute | solution.py:113
  49.2 22.6 %collective-permute-start.1 = (bf16[8,12,16,128]{3,2,1,0:T(8,128)(2,1)S(1)}, bf16[8,12,16,128]{3,2,1,0:T(8,128)(2,1)S(1)}, u32[]{:S(2)}, u32[]{:S(2)}) collective-permute-start(bf16[8,12,16,128]{3,2,1,0:T(8,128)(2,1)S(1)} %pad_maximum_fusion.refs_1_.refs_3_.refs_0_), channel_id=1, source_target_pairs={{0,1009},{1,16},{2,1011},{3,18},{4,1013},{5,20},{6,1015},{7,22},{8... | collective-permute-start | bytes 1179656 | tf_op jit(solution)/shard_map/ppermute | solution.py:133
  51.1 14.2 %collective-permute-start.11 = (bf16[8,12,16,128]{3,2,1,0:T(8,128)(2,1)S(1)}, bf16[8,12,16,128]{3,2,1,0:T(8,128)(2,1)S(1)}, u32[]{:S(2)}, u32[]{:S(2)}) collective-permute-start(bf16[8,12,16,128]{3,2,1,0:T(8,128)(2,1)S(1)} %collective-permute-done.10.refs_4_), channel_id=1, source_target_pairs={{2,0},{15,1},{4,2},{1,3},{6,4},{3,5},{8,6},{5,7},{10,8},{7,9},{12,... | collective-permute-start | bytes 1179656 | tf_op jit(solution)/shard_map/ppermute | solution.py:114
  53.0 14.2 %collective-permute-start.15 = (bf16[8,12,16,128]{3,2,1,0:T(8,128)(2,1)S(1)}, bf16[8,12,16,128]{3,2,1,0:T(8,128)(2,1)S(1)}, u32[]{:S(2)}, u32[]{:S(2)}) collective-permute-start(bf16[8,12,16,128]{3,2,1,0:T(8,128)(2,1)S(1)} %collective-permute-done.14.refs_9_), channel_id=1, source_target_pairs={{0,2},{1,15},{2,4},{3,1},{4,6},{5,3},{6,8},{7,5},{8,10},{9,7},{10,... | collective-permute-start | bytes 1179656 | tf_op jit(solution)/shard_map/ppermute | solution.py:113
  58.7 13.1 %collective-permute-start.4 = (bf16[8,12,16,128]{3,2,1,0:T(8,128)(2,1)S(1)}, bf16[8,12,16,128]{3,2,1,0:T(8,128)(2,1)S(1)}, u32[]{:S(2)}, u32[]{:S(2)}) collective-permute-start(bf16[8,12,16,128]{3,2,1,0:T(8,128)(2,1)S(1)} %collective-permute-done.3.refs_5_), channel_id=1, source_target_pairs={{2,0},{15,1},{4,2},{1,3},{6,4},{3,5},{8,6},{5,7},{10,8},{7,9},{12,... | collective-permute-start | bytes 1179656 | tf_op jit(solution)/shard_map/ppermute | solution.py:114
  60.6 13.6 %collective-permute-start.8 = (bf16[8,12,16,128]{3,2,1,0:T(8,128)(2,1)S(1)}, bf16[8,12,16,128]{3,2,1,0:T(8,128)(2,1)S(1)}, u32[]{:S(2)}, u32[]{:S(2)}) collective-permute-start(bf16[8,12,16,128]{3,2,1,0:T(8,128)(2,1)S(1)} %collective-permute-done.7.refs_8_), channel_id=1, source_target_pairs={{0,2},{1,15},{2,4},{3,1},{4,6},{5,3},{6,8},{7,5},{8,10},{9,7},{10,... | collective-permute-start | bytes 1179656 | tf_op jit(solution)/shard_map/ppermute | solution.py:115
  65.3 20.1 %collective-permute-start.12 = (bf16[8,12,16,128]{3,2,1,0:T(8,128)(2,1)S(1)}, bf16[8,12,16,128]{3,2,1,0:T(8,128)(2,1)S(1)}, u32[]{:S(2)}, u32[]{:S(2)}) collective-permute-start(bf16[8,12,16,128]{3,2,1,0:T(8,128)(2,1)S(1)} %collective-permute-done.11.refs_5_), channel_id=1, source_target_pairs={{2,0},{15,1},{4,2},{1,3},{6,4},{3,5},{8,6},{5,7},{10,8},{7,9},{12,... | collective-permute-start | bytes 1179656 | tf_op jit(solution)/shard_map/ppermute | solution.py:114
  67.2 18.2 %collective-permute-start.16 = (bf16[8,12,16,128]{3,2,1,0:T(8,128)(2,1)S(1)}, bf16[8,12,16,128]{3,2,1,0:T(8,128)(2,1)S(1)}, u32[]{:S(2)}, u32[]{:S(2)}) collective-permute-start(bf16[8,12,16,128]{3,2,1,0:T(8,128)(2,1)S(1)} %collective-permute-done.15.refs_8_), channel_id=1, source_target_pairs={{0,2},{1,15},{2,4},{3,1},{4,6},{5,3},{6,8},{7,5},{8,10},{9,7},{10,... | collective-permute-start | bytes 1179656 | tf_op jit(solution)/shard_map/ppermute | solution.py:115
  77.0 19.9 %collective-permute-start.9 = (bf16[8,12,16,128]{3,2,1,0:T(8,128)(2,1)S(1)}, bf16[8,12,16,128]{3,2,1,0:T(8,128)(2,1)S(1)}, u32[]{:S(2)}, u32[]{:S(2)}) collective-permute-start(bf16[8,12,16,128]{3,2,1,0:T(8,128)(2,1)S(1)} %shard_map.37.refs_11_.refs_0_.refs_1_), channel_id=1, source_target_pairs={{0,1009},{1,16},{2,1011},{3,18},{4,1013},{5,20},{6,1015},{7,22},{8... | collective-permute-start | bytes 1179656 | tf_op jit(solution)/shard_map/ppermute | solution.py:133
  88.5 5.5 %collective-permute-start.17 = (bf16[7,12,16,128]{3,2,1,0:T(8,128)(2,1)S(1)}, bf16[7,12,16,128]{3,2,1,0:T(8,128)(2,1)S(1)}, u32[]{:S(2)}, u32[]{:S(2)}) collective-permute-start(bf16[7,12,16,128]{3,2,1,0:T(8,128)(2,1)S(1)} %get-tuple-element.16), channel_id=1, source_target_pairs={{0,1},{1,0},{2,3},{3,2},{4,5},{5,4},{6,7},{7,6},{8,9},{9,8},{10,11... | collective-permute-start | bytes 1032200 | tf_op jit(solution)/shard_map/ppermute | solution.py:162
  100.1 3.6 %collective-permute-start.18 = (bf16[16,12,8,128]{3,2,1,0:T(8,128)(2,1)S(1)}, bf16[16,12,8,128]{3,2,1,0:T(8,128)(2,1)S(1)}, u32[]{:S(2)}, u32[]{:S(2)}) collective-permute-start(bf16[16,12,8,128]{3,2,1,0:T(8,128)(2,1)S(1)} %get-tuple-element.20), channel_id=1, source_target_pairs={{0,1},{1,0},{2,3},{3,2},{4,5},{5,4},{6,7},{7,6},{8,9},{9,8},{10,11... | collective-permute-start | bytes 1179656 | tf_op jit(solution)/shard_map/ppermute | solution.py:167

commit v6 on v5

--- a/solution.py
+++ b/solution.py
@@ -47,8 +47,9 @@
             for u in range(t, t + 6):
                 tiles = []
                 for s in range(slots):
-                    word = index_ref[u % 4, s, first_row + i]
-                    tiles.append(tile_at[lax.shift_right_logical(word, 10 * (u // 4)) & 1023])
+                    word = index_ref[s, 4 * rows * (u % 4) + first_row + i]
+                    place = (word & 1023, lax.shift_right_logical(word, 10) & 1023, lax.shift_right_logical(word, 20))[u // 4]
+                    tiles.append(tile_at[place])
                 columns.append(jnp.concatenate(tiles, axis=0))
                 blocks += [piece[i, u] for piece in pieces]
             picked = jnp.concatenate(columns, axis=1)
@@ -139,6 +140,7 @@
     place = (part * 8 + away % 8) * 16
     index = jnp.where(fetch >= 0, place[:, :, None] + fetch, 32 * 16).transpose(1, 2, 0)
     index = index[:4] + index[4:8] * 1024 + index[8:] * 1024**2
+    index = jnp.concatenate([index[k] for k in range(4)], axis=1)
 
     other = lax.ppermute(values, "cols", swap)
     other, index = lax.optimization_barrier((other, index))

time: 105 us -> 104 us (level)
  Pallas kernels: 11.9 us -> 9.9 us
    pallas_call x4, Pallas kernels: 11.9 us -> 9.9 us  [product(): pl.pallas_call(functools.partial(product_kernel, first_block, is_first, s...]
  transfers between devices with their start and end apart: 19 -> 19, of which waited for: 6 -> 6; matrix products, arithmetic and copies ran while one was open for 1% -> 1% of each run, Pallas kernels for 8% -> 7%
where the time goes in v6:
time: 104 us; the launch traced here: 103 us
  starting transfers between devices  81 us (78%)
  Pallas kernels  9.9 us (10%)
  waiting for transfers between devices  7.91 us (8%)
  other arithmetic  3.43 us (3%)
    ppermute x6, starting transfers between devices, gather_ring(): gone[k].append(lax.ppermute(gone[k][-1], 'cols', ahead))  25.4 us
    ppermute x1, starting transfers between devices, local(): other = lax.ppermute(values, 'cols', swap)  16.1 us
    ppermute x6, starting transfers between devices, gather_ring(): come[k].append(lax.ppermute(come[k][-1], 'cols', back))  13 us
    ppermute x2, starting transfers between devices, outward(): return lax.ppermute(piece, ('rows', 'cols'), pairs)  10.3 us
    pallas_call x4, Pallas kernels, product(): pl.pallas_call(functools.partial(product_kernel, first_block, is_first, s...  9.9 us
    ppermute x2, starting transfers between devices, gather_ring(): lax.ppermute(gone[k][-1], 'cols', ahead)  9.15 us
    ppermute x1, starting transfers between devices, local(): shifted_beyond = lax.ppermute(inner_edge, 'cols', swap)  4.27 us
    ppermute x1, starting transfers between devices, local(): got = lax.ppermute(send, 'cols', swap)  2.99 us
  transfers between devices with their start and end apart: 19, of which 6 were waited for; matrix products, arithmetic and copies ran while one was open for 1% of the time, Pallas kernels for 7%

profile of v6, /device:TPU:1, one launch (start us, length us, event | category | flops | bytes accessed | tf_op | source)
XLA Modules:
  0.0 103.3 jit_solution(2845008894912574701)
XLA Ops:
  0.0 16.1 %collective-permute-start = (bf16[32,12,8,128]{3,2,1,0:T(8,128)(2,1)}, bf16[32,12,8,128]{3,2,1,0:T(8,128)(2,1)S(1)}, u32[]{:S(2)}, u32[]{:S(2)}) collective-permute-start(bf16[32,12,8,128]{3,2,1,0:T(8,128)(2,1)} %param.5), channel_id=1, source_target_pairs={{0,1},{1,0},{2,3},{3,2},{4,5},{5,4},{6,7},{7,6},{8,9},{9,8},{10,11... | collective-permute-start | bytes 2359304 | tf_op jit(solution)/shard_map/ppermute | solution.py:145
  19.4 4.4 %collective-permute-start.5 = (bf16[8,12,16,128]{3,2,1,0:T(8,128)(2,1)S(1)}, bf16[8,12,16,128]{3,2,1,0:T(8,128)(2,1)S(1)}, u32[]{:S(2)}, u32[]{:S(2)}) collective-permute-start(bf16[8,12,16,128]{3,2,1,0:T(8,128)(2,1)S(1)} %pad_maximum_fusion.refs_1_.refs_3_.refs_0_), channel_id=1, source_target_pairs={{0,2},{1,15},{2,4},{3,1},{4,6},{5,3},{6,8},{7,5},{8,10},{9,7},{10,... | collective-permute-start | bytes 1179656 | tf_op jit(solution)/shard_map/ppermute | solution.py:114
  23.9 1.9 %collective-permute-start.13 = (bf16[8,12,16,128]{3,2,1,0:T(8,128)(2,1)S(1)}, bf16[8,12,16,128]{3,2,1,0:T(8,128)(2,1)S(1)}, u32[]{:S(2)}, u32[]{:S(2)}) collective-permute-start(bf16[8,12,16,128]{3,2,1,0:T(8,128)(2,1)S(1)} %pad_maximum_fusion.1.refs_2_.refs_1_.refs_3_), channel_id=1, source_target_pairs={{0,2},{1,15},{2,4},{3,1},{4,6},{5,3},{6,8},{7,5},{8,10},{9,7},{10,... | collective-permute-start | bytes 1179656 | tf_op jit(solution)/shard_map/ppermute | solution.py:114
  25.8 3.4 %collective-permute-start.2 = (bf16[8,12,16,128]{3,2,1,0:T(8,128)(2,1)S(1)}, bf16[8,12,16,128]{3,2,1,0:T(8,128)(2,1)S(1)}, u32[]{:S(2)}, u32[]{:S(2)}) collective-permute-start(bf16[8,12,16,128]{3,2,1,0:T(8,128)(2,1)S(1)} %pad_maximum_fusion.refs_1_.refs_3_.refs_0_), channel_id=1, source_target_pairs={{2,0},{15,1},{4,2},{1,3},{6,4},{3,5},{8,6},{5,7},{10,8},{7,9},{12,... | collective-permute-start | bytes 1179656 | tf_op jit(solution)/shard_map/ppermute | solution.py:115
  29.2 4.3 %collective-permute-start.6 = (bf16[8,12,16,128]{3,2,1,0:T(8,128)(2,1)S(1)}, bf16[8,12,16,128]{3,2,1,0:T(8,128)(2,1)S(1)}, u32[]{:S(2)}, u32[]{:S(2)}) collective-permute-start(bf16[8,12,16,128]{3,2,1,0:T(8,128)(2,1)S(1)} %collective-permute-done.5.refs_10_), channel_id=1, source_target_pairs={{0,2},{1,15},{2,4},{3,1},{4,6},{5,3},{6,8},{7,5},{8,10},{9,7},{10,... | collective-permute-start | bytes 1179656 | tf_op jit(solution)/shard_map/ppermute | solution.py:114
  33.6 1.9 %collective-permute-start.10 = (bf16[8,12,16,128]{3,2,1,0:T(8,128)(2,1)S(1)}, bf16[8,12,16,128]{3,2,1,0:T(8,128)(2,1)S(1)}, u32[]{:S(2)}, u32[]{:S(2)}) collective-permute-start(bf16[8,12,16,128]{3,2,1,0:T(8,128)(2,1)S(1)} %pad_maximum_fusion.1.refs_2_.refs_1_.refs_3_), channel_id=1, source_target_pairs={{2,0},{15,1},{4,2},{1,3},{6,4},{3,5},{8,6},{5,7},{10,8},{7,9},{12,... | collective-permute-start | bytes 1179656 | tf_op jit(solution)/shard_map/ppermute | solution.py:115
  36.6 4.5 %collective-permute-start.14 = (bf16[8,12,16,128]{3,2,1,0:T(8,128)(2,1)S(1)}, bf16[8,12,16,128]{3,2,1,0:T(8,128)(2,1)S(1)}, u32[]{:S(2)}, u32[]{:S(2)}) collective-permute-start(bf16[8,12,16,128]{3,2,1,0:T(8,128)(2,1)S(1)} %collective-permute-done.13.refs_10_), channel_id=1, source_target_pairs={{0,2},{1,15},{2,4},{3,1},{4,6},{5,3},{6,8},{7,5},{8,10},{9,7},{10,... | collective-permute-start | bytes 1179656 | tf_op jit(solution)/shard_map/ppermute | solution.py:114
  41.2 1.9 %collective-permute-start.3 = (bf16[8,12,16,128]{3,2,1,0:T(8,128)(2,1)S(1)}, bf16[8,12,16,128]{3,2,1,0:T(8,128)(2,1)S(1)}, u32[]{:S(2)}, u32[]{:S(2)}) collective-permute-start(bf16[8,12,16,128]{3,2,1,0:T(8,128)(2,1)S(1)} %collective-permute-done.2.refs_4_), channel_id=1, source_target_pairs={{2,0},{15,1},{4,2},{1,3},{6,4},{3,5},{8,6},{5,7},{10,8},{7,9},{12,... | collective-permute-start | bytes 1179656 | tf_op jit(solution)/shard_map/ppermute | solution.py:115
  44.6 4.6 %collective-permute-start.7 = (bf16[8,12,16,128]{3,2,1,0:T(8,128)(2,1)S(1)}, bf16[8,12,16,128]{3,2,1,0:T(8,128)(2,1)S(1)}, u32[]{:S(2)}, u32[]{:S(2)}) collective-permute-start(bf16[8,12,16,128]{3,2,1,0:T(8,128)(2,1)S(1)} %collective-permute-done.6.refs_9_), channel_id=1, source_target_pairs={{0,2},{1,15},{2,4},{3,1},{4,6},{5,3},{6,8},{7,5},{8,10},{9,7},{10,... | collective-permute-start | bytes 1179656 | tf_op jit(solution)/shard_map/ppermute | solution.py:114
  49.2 1.9 %collective-permute-start.1 = (bf16[8,12,16,128]{3,2,1,0:T(8,128)(2,1)S(1)}, bf16[8,12,16,128]{3,2,1,0:T(8,128)(2,1)S(1)}, u32[]{:S(2)}, u32[]{:S(2)}) collective-permute-start(bf16[8,12,16,128]{3,2,1,0:T(8,128)(2,1)S(1)} %pad_maximum_fusion.refs_1_.refs_3_.refs_0_), channel_id=1, source_target_pairs={{0,1009},{1,16},{2,1011},{3,18},{4,1013},{5,20},{6,1015},{7,22},{8... | collective-permute-start | bytes 1179656 | tf_op jit(solution)/shard_map/ppermute | solution.py:134
  51.1 1.9 %collective-permute-start.11 = (bf16[8,12,16,128]{3,2,1,0:T(8,128)(2,1)S(1)}, bf16[8,12,16,128]{3,2,1,0:T(8,128)(2,1)S(1)}, u32[]{:S(2)}, u32[]{:S(2)}) collective-permute-start(bf16[8,12,16,128]{3,2,1,0:T(8,128)(2,1)S(1)} %collective-permute-done.10.refs_4_), channel_id=1, source_target_pairs={{2,0},{15,1},{4,2},{1,3},{6,4},{3,5},{8,6},{5,7},{10,8},{7,9},{12,... | collective-permute-start | bytes 1179656 | tf_op jit(solution)/shard_map/ppermute | solution.py:115
  53.0 5.6 %collective-permute-start.15 = (bf16[8,12,16,128]{3,2,1,0:T(8,128)(2,1)S(1)}, bf16[8,12,16,128]{3,2,1,0:T(8,128)(2,1)S(1)}, u32[]{:S(2)}, u32[]{:S(2)}) collective-permute-start(bf16[8,12,16,128]{3,2,1,0:T(8,128)(2,1)S(1)} %collective-permute-done.14.refs_9_), channel_id=1, source_target_pairs={{0,2},{1,15},{2,4},{3,1},{4,6},{5,3},{6,8},{7,5},{8,10},{9,7},{10,... | collective-permute-start | bytes 1179656 | tf_op jit(solution)/shard_map/ppermute | solution.py:114
  58.7 1.9 %collective-permute-start.4 = (bf16[8,12,16,128]{3,2,1,0:T(8,128)(2,1)S(1)}, bf16[8,12,16,128]{3,2,1,0:T(8,128)(2,1)S(1)}, u32[]{:S(2)}, u32[]{:S(2)}) collective-permute-start(bf16[8,12,16,128]{3,2,1,0:T(8,128)(2,1)S(1)} %collective-permute-done.3.refs_5_), channel_id=1, source_target_pairs={{2,0},{15,1},{4,2},{1,3},{6,4},{3,5},{8,6},{5,7},{10,8},{7,9},{12,... | collective-permute-start | bytes 1179656 | tf_op jit(solution)/shard_map/ppermute | solution.py:115
  60.6 4.6 %collective-permute-start.8 = (bf16[8,12,16,128]{3,2,1,0:T(8,128)(2,1)S(1)}, bf16[8,12,16,128]{3,2,1,0:T(8,128)(2,1)S(1)}, u32[]{:S(2)}, u32[]{:S(2)}) collective-permute-start(bf16[8,12,16,128]{3,2,1,0:T(8,128)(2,1)S(1)} %collective-permute-done.7.refs_8_), channel_id=1, source_target_pairs={{0,2},{1,15},{2,4},{3,1},{4,6},{5,3},{6,8},{7,5},{8,10},{9,7},{10,... | collective-permute-start | bytes 1179656 | tf_op jit(solution)/shard_map/ppermute | solution.py:116
  65.3 1.9 %collective-permute-start.12 = (bf16[8,12,16,128]{3,2,1,0:T(8,128)(2,1)S(1)}, bf16[8,12,16,128]{3,2,1,0:T(8,128)(2,1)S(1)}, u32[]{:S(2)}, u32[]{:S(2)}) collective-permute-start(bf16[8,12,16,128]{3,2,1,0:T(8,128)(2,1)S(1)} %collective-permute-done.11.refs_5_), channel_id=1, source_target_pairs={{2,0},{15,1},{4,2},{1,3},{6,4},{3,5},{8,6},{5,7},{10,8},{7,9},{12,... | collective-permute-start | bytes 1179656 | tf_op jit(solution)/shard_map/ppermute | solution.py:115
  67.2 4.6 %collective-permute-start.16 = (bf16[8,12,16,128]{3,2,1,0:T(8,128)(2,1)S(1)}, bf16[8,12,16,128]{3,2,1,0:T(8,128)(2,1)S(1)}, u32[]{:S(2)}, u32[]{:S(2)}) collective-permute-start(bf16[8,12,16,128]{3,2,1,0:T(8,128)(2,1)S(1)} %collective-permute-done.15.refs_8_), channel_id=1, source_target_pairs={{0,2},{1,15},{2,4},{3,1},{4,6},{5,3},{6,8},{7,5},{8,10},{9,7},{10,... | collective-permute-start | bytes 1179656 | tf_op jit(solution)/shard_map/ppermute | solution.py:116
  71.8 2.3 %collective-permute-done.8.refs_7_ = bf16[8,12,16,128]{3,2,1,0:T(8,128)(2,1)S(1)} collective-permute-done((bf16[8,12,16,128]{3,2,1,0:T(8,128)(2,1)S(1)}, bf16[8,12,16,128]{3,2,1,0:T(8,128)(2,1)S(1)}, u32[]{:S(2)}, u32[]{:S(2)}) %collective-permute-start.8) | collective-permute-done | bytes 393248 | tf_op jit(solution)/shard_map/ppermute | solution.py:116
  74.2 2.5 %shard_map.37.refs_11_.refs_0_.refs_1_ = bf16[8,12,16,128]{3,2,1,0:T(8,128)(2,1)S(1)} custom-call(s32[12,128]{1,0:T(8,128)S(1)} %pad_add_fusion.index_from, bf16[8,12,16,128]{3,2,1,0:T(8,128)(2,1)S(1)} %collective-permute-done.1.refs_0_, bf16[8,12,16,128]{3,2,1,0:T(8,128)(2,1)S(1)} %pad_maximum_fusion.refs_1_.refs_3_.refs_0_, ...), custom_call_target="tpu_custom_call" | custom-call | flops 6039797760 | bytes 3145728 | tf_op jit(solution)/shard_map/pallas_call | solution.py:89
  76.6 8.3 %collective-permute-start.9 = (bf16[8,12,16,128]{3,2,1,0:T(8,128)(2,1)S(1)}, bf16[8,12,16,128]{3,2,1,0:T(8,128)(2,1)S(1)}, u32[]{:S(2)}, u32[]{:S(2)}) collective-permute-start(bf16[8,12,16,128]{3,2,1,0:T(8,128)(2,1)S(1)} %shard_map.37.refs_11_.refs_0_.refs_1_), channel_id=1, source_target_pairs={{0,1009},{1,16},{2,1011},{3,18},{4,1013},{5,20},{6,1015},{7,22},{8... | collective-permute-start | bytes 1179656 | tf_op jit(solution)/shard_map/ppermute | solution.py:134
  85.0 2.5 %shard_map.38 = (bf16[8,12,16,128]{3,2,1,0:T(8,128)(2,1)S(1)}, bf16[7,12,16,128]{3,2,1,0:T(8,128)(2,1)S(1)}) custom-call(s32[12,128]{1,0:T(8,128)S(1)} %pad_add_fusion.index_from, bf16[8,12,16,128]{3,2,1,0:T(8,128)(2,1)S(1)} %pad_maximum_fusion.refs_1_.refs_3_.refs_0_, bf16[8,12,16,128]{3,2,1,0:T(8,128)(2,1)S(1)} %pad_maximum_fusion.1.refs_2_.refs_1_.refs_3_, ...), custom_call_target="tpu_custom_call" | custom-call | flops 6039797760 | bytes 3145728 | tf_op jit(solution)/shard_map/pallas_call | solution.py:89
  87.5 4.3 %collective-permute-start.17 = (bf16[7,12,16,128]{3,2,1,0:T(8,128)(2,1)S(1)}, bf16[7,12,16,128]{3,2,1,0:T(8,128)(2,1)S(1)}, u32[]{:S(2)}, u32[]{:S(2)}) collective-permute-start(bf16[7,12,16,128]{3,2,1,0:T(8,128)(2,1)S(1)} %get-tuple-element.16), channel_id=1, source_target_pairs={{0,1},{1,0},{2,3},{3,2},{4,5},{5,4},{6,7},{7,6},{8,9},{9,8},{10,11... | collective-permute-start | bytes 1032200 | tf_op jit(solution)/shard_map/ppermute | solution.py:164
  93.0 2.5 %shard_map.39 = (bf16[8,12,8,128]{3,2,1,0:T(8,128)(2,1)S(1)}, bf16[8,12,8,128]{3,2,1,0:T(8,128)(2,1)S(1)}) custom-call(s32[12,128]{1,0:T(8,128)S(1)} %pad_add_fusion.index_from, bf16[8,12,16,128]{3,2,1,0:T(8,128)(2,1)S(1)} %shard_map.37.refs_11_.refs_0_.refs_1_, bf16[8,12,16,128]{3,2,1,0:T(8,128)(2,1)S(1)} %get-tuple-element.15.refs_1_.refs_2_, ...), custom_call_target="tpu_custom_call" | custom-call | flops 6039797 | bytes 3145728 | tf_op jit(solution)/shard_map/pallas_call | solution.py:89
  95.5 2.5 %shard_map.40 = (bf16[16,12,8,128]{3,2,1,0:T(8,128)(2,1)S(1)}, bf16[16,12,8,128]{3,2,1,0:T(8,128)(2,1)S(1)}) custom-call(s32[12,128]{1,0:T(8,128)S(1)} %pad_add_fusion.index_from, bf16[8,12,16,128]{3,2,1,0:T(8,128)(2,1)S(1)} %collective-permute-done.9.refs_0_, bf16[8,12,16,128]{3,2,1,0:T(8,128)(2,1)S(1)} %shard_map.37.refs_11_.refs_0_.refs_1_, ...), custom_call_target="tpu_custom_call" | custom-call | flops 6039797760 | bytes 3145728 | tf_op jit(solution)/shard_map/pallas_call | solution.py:89
  98.0 3.0 %collective-permute-start.18 = (bf16[16,12,8,128]{3,2,1,0:T(8,128)(2,1)S(1)}, bf16[16,12,8,128]{3,2,1,0:T(8,128)(2,1)S(1)}, u32[]{:S(2)}, u32[]{:S(2)}) collective-permute-start(bf16[16,12,8,128]{3,2,1,0:T(8,128)(2,1)S(1)} %get-tuple-element.20), channel_id=1, source_target_pairs={{0,1},{1,0},{2,3},{3,2},{4,5},{5,4},{6,7},{7,6},{8,9},{9,8},{10,11... | collective-permute-start | bytes 1179656 | tf_op jit(solution)/shard_map/ppermute | solution.py:169
  (30 shorter events, 9.7 us)
Async XLA Ops:
  0.0 18.2 %collective-permute-start = (bf16[32,12,8,128]{3,2,1,0:T(8,128)(2,1)}, bf16[32,12,8,128]{3,2,1,0:T(8,128)(2,1)S(1)}, u32[]{:S(2)}, u32[]{:S(2)}) collective-permute-start(bf16[32,12,8,128]{3,2,1,0:T(8,128)(2,1)} %param.5), channel_id=1, source_target_pairs={{0,1},{1,0},{2,3},{3,2},{4,5},{5,4},{6,7},{7,6},{8,9},{9,8},{10,11... | collective-permute-start | bytes 2359304 | tf_op jit(solution)/shard_map/ppermute | solution.py:145
  16.1 0.7 copy-start
  19.4 9.8 %collective-permute-start.5 = (bf16[8,12,16,128]{3,2,1,0:T(8,128)(2,1)S(1)}, bf16[8,12,16,128]{3,2,1,0:T(8,128)(2,1)S(1)}, u32[]{:S(2)}, u32[]{:S(2)}) collective-permute-start(bf16[8,12,16,128]{3,2,1,0:T(8,128)(2,1)S(1)} %pad_maximum_fusion.refs_1_.refs_3_.refs_0_), channel_id=1, source_target_pairs={{0,2},{1,15},{2,4},{3,1},{4,6},{5,3},{6,8},{7,5},{8,10},{9,7},{10,... | collective-permute-start | bytes 1179656 | tf_op jit(solution)/shard_map/ppermute | solution.py:114
  23.9 12.7 %collective-permute-start.13 = (bf16[8,12,16,128]{3,2,1,0:T(8,128)(2,1)S(1)}, bf16[8,12,16,128]{3,2,1,0:T(8,128)(2,1)S(1)}, u32[]{:S(2)}, u32[]{:S(2)}) collective-permute-start(bf16[8,12,16,128]{3,2,1,0:T(8,128)(2,1)S(1)} %pad_maximum_fusion.1.refs_2_.refs_1_.refs_3_), channel_id=1, source_target_pairs={{0,2},{1,15},{2,4},{3,1},{4,6},{5,3},{6,8},{7,5},{8,10},{9,7},{10,... | collective-permute-start | bytes 1179656 | tf_op jit(solution)/shard_map/ppermute | solution.py:114
  25.8 15.3 %collective-permute-start.2 = (bf16[8,12,16,128]{3,2,1,0:T(8,128)(2,1)S(1)}, bf16[8,12,16,128]{3,2,1,0:T(8,128)(2,1)S(1)}, u32[]{:S(2)}, u32[]{:S(2)}) collective-permute-start(bf16[8,12,16,128]{3,2,1,0:T(8,128)(2,1)S(1)} %pad_maximum_fusion.refs_1_.refs_3_.refs_0_), channel_id=1, source_target_pairs={{2,0},{15,1},{4,2},{1,3},{6,4},{3,5},{8,6},{5,7},{10,8},{7,9},{12,... | collective-permute-start | bytes 1179656 | tf_op jit(solution)/shard_map/ppermute | solution.py:115
  29.2 15.3 %collective-permute-start.6 = (bf16[8,12,16,128]{3,2,1,0:T(8,128)(2,1)S(1)}, bf16[8,12,16,128]{3,2,1,0:T(8,128)(2,1)S(1)}, u32[]{:S(2)}, u32[]{:S(2)}) collective-permute-start(bf16[8,12,16,128]{3,2,1,0:T(8,128)(2,1)S(1)} %collective-permute-done.5.refs_10_), channel_id=1, source_target_pairs={{0,2},{1,15},{2,4},{3,1},{4,6},{5,3},{6,8},{7,5},{8,10},{9,7},{10,... | collective-permute-start | bytes 1179656 | tf_op jit(solution)/shard_map/ppermute | solution.py:114
  33.6 17.5 %collective-permute-start.10 = (bf16[8,12,16,128]{3,2,1,0:T(8,128)(2,1)S(1)}, bf16[8,12,16,128]{3,2,1,0:T(8,128)(2,1)S(1)}, u32[]{:S(2)}, u32[]{:S(2)}) collective-permute-start(bf16[8,12,16,128]{3,2,1,0:T(8,128)(2,1)S(1)} %pad_maximum_fusion.1.refs_2_.refs_1_.refs_3_), channel_id=1, source_target_pairs={{2,0},{15,1},{4,2},{1,3},{6,4},{3,5},{8,6},{5,7},{10,8},{7,9},{12,... | collective-permute-start | bytes 1179656 | tf_op jit(solution)/shard_map/ppermute | solution.py:115
  36.6 16.4 %collective-permute-start.14 = (bf16[8,12,16,128]{3,2,1,0:T(8,128)(2,1)S(1)}, bf16[8,12,16,128]{3,2,1,0:T(8,128)(2,1)S(1)}, u32[]{:S(2)}, u32[]{:S(2)}) collective-permute-start(bf16[8,12,16,128]{3,2,1,0:T(8,128)(2,1)S(1)} %collective-permute-done.13.refs_10_), channel_id=1, source_target_pairs={{0,2},{1,15},{2,4},{3,1},{4,6},{5,3},{6,8},{7,5},{8,10},{9,7},{10,... | collective-permute-start | bytes 1179656 | tf_op jit(solution)/shard_map/ppermute | solution.py:114
  41.2 17.5 %collective-permute-start.3 = (bf16[8,12,16,128]{3,2,1,0:T(8,128)(2,1)S(1)}, bf16[8,12,16,128]{3,2,1,0:T(8,128)(2,1)S(1)}, u32[]{:S(2)}, u32[]{:S(2)}) collective-permute-start(bf16[8,12,16,128]{3,2,1,0:T(8,128)(2,1)S(1)} %collective-permute-done.2.refs_4_), channel_id=1, source_target_pairs={{2,0},{15,1},{4,2},{1,3},{6,4},{3,5},{8,6},{5,7},{10,8},{7,9},{12,... | collective-permute-start | bytes 1179656 | tf_op jit(solution)/shard_map/ppermute | solution.py:115
  44.6 16.0 %collective-permute-start.7 = (bf16[8,12,16,128]{3,2,1,0:T(8,128)(2,1)S(1)}, bf16[8,12,16,128]{3,2,1,0:T(8,128)(2,1)S(1)}, u32[]{:S(2)}, u32[]{:S(2)}) collective-permute-start(bf16[8,12,16,128]{3,2,1,0:T(8,128)(2,1)S(1)} %collective-permute-done.6.refs_9_), channel_id=1, source_target_pairs={{0,2},{1,15},{2,4},{3,1},{4,6},{5,3},{6,8},{7,5},{8,10},{9,7},{10,... | collective-permute-start | bytes 1179656 | tf_op jit(solution)/shard_map/ppermute | solution.py:114
  49.2 22.6 %collective-permute-start.1 = (bf16[8,12,16,128]{3,2,1,0:T(8,128)(2,1)S(1)}, bf16[8,12,16,128]{3,2,1,0:T(8,128)(2,1)S(1)}, u32[]{:S(2)}, u32[]{:S(2)}) collective-permute-start(bf16[8,12,16,128]{3,2,1,0:T(8,128)(2,1)S(1)} %pad_maximum_fusion.refs_1_.refs_3_.refs_0_), channel_id=1, source_target_pairs={{0,1009},{1,16},{2,1011},{3,18},{4,1013},{5,20},{6,1015},{7,22},{8... | collective-permute-start | bytes 1179656 | tf_op jit(solution)/shard_map/ppermute | solution.py:134
  51.1 14.2 %collective-permute-start.11 = (bf16[8,12,16,128]{3,2,1,0:T(8,128)(2,1)S(1)}, bf16[8,12,16,128]{3,2,1,0:T(8,128)(2,1)S(1)}, u32[]{:S(2)}, u32[]{:S(2)}) collective-permute-start(bf16[8,12,16,128]{3,2,1,0:T(8,128)(2,1)S(1)} %collective-permute-done.10.refs_4_), channel_id=1, source_target_pairs={{2,0},{15,1},{4,2},{1,3},{6,4},{3,5},{8,6},{5,7},{10,8},{7,9},{12,... | collective-permute-start | bytes 1179656 | tf_op jit(solution)/shard_map/ppermute | solution.py:115
  53.0 14.2 %collective-permute-start.15 = (bf16[8,12,16,128]{3,2,1,0:T(8,128)(2,1)S(1)}, bf16[8,12,16,128]{3,2,1,0:T(8,128)(2,1)S(1)}, u32[]{:S(2)}, u32[]{:S(2)}) collective-permute-start(bf16[8,12,16,128]{3,2,1,0:T(8,128)(2,1)S(1)} %collective-permute-done.14.refs_9_), channel_id=1, source_target_pairs={{0,2},{1,15},{2,4},{3,1},{4,6},{5,3},{6,8},{7,5},{8,10},{9,7},{10,... | collective-permute-start | bytes 1179656 | tf_op jit(solution)/shard_map/ppermute | solution.py:114
  58.7 13.1 %collective-permute-start.4 = (bf16[8,12,16,128]{3,2,1,0:T(8,128)(2,1)S(1)}, bf16[8,12,16,128]{3,2,1,0:T(8,128)(2,1)S(1)}, u32[]{:S(2)}, u32[]{:S(2)}) collective-permute-start(bf16[8,12,16,128]{3,2,1,0:T(8,128)(2,1)S(1)} %collective-permute-done.3.refs_5_), channel_id=1, source_target_pairs={{2,0},{15,1},{4,2},{1,3},{6,4},{3,5},{8,6},{5,7},{10,8},{7,9},{12,... | collective-permute-start | bytes 1179656 | tf_op jit(solution)/shard_map/ppermute | solution.py:115
  60.6 13.6 %collective-permute-start.8 = (bf16[8,12,16,128]{3,2,1,0:T(8,128)(2,1)S(1)}, bf16[8,12,16,128]{3,2,1,0:T(8,128)(2,1)S(1)}, u32[]{:S(2)}, u32[]{:S(2)}) collective-permute-start(bf16[8,12,16,128]{3,2,1,0:T(8,128)(2,1)S(1)} %collective-permute-done.7.refs_8_), channel_id=1, source_target_pairs={{0,2},{1,15},{2,4},{3,1},{4,6},{5,3},{6,8},{7,5},{8,10},{9,7},{10,... | collective-permute-start | bytes 1179656 | tf_op jit(solution)/shard_map/ppermute | solution.py:116
  65.3 19.7 %collective-permute-start.12 = (bf16[8,12,16,128]{3,2,1,0:T(8,128)(2,1)S(1)}, bf16[8,12,16,128]{3,2,1,0:T(8,128)(2,1)S(1)}, u32[]{:S(2)}, u32[]{:S(2)}) collective-permute-start(bf16[8,12,16,128]{3,2,1,0:T(8,128)(2,1)S(1)} %collective-permute-done.11.refs_5_), channel_id=1, source_target_pairs={{2,0},{15,1},{4,2},{1,3},{6,4},{3,5},{8,6},{5,7},{10,8},{7,9},{12,... | collective-permute-start | bytes 1179656 | tf_op jit(solution)/shard_map/ppermute | solution.py:115
  67.2 17.8 %collective-permute-start.16 = (bf16[8,12,16,128]{3,2,1,0:T(8,128)(2,1)S(1)}, bf16[8,12,16,128]{3,2,1,0:T(8,128)(2,1)S(1)}, u32[]{:S(2)}, u32[]{:S(2)}) collective-permute-start(bf16[8,12,16,128]{3,2,1,0:T(8,128)(2,1)S(1)} %collective-permute-done.15.refs_8_), channel_id=1, source_target_pairs={{0,2},{1,15},{2,4},{3,1},{4,6},{5,3},{6,8},{7,5},{8,10},{9,7},{10,... | collective-permute-start | bytes 1179656 | tf_op jit(solution)/shard_map/ppermute | solution.py:116
  76.6 18.9 %collective-permute-start.9 = (bf16[8,12,16,128]{3,2,1,0:T(8,128)(2,1)S(1)}, bf16[8,12,16,128]{3,2,1,0:T(8,128)(2,1)S(1)}, u32[]{:S(2)}, u32[]{:S(2)}) collective-permute-start(bf16[8,12,16,128]{3,2,1,0:T(8,128)(2,1)S(1)} %shard_map.37.refs_11_.refs_0_.refs_1_), channel_id=1, source_target_pairs={{0,1009},{1,16},{2,1011},{3,18},{4,1013},{5,20},{6,1015},{7,22},{8... | collective-permute-start | bytes 1179656 | tf_op jit(solution)/shard_map/ppermute | solution.py:134
  87.5 5.5 %collective-permute-start.17 = (bf16[7,12,16,128]{3,2,1,0:T(8,128)(2,1)S(1)}, bf16[7,12,16,128]{3,2,1,0:T(8,128)(2,1)S(1)}, u32[]{:S(2)}, u32[]{:S(2)}) collective-permute-start(bf16[7,12,16,128]{3,2,1,0:T(8,128)(2,1)S(1)} %get-tuple-element.16), channel_id=1, source_target_pairs={{0,1},{1,0},{2,3},{3,2},{4,5},{5,4},{6,7},{7,6},{8,9},{9,8},{10,11... | collective-permute-start | bytes 1032200 | tf_op jit(solution)/shard_map/ppermute | solution.py:164
  98.0 4.3 %collective-permute-start.18 = (bf16[16,12,8,128]{3,2,1,0:T(8,128)(2,1)S(1)}, bf16[16,12,8,128]{3,2,1,0:T(8,128)(2,1)S(1)}, u32[]{:S(2)}, u32[]{:S(2)}) collective-permute-start(bf16[16,12,8,128]{3,2,1,0:T(8,128)(2,1)S(1)} %get-tuple-element.20), channel_id=1, source_target_pairs={{0,1},{1,0},{2,3},{3,2},{4,5},{5,4},{6,7},{7,6},{8,9},{9,8},{10,11... | collective-permute-start | bytes 1179656 | tf_op jit(solution)/shard_map/ppermute | solution.py:169
